TPU v7x, 512 devices: a whole 4x8x8 slice. The times are simulated.
512 devices in a mesh: wide: 64 (over y, z), narrow: 8 (over x, core).
Axes of the slice: x: 4, y: 8, z: 8, core: 2. Of those that a mesh axis runs over, the one named last changes fastest.
Arguments:
- item_states: bfloat16 [65536, 2048], P(('wide', 'narrow'))
- item_gain: bfloat16 [2048], replicated, may hold values from 0.5 to 1.5
- wq_item: bfloat16 [2048, 2048], P(None, 'narrow')
- wkv_item: bfloat16 [2048, 8, 128], P(None, 'narrow')
- wo_item: bfloat16 [2048, 2048], P('narrow'), may hold values from -0.125 to 0.125
- user_gain: bfloat16 [2048], replicated, may hold values from 0.5 to 1.5
- wq_user: bfloat16 [2048, 2048], P('wide', 'narrow')
- wkv_user: bfloat16 [2048, 8, 128], P('wide', 'narrow')
- wo_user: bfloat16 [2048, 2048], P('narrow', 'wide'), may hold values from -0.125 to 0.125
- history_items: int32 [64, 512], P('wide'), may hold values from 0 to 511, as said below
- history_lengths: int32 [64], P('wide'), may hold values from 1 to 512, 16384 in all
Outputs:
- item_embeddings: bfloat16 [512, 2048], P('wide', 'narrow')
- user_states: bfloat16 [32768, 2048], P('wide', 'narrow')
Inputs may be any that keep to these rules, and one draw needn't show every extreme that they name: `history_items`: every user's history names at most 16 slots of items whose ids lie in one run of 8 ids (k * 8 to (k + 1) * 8 - 1), and exactly 16 for some run.
All inputs are finite; a program needn't handle non-finite values. No bound on the sum of `history_lengths` on one device may be relied on, other than what follows from the above.
Results may differ from a plain program's by a relative error of at most 0.0065.
Values may be sent and summed in bfloat16 or wider, within the bound.
No kernel may reach another device: no remote copies, remote signals or barrier semaphores. Data moves between devices by JAX's collectives and lax.ppermute only.
A program may use at most 64 MiB of HBM per device.

v0:
```python
import math

import jax
import jax.numpy as jnp
from jax import lax
from jax.sharding import PartitionSpec as P

HEAD_DIM = 64
TXT = 128


epsilon = 1e-05


def rms_scale(values, gain):
    wide = values.astype(jnp.float32)
    power = jnp.mean(wide * wide, axis=-1, keepdims=True)
    return (wide * lax.rsqrt(power + epsilon) * gain.astype(jnp.float32)).astype(jnp.bfloat16)


def item_attend(queries, keyvals, head_dim):
    scores = jnp.einsum(
        "gkrd,gtkd->gkrt", queries, keyvals[..., :head_dim], preferred_element_type=jnp.float32
    )
    scores = scores * (1.0 / math.sqrt(head_dim))
    weights = jax.nn.softmax(scores, axis=-1).astype(jnp.bfloat16)
    mixed = jnp.einsum(
        "gkrt,gtkd->gkrd", weights, keyvals[..., head_dim:], preferred_element_type=jnp.float32
    )
    return mixed.astype(jnp.bfloat16).reshape(mixed.shape[0], -1)


def user_attend(queries, keyvals, offset, length, head_dim):
    scores = jnp.einsum(
        "ikrd,jkd->krij", queries, keyvals[..., :head_dim], preferred_element_type=jnp.float32
    )
    scores = scores * (1.0 / math.sqrt(head_dim))
    query_slots = offset + jnp.arange(queries.shape[0], dtype=jnp.int32)
    key_slots = jnp.arange(keyvals.shape[0], dtype=jnp.int32)
    allowed = (key_slots[None, :] <= query_slots[:, None]) & (key_slots[None, :] < length)
    scores = jnp.where(allowed[None, None], scores, -1e30)
    weights = jax.nn.softmax(scores, axis=-1).astype(jnp.bfloat16)
    mixed = jnp.einsum(
        "krij,jkd->ikrd", weights, keyvals[..., head_dim:], preferred_element_type=jnp.float32
    )
    return mixed.astype(jnp.bfloat16).reshape(queries.shape[0], -1)


def local(
    item_states,
    item_gain,
    wq_item,
    wkv_item,
    wo_item,
    user_gain,
    wq_user,
    wkv_user,
    wo_user,
    history_items,
    history_lengths,
):
    head_dim = HEAD_DIM
    text = TXT
    width = item_states.shape[1]
    rows_all = lax.all_gather(item_states, "narrow", axis=0, tiled=True)
    normed = rms_scale(rows_all, item_gain)
    group = rows_all.shape[0] // text
    keyvals = jnp.dot(
        normed, wkv_item.reshape(width, -1), preferred_element_type=jnp.float32
    ).astype(jnp.bfloat16)
    keyvals = keyvals.reshape(group, text, wkv_item.shape[1], 2 * head_dim)
    last_raw = rows_all.reshape(group, text, width)[:, -1]
    last_normed = normed.reshape(group, text, width)[:, -1]
    kv_local = keyvals.shape[2]
    queries = jnp.dot(last_normed, wq_item, preferred_element_type=jnp.float32).astype(jnp.bfloat16)
    queries = queries.reshape(group, kv_local, -1, head_dim)
    mixed = item_attend(queries, keyvals, head_dim)
    partial_sum = jnp.dot(mixed, wo_item, preferred_element_type=jnp.float32)
    share = width // lax.axis_size("narrow")
    offset = lax.axis_index("narrow") * share
    total = lax.psum(partial_sum, "narrow")
    source = (last_raw.astype(jnp.float32) + total).astype(jnp.bfloat16)
    item_part = lax.dynamic_slice_in_dim(source, offset, share, 1)
    item_ids = history_items[0]
    hist_len = item_ids.shape[0]
    catalog = lax.all_gather(source, "wide", axis=0, tiled=True)
    history = jnp.take(catalog, item_ids, axis=0)
    residual = lax.dynamic_slice_in_dim(history, offset, share, 1)
    normed_user = rms_scale(history, user_gain)
    kv_heads_local = wkv_user.shape[1]
    pieces = (
        lax.all_gather(wq_user, "wide", axis=0, tiled=True),
        lax.all_gather(wkv_user, "wide", axis=0, tiled=True),
    )
    query_part = jnp.dot(normed_user, pieces[0], preferred_element_type=jnp.float32)
    kv_part = jnp.dot(
        normed_user, pieces[1].reshape(pieces[1].shape[0], -1), preferred_element_type=jnp.float32
    )
    user_queries = query_part.astype(jnp.bfloat16).reshape(hist_len, kv_heads_local, -1, head_dim)
    user_keyvals = kv_part.astype(jnp.bfloat16).reshape(hist_len, kv_heads_local, 2 * head_dim)
    length = history_lengths[0]
    block = min(hist_len, 512)
    count = hist_len // block
    query_blocks = user_queries.reshape((count, block) + user_queries.shape[1:])
    block_starts = jnp.arange(count, dtype=jnp.int32) * block

    def attend_block(inputs):
        return user_attend(inputs[0], user_keyvals, inputs[1], length, head_dim)

    user_mixed = lax.map(attend_block, (query_blocks, block_starts)).reshape(hist_len, -1)
    terms = jnp.dot(
        user_mixed,
        lax.all_gather(wo_user, "wide", axis=1, tiled=True),
        preferred_element_type=jnp.float32,
    )
    summed = lax.psum_scatter(
        terms.astype(jnp.bfloat16), "narrow", scatter_dimension=1, tiled=True
    ).astype(jnp.float32)
    live = (jnp.arange(hist_len, dtype=jnp.int32) < length)[:, None]
    user_states = jnp.where(live, residual.astype(jnp.float32) + summed, 0.0).astype(jnp.bfloat16)
    return (item_part, user_states)


def solution(mesh):
    return jax.shard_map(
        local,
        mesh=mesh,
        in_specs=(
            P(("wide", "narrow"), None),
            P(),
            P(None, "narrow"),
            P(None, "narrow", None),
            P("narrow", None),
            P(),
            P("wide", "narrow"),
            P("wide", "narrow", None),
            P("narrow", "wide"),
            P("wide", None),
            P("wide"),
        ),
        out_specs=(P("wide", "narrow"), P("wide", "narrow")),
        check_vma=False,
    )
```

profile of v0, /device:TPU:8, one launch (start us, length us, event | category | flops | bytes accessed | tf_op | source)
XLA Modules:
  0.0 429.0 jit_solution(4521393691965242649)
XLA Ops:
  7.2 0.0 copy-start
  7.2 0.0 all-gather.5.cloned.1.call-start
  7.2 0.7 all-gather.5.cloned.1.call-update
  7.9 0.0 all-reduce.2.cloned.1.call-start
  8.0 0.7 convert_element_type.76
  8.7 43.5 %all-gather.5.cloned.1.call-done = bf16[1024,2048]{1,0:T(8,128)(2,1)} async-done(((bf16[128,2048]{1,0:T(8,128)(2,1)}), bf16[1024,2048]{1,0:T(8,128)(2,1)}) %all-gather.5.cloned.1.call-update) | async-done | bytes 4194320 | tf_op jit(solution)/shard_map/all_gather | solution.py:65
  52.2 3.2 fusion.1
  55.4 0.2 copy-done.1
  55.7 1.0 fusion.3
  56.7 0.0 copy-done.8
  56.7 1.2 convolution_convert_fusion.2
  58.0 0.1 slice.29
  58.1 0.2 convolution_convert_fusion.5
  58.3 0.1 reshape.192
  58.4 0.2 convolution_multiply_fusion
  58.6 0.2 fusion.27
  58.8 0.4 convolution_convert_fusion.4
  59.2 0.1 reshape.197
  59.3 0.9 fusion.28
  60.2 0.0 all-reduce.2.cloned.1.call-update
  60.2 0.0 all-gather.7.cloned.1.call-start
  60.2 1.0 slice.28
  61.3 68.5 %all-reduce.2.cloned.1.call-done = f32[8,2048]{1,0:T(8,128)} async-done(((f32[8,2048]{1,0:T(8,128)}), f32[8,2048]{1,0:T(8,128)}) %all-reduce.2.cloned.1.call-update) | async-done | bytes 65552 | tf_op jit(solution)/shard_map/psum | solution.py:81
  129.8 1.5 fusion.23
  131.3 0.0 all-gather.7.cloned.1.call-update
  131.3 0.0 all-gather.9.cloned.1.call-start
  131.4 0.5 all-gather.9.cloned.1.call-update
  131.9 0.0 all-gather.11.cloned.1.call-start
  131.9 0.5 all-gather.11.cloned.1.call-update
  132.5 0.0 reduce-scatter.2.cloned.1.call-start
  132.6 54.9 %all_gather.17 = bf16[2048,1,128]{2,0,1:T(8,128)(2,1)} all-gather(bf16[32,1,128]{2,0,1:T(8,128)(2,1)S(1)} %copy-done.5), channel_id=1, replica_groups=mesh['wide'=64,'narrow'=8] {'wide'}, dimensions={0}, use_global_device_ids=true | all-gather | bytes 532480 | tf_op jit(solution)/shard_map/all_gather | solution.py:93
  188.2 0.1 fusion.17
  188.4 27.8 %all-gather.7.cloned.1.call-done = bf16[512,2048]{1,0:T(8,128)(2,1)} async-done(((bf16[8,2048]{1,0:T(8,128)(2,1)}), bf16[512,2048]{1,0:T(8,128)(2,1)}) %all-gather.7.cloned.1.call-update) | async-done | bytes 2097168 | tf_op jit(solution)/shard_map/all_gather | solution.py:86
  216.1 6.3 %gather_fusion = bf16[512,2048]{1,0:T(8,128)(2,1)S(1)} fusion(bf16[512,2048]{1,0:T(8,128)(2,1)} %all-gather.7.cloned.1.call-done, s32[1024]{0:T(1024)S(1)} %pad_clamp_fusion), kind=kCustom, calls=%fused_computation | custom fusion | bytes 4196352 | tf_op jit(solution)/shard_map/jit(_take)/gather | solution.py:87
  222.4 0.8 fusion.4
  223.2 1.3 copy-done.2
  224.5 0.9 fusion.14
  225.5 72.7 %all-gather.9.cloned.1.call-done = bf16[2048,256]{1,0:T(8,128)(2,1)} async-done(((bf16[32,256]{1,0:T(8,128)(2,1)}), bf16[2048,256]{1,0:T(8,128)(2,1)}) %all-gather.9.cloned.1.call-update) | async-done | bytes 1048592 | tf_op jit(solution)/shard_map/all_gather | solution.py:92
  298.1 2.8 convolution_convert_fusion.1
  300.9 0.9 fusion.8
  301.8 0.9 fusion.7
  302.7 1.4 fusion.11
  304.1 76.2 %all-gather.11.cloned.1.call-done = bf16[256,2048]{0,1:T(8,128)(2,1)} async-done(((bf16[256,32]{0,1:T(8,128)(2,1)}), bf16[256,2048]{0,1:T(8,128)(2,1)}) %all-gather.11.cloned.1.call-update) | async-done | bytes 1048592 | tf_op jit(solution)/shard_map/all_gather | solution.py:113
  380.3 3.3 convolution_convert_fusion
  383.6 0.0 reduce-scatter.2.cloned.1.call-update
  383.6 1.3 constant_dynamic-slice_fusion
  384.9 35.4 %reduce-scatter.2.cloned.1.call-done = bf16[512,256]{1,0:T(8,128)(2,1)} async-done(((bf16[512,2048]{1,0:T(8,128)(2,1)}), bf16[512,256]{1,0:T(8,128)(2,1)}) %reduce-scatter.2.cloned.1.call-update) | async-done | bytes 262160 | tf_op jit(solution)/shard_map/reduce_scatter | solution.py:116
  420.3 1.9 select_convert_fusion
  (21 shorter events, 0.1 us)
Async XLA Ops:
  7.2 52.1 %copy-start = (bf16[256,2048]{1,0:T(8,128)(2,1)S(1)}, bf16[256,2048]{1,0:T(8,128)(2,1)}, u32[]{:S(2)}) copy-start(bf16[256,2048]{1,0:T(8,128)(2,1)} %param.15) | copy-start | bytes 3145732
  7.2 45.0 %all-gather.5.cloned.1.call-start = ((), (), s32[]{:S(2)}) async-start(), calls=%async_computation.1 | async-start | bytes 4718592 | tf_op jit(solution)/shard_map/all_gather | solution.py:65
  7.9 121.9 %all-reduce.2.cloned.1.call-start = ((), (), s32[]{:S(2)}) async-start(), calls=%async_computation.2 | async-start | bytes 131072 | tf_op jit(solution)/shard_map/psum | solution.py:81
  52.2 3.4 copy-start.1
  55.6 1.0 copy-start.8
  56.7 1.4 copy-start.3
  56.7 75.8 %copy-start.6 = (s32[1,512]{1,0:T(1,128)S(1)}, s32[1,512]{1,0:T(1,128)}, u32[]{:S(2)}) copy-start(s32[1,512]{1,0:T(1,128)} %param.20) | copy-start | bytes 6148
  56.7 75.9 %copy-start.7 = (bf16[2048]{0:T(1024)(128)(2,1)S(1)}, bf16[2048]{0:T(1024)(128)(2,1)}, u32[]{:S(2)}) copy-start(bf16[2048]{0:T(1024)(128)(2,1)} %param.16) | copy-start | bytes 12292
  56.7 75.9 %copy-start.5 = (bf16[32,1,128]{2,0,1:T(8,128)(2,1)S(1)}, bf16[32,1,128]{2,0,1:T(8,128)(2,1)}, u32[]{:S(2)}) copy-start(bf16[32,1,128]{2,0,1:T(8,128)(2,1)} %param.18) | copy-start | bytes 24580
  60.2 155.9 %all-gather.7.cloned.1.call-start = ((), (), s32[]{:S(2)}) async-start(), calls=%async_computation.3 | async-start | bytes 2129920 | tf_op jit(solution)/shard_map/all_gather | solution.py:86
  131.3 166.8 %all-gather.9.cloned.1.call-start = ((), (), s32[]{:S(2)}) async-start(), calls=%async_computation.4 | async-start | bytes 1064960 | tf_op jit(solution)/shard_map/all_gather | solution.py:92
  131.9 248.4 %all-gather.11.cloned.1.call-start = ((), (), s32[]{:S(2)}) async-start(), calls=%async_computation.5 | async-start | bytes 1064960 | tf_op jit(solution)/shard_map/all_gather | solution.py:113
  132.5 287.8 %reduce-scatter.2.cloned.1.call-start = ((), (), s32[]{:S(2)}) async-start(), calls=%async_computation.6 | async-start | bytes 2359296 | tf_op jit(solution)/shard_map/reduce_scatter | solution.py:116
  222.4 2.1 copy-start.4
  223.2 1.3 copy-start.2
Sparse Core Ops, SparseCore 0:
  10.2 41.9 all-gather.4
  60.3 69.4 all-reduce.1
  133.8 82.2 all-gather.6
  219.4 78.6 all-gather.8
  301.4 78.8 all-gather.10
  383.7 36.5 reduce-scatter.1
where the time goes:
time: 429 us
  waiting for transfers between devices  326 us (76%)
  blocking collectives  54.9 us (13%)
  between operations  15 us (3%)
  matrix products  12.2 us (3%)
  local copies, waits for them, and re-layouts  10.4 us (2%)
  other arithmetic  10.3 us (2%)
    all_gather x1, waiting for transfers between devices, local(): lax.all_gather(wo_user, 'wide', axis=1, tiled=True)  76.2 us
    all_gather x1, waiting for transfers between devices, local(): lax.all_gather(wq_user, 'wide', axis=0, tiled=True)  72.7 us
    psum x1, waiting for transfers between devices, local(): total = lax.psum(partial_sum, 'narrow')  68.5 us
    all_gather x1, blocking collectives, local(): lax.all_gather(wkv_user, 'wide', axis=0, tiled=True)  54.9 us
    all_gather x1, waiting for transfers between devices, local(): rows_all = lax.all_gather(item_states, 'narrow', axis=0, tiled=True)  43.5 us
    reduce_scatter x1, waiting for transfers between devices, local(): lax.psum_scatter(terms.astype(jnp.bfloat16), 'narrow', scatter_dimension=...  35.4 us
    all_gather x1, waiting for transfers between devices, local(): catalog = lax.all_gather(source, 'wide', axis=0, tiled=True)  27.8 us
  transfers between devices with their start and end apart: 6, of which 6 were waited for; matrix products, arithmetic and copies ran while one was open for 4% of the time, Pallas kernels for 0%

commit v1 on v0

v1 whole, which is shorter than its diff:
```python
import math

import jax
import jax.numpy as jnp
from jax import lax
from jax.sharding import PartitionSpec as P

HEAD_DIM = 64
TXT = 128
epsilon = 1e-05


def rms_scale(values, gain):
    wide = values.astype(jnp.float32)
    power = jnp.mean(wide * wide, axis=-1, keepdims=True)
    return (wide * lax.rsqrt(power + epsilon) * gain.astype(jnp.float32)).astype(jnp.bfloat16)


def dot_t(left, right):
    return lax.dot_general(
        left, right, (((1,), (1,)), ((), ())), preferred_element_type=jnp.float32
    )


def spread(values, axis, groups=None):
    size = lax.axis_size(axis) if groups is None else len(groups[0])
    copies = jnp.broadcast_to(values[None], (size,) + values.shape)
    return lax.all_to_all(copies, axis, 0, 0, axis_index_groups=groups)


def local(
    item_states,
    item_gain,
    wq_item,
    wkv_item,
    wo_item,
    user_gain,
    wq_user,
    wkv_user,
    wo_user,
    history_items,
    history_lengths,
):
    width = item_states.shape[1]
    n_narrow = lax.axis_size("narrow")
    n_x = n_narrow // 2
    share = width // n_narrow
    me = lax.axis_index("narrow")
    core = me % 2
    same_core = [[2 * x + c for x in range(n_x)] for c in range(2)]
    scale = 1.0 / math.sqrt(HEAD_DIM)

    parts = jnp.concatenate(
        [wq_user, wkv_user.reshape(wkv_user.shape[0], -1), wo_user.T], axis=1
    )
    weights_all = lax.all_gather(parts, "wide", axis=0, tiled=True)

    last_raw = spread(item_states[TXT - 1 :], "narrow").reshape(n_narrow, width)
    last_normed = rms_scale(last_raw, item_gain)
    queries = jnp.dot(last_normed, wq_item, preferred_element_type=jnp.float32)
    queries = queries.astype(jnp.bfloat16)
    per = queries.shape[1] // HEAD_DIM
    wk = wkv_item[:, 0, :HEAD_DIM]
    wv = wkv_item[:, 0, HEAD_DIM:]
    probes = dot_t(queries.reshape(-1, HEAD_DIM), wk).astype(jnp.bfloat16)
    probes = lax.all_to_all(probes.reshape(n_narrow, per, width), "narrow", 0, 0)
    normed = rms_scale(item_states, item_gain)
    scores = dot_t(probes.reshape(-1, width), normed) * scale
    attn = jax.nn.softmax(scores, axis=-1).astype(jnp.bfloat16)
    pooled = jnp.dot(attn, normed, preferred_element_type=jnp.float32).astype(jnp.bfloat16)
    pooled = lax.all_to_all(pooled.reshape(n_narrow, per, width), "narrow", 0, 0)
    mixed = jnp.dot(pooled.reshape(-1, width), wv, preferred_element_type=jnp.float32)
    mixed = mixed.astype(jnp.bfloat16).reshape(n_narrow, -1)
    partial_sum = jnp.dot(mixed, wo_item, preferred_element_type=jnp.float32)
    pieces = partial_sum.reshape(n_narrow, n_narrow, share).transpose(1, 0, 2)
    total = jnp.sum(lax.all_to_all(pieces, "narrow", 0, 0), axis=0)
    last_share = lax.dynamic_slice_in_dim(last_raw, me * share, share, 1)
    item_part = (last_share.astype(jnp.float32) + total).astype(jnp.bfloat16)

    catalog_part = spread(item_part, "wide").reshape(-1, share)
    mine = spread(catalog_part, "narrow", same_core)
    other = lax.ppermute(mine, "narrow", [(i, i ^ 1) for i in range(n_narrow)])
    low = jnp.where(core == 0, mine, other)
    high = jnp.where(core == 0, other, mine)
    catalog = jnp.stack([low, high], axis=1).transpose(2, 0, 1, 3).reshape(-1, width)
    user_normed = rms_scale(catalog, user_gain)

    q_width = wq_user.shape[1]
    kv_width = 2 * HEAD_DIM
    projected = jnp.dot(
        user_normed, weights_all[:, : q_width + kv_width], preferred_element_type=jnp.float32
    ).astype(jnp.bfloat16)
    item_ids = history_items[0]
    slots = item_ids.shape[0]
    picks = (item_ids[:, None] == jnp.arange(catalog.shape[0], dtype=jnp.int32)[None, :]).astype(
        jnp.bfloat16
    )
    rows = jnp.dot(
        picks,
        jnp.concatenate([projected, catalog_part], axis=1),
        preferred_element_type=jnp.float32,
    ).astype(jnp.bfloat16)
    heads = q_width // HEAD_DIM
    user_queries = rows[:, :q_width].reshape(slots, heads, HEAD_DIM)
    keys = rows[:, q_width : q_width + HEAD_DIM]
    values = rows[:, q_width + HEAD_DIM : q_width + kv_width]
    residual = rows[:, q_width + kv_width :]
    length = history_lengths[0]
    user_scores = jnp.einsum(
        "ird,jd->rij", user_queries, keys, preferred_element_type=jnp.float32
    ) * scale
    index = jnp.arange(slots, dtype=jnp.int32)
    allowed = (index[None, :] <= index[:, None]) & (index[None, :] < length)
    user_scores = jnp.where(allowed[None], user_scores, -1e30)
    user_attn = jax.nn.softmax(user_scores, axis=-1).astype(jnp.bfloat16)
    user_mixed = jnp.einsum(
        "rij,jd->ird", user_attn, values, preferred_element_type=jnp.float32
    ).astype(jnp.bfloat16).reshape(slots, -1)

    wo_t = weights_all[:, q_width + kv_width :].reshape(n_x, 2, share, -1)
    wo_mine = lax.dynamic_index_in_dim(wo_t, core, 1, keepdims=False)
    wo_other = lax.dynamic_index_in_dim(wo_t, 1 - core, 1, keepdims=False)

    def project(weights):
        return jnp.einsum("ih,xch->xic", user_mixed, weights, preferred_element_type=jnp.float32)

    theirs = lax.ppermute(
        project(wo_other).astype(jnp.bfloat16), "narrow", [(i, i ^ 1) for i in range(n_narrow)]
    )
    pair = (project(wo_mine) + theirs.astype(jnp.float32)).astype(jnp.bfloat16)
    shares = lax.all_to_all(pair, "narrow", 0, 0, axis_index_groups=same_core)
    summed = jnp.sum(shares.astype(jnp.float32), axis=0)
    live = (index < length)[:, None]
    user_states = jnp.where(live, residual.astype(jnp.float32) + summed, 0.0).astype(jnp.bfloat16)
    return (item_part, user_states)


def solution(mesh):
    return jax.shard_map(
        local,
        mesh=mesh,
        in_specs=(
            P(("wide", "narrow"), None),
            P(),
            P(None, "narrow"),
            P(None, "narrow", None),
            P("narrow", None),
            P(),
            P("wide", "narrow"),
            P("wide", "narrow", None),
            P("narrow", "wide"),
            P("wide", None),
            P("wide"),
        ),
        out_specs=(P("wide", "narrow"), P("wide", "narrow")),
        check_vma=False,
    )
```

time: 429 us -> 155 us (0.36)
  the two profiles are of different devices: /device:TPU:8 before, /device:TPU:16 now
where the time goes in v1:
time: 155 us; the launch traced here: 154 us
  blocking collectives  66.3 us (43%)
  waiting for transfers between devices  23.4 us (15%)
  starting transfers between devices  18.4 us (12%)
  between operations  15.1 us (10%)
  matrix products  14.9 us (10%)
  other arithmetic  8.74 us (6%)
  local copies, waits for them, and re-layouts  7.36 us (5%)
    all_to_all x2, blocking collectives, spread(): return lax.all_to_all(copies, axis, 0, 0, axis_index_groups=groups)  46.7 us
    all_to_all x1, blocking collectives, local(): shares = lax.all_to_all(pair, 'narrow', 0, 0, axis_index_groups=same_core)  19.6 us
    all_to_all x1, waiting for transfers between devices, local(): lax.all_to_all(probes.reshape(n_narrow, per, width), 'narrow', 0, 0)  6.03 us
    all_to_all x1, waiting for transfers between devices, local(): total = jnp.sum(lax.all_to_all(pieces, 'narrow', 0, 0), axis=0)  5.51 us
    all_to_all x1, waiting for transfers between devices, local(): lax.all_to_all(pooled.reshape(n_narrow, per, width), 'narrow', 0, 0)  4.56 us
    all_to_all x1, starting transfers between devices, spread(): return lax.all_to_all(copies, axis, 0, 0, axis_index_groups=groups)  4.3 us
    sub x1, matrix products, local(): user_attn = jax.nn.softmax(user_scores, axis=-1).astype(jnp.bfloat16)  3.51 us
    all_to_all x1, starting transfers between devices, local(): total = jnp.sum(lax.all_to_all(pieces, 'narrow', 0, 0), axis=0)  3.48 us
  transfers between devices with their start and end apart: 7, of which 7 were waited for; matrix products, arithmetic and copies ran while one was open for 9% of the time, Pallas kernels for 0%

profile of v1, /device:TPU:16, one launch (start us, length us, event | category | flops | bytes accessed | tf_op | source)
XLA Modules:
  0.0 154.2 jit_solution(11367806473106478293)
XLA Ops:
  7.2 0.9 slice_reduce_fusion
  8.1 0.5 broadcast.79
  8.7 0.8 reduce.4
  9.5 0.6 reshape.146
  10.1 4.3 %all-to-all-start = ((bf16[8,2,1024]{2,1,0:T(2,128)(2,1)}), bf16[8,2,1024]{2,1,0:T(2,128)(2,1)S(1)}, u32[]{:S(2)}, u32[]{:S(2)}) async-start(bf16[8,2,1024]{2,1,0:T(2,128)(2,1)} %reshape.146), calls=%async_computation | async-start | bytes 65536 | tf_op jit(solution)/shard_map/all_to_all | solution.py:28
  14.5 1.4 pad_maximum_fusion
  15.9 1.2 fusion.16
  17.1 0.7 convert_element_type.111
  17.8 2.1 %all-to-all-done = bf16[8,2,1024]{2,1,0:T(2,128)(2,1)S(1)} async-done(((bf16[8,2,1024]{2,1,0:T(2,128)(2,1)}), bf16[8,2,1024]{2,1,0:T(2,128)(2,1)S(1)}, u32[]{:S(2)}, u32[]{:S(2)}) %all-to-all-start) | async-done | bytes 32800 | tf_op jit(solution)/shard_map/all_to_all | solution.py:28
  20.1 0.3 convolution_convert_fusion.5
  20.5 1.3 convolution_convert_fusion.1
  21.8 0.7 reshape.127
  22.5 3.4 %all-to-all-start.1 = ((bf16[8,4,2048]{2,1,0:T(4,128)(2,1)}), bf16[8,4,2048]{2,1,0:T(4,128)(2,1)S(1)}, u32[]{:S(2)}, u32[]{:S(2)}) async-start(bf16[8,4,2048]{2,1,0:T(4,128)(2,1)} %reshape.127), calls=%async_computation.1 | async-start | bytes 262144 | tf_op jit(solution)/shard_map/all_to_all | solution.py:66
  25.9 6.0 %all-to-all-done.1 = bf16[8,4,2048]{2,1,0:T(4,128)(2,1)S(1)} async-done(((bf16[8,4,2048]{2,1,0:T(4,128)(2,1)}), bf16[8,4,2048]{2,1,0:T(4,128)(2,1)S(1)}, u32[]{:S(2)}, u32[]{:S(2)}) %all-to-all-start.1) | async-done | bytes 131104 | tf_op jit(solution)/shard_map/all_to_all | solution.py:66
  32.0 0.5 fusion.52
  32.5 0.2 fusion.43
  32.7 0.3 convolution_convert_fusion
  33.0 0.7 reshape.129
  33.7 3.4 %all-to-all-start.2 = ((bf16[8,4,2048]{2,1,0:T(4,128)(2,1)}), bf16[8,4,2048]{2,1,0:T(4,128)(2,1)S(1)}, u32[]{:S(2)}, u32[]{:S(2)}) async-start(bf16[8,4,2048]{2,1,0:T(4,128)(2,1)} %reshape.129), calls=%async_computation.2 | async-start | bytes 262144 | tf_op jit(solution)/shard_map/all_to_all | solution.py:71
  37.1 1.5 copy.64
  38.6 4.6 %all-to-all-done.2 = bf16[8,4,2048]{2,1,0:T(4,128)(2,1)S(1)} async-done(((bf16[8,4,2048]{2,1,0:T(4,128)(2,1)}), bf16[8,4,2048]{2,1,0:T(4,128)(2,1)S(1)}, u32[]{:S(2)}, u32[]{:S(2)}) %all-to-all-start.2) | async-done | bytes 131104 | tf_op jit(solution)/shard_map/all_to_all | solution.py:71
  43.2 0.3 convolution_convert_fusion.4
  43.7 1.0 convolution_bitcast_fusion
  44.7 3.5 %all-to-all-start.3 = ((f32[8,8,256]{2,1,0:T(8,128)}), f32[8,8,256]{2,1,0:T(8,128)S(1)}, u32[]{:S(2)}, u32[]{:S(2)}) async-start(f32[8,8,256]{2,1,0:T(8,128)} %convolution_bitcast_fusion), calls=%async_computation.3 | async-start | bytes 131072 | tf_op jit(solution)/shard_map/all_to_all | solution.py:76
  48.2 5.5 %all-to-all-done.3 = f32[8,8,256]{2,1,0:T(8,128)S(1)} async-done(((f32[8,8,256]{2,1,0:T(8,128)}), f32[8,8,256]{2,1,0:T(8,128)S(1)}, u32[]{:S(2)}, u32[]{:S(2)}) %all-to-all-start.3) | async-done | bytes 65568 | tf_op jit(solution)/shard_map/all_to_all | solution.py:76
  53.8 30.1 %all_to_all.35 = bf16[64,8,256]{2,1,0:T(8,128)(2,1)S(1)} all-to-all(bf16[64,8,256]{2,1,0:T(8,128)(2,1)S(1)} %broadcast_in_dim.33), channel_id=1, replica_groups=mesh['wide'=64,'narrow'=8] {'wide'}, dimensions={0} | all-to-all | bytes 524288 | tf_op jit(solution)/shard_map/all_to_all | solution.py:28
  84.1 16.5 %all_to_all.36 = bf16[4,512,256]{1,2,0:T(8,128)(2,1)S(1)} all-to-all(bf16[4,512,256]{1,2,0:T(8,128)(2,1)S(1)} %broadcast_in_dim.35), channel_id=1, replica_groups={{0,2,4,6},{1,3,5,7},{8,10,12,14},{9,11,13,15},{16,18,20,22},{17,19,21,2..., dimensions={0} | all-to-all | bytes 2097152 | tf_op jit(solution)/shard_map/all_to_all | solution.py:28
  100.7 1.9 %collective-permute-start = (bf16[4,512,256]{1,2,0:T(8,128)(2,1)S(1)}, bf16[4,512,256]{1,2,0:T(8,128)(2,1)S(1)}, u32[]{:S(2)}, u32[]{:S(2)}) collective-permute-start(bf16[4,512,256]{1,2,0:T(8,128)(2,1)S(1)} %all_to_all.36), channel_id=1, source_target_pairs={{0,1},{1,0},{2,3},{3,2},{4,5},{5,4},{6,7},{7,6},{8,9},{9,8},{10,11... | collective-permute-start | bytes 3145736 | tf_op jit(solution)/shard_map/ppermute | solution.py:82
  103.3 0.8 fusion.19
  104.1 1.1 collective-permute-done
  105.4 0.6 multiply_reduce_fusion
  105.9 0.3 maximum_convert_fusion
  106.2 0.4 fusion.2
  106.7 1.3 all-gather.2.cloned.1.call-done
  108.0 2.4 %fusion.12 = bf16[512,384]{0,1:T(8,128)(2,1)S(1)} fusion(bf16[512,2048]{0,1:T(8,128)(2,1)S(1)} %fusion.2, bf16[2048,640]{1,0:T(8,128)(2,1)} %all-gather.2.cloned.1.call-done), kind=kOutput, calls=%fused_computation.26 | convolution fusion | flops 805502976 | bytes 4063232 | tf_op jit(solution)/shard_map/dot_general | solution.py:90
  110.4 0.6 convolution_convert_fusion.3
  111.1 0.1 copy.51
  111.4 3.5 %fusion.53 = (f32[4,512]{1,0:T(4,128)S(1)}, f32[4,512,512]{1,2,0:T(8,128)}) fusion(pred[512,512]{0,1:T(8,128)(4,1)S(1)} %copy-done.4, bf16[512,4,64]{0,2,1:T(8,128)(2,1)S(1)} %bitcast.112, bf16[512,640]{1,0:T(8,128)(2,1)S(1)} %convolution_convert_fusion.3), kind=kOutput, calls=%fused_computation.84 | convolution fusion | flops 138412544 | bytes 4857856 | tf_op jit(solution)/shard_map/sub | solution.py:115
  114.9 2.8 %fusion.15 = bf16[64,4,512]{2,0,1:T(8,128)(2,1)S(1)} fusion(f32[4,512,512]{1,2,0:T(8,128)} %get-tuple-element.7, f32[4,512]{1,0:T(4,128)S(1)} %get-tuple-element.6, bf16[512,640]{1,0:T(8,128)(2,1)S(1)} %convolution_convert_fusion.3), kind=kOutput, calls=%fused_computation.27 | convolution fusion | flops 136445952 | bytes 4595712 | tf_op jit(solution)/shard_map/rij,jd->ird/dot_general | solution.py:116
  117.6 1.3 slice.38
  118.9 1.4 fusion.11
  120.4 1.9 %collective-permute-start.1 = (bf16[4,512,256]{1,2,0:T(8,128)(2,1)}, bf16[4,512,256]{1,2,0:T(8,128)(2,1)S(1)}, u32[]{:S(2)}, u32[]{:S(2)}) collective-permute-start(bf16[4,512,256]{1,2,0:T(8,128)(2,1)} %fusion.11), channel_id=1, source_target_pairs={{0,1},{1,0},{2,3},{3,2},{4,5},{5,4},{6,7},{7,6},{8,9},{9,8},{10,11... | collective-permute-start | bytes 3145736 | tf_op jit(solution)/shard_map/ppermute | solution.py:127
  122.3 2.8 %collective-permute-done.1 = bf16[4,512,256]{1,2,0:T(8,128)(2,1)S(1)} collective-permute-done((bf16[4,512,256]{1,2,0:T(8,128)(2,1)}, bf16[4,512,256]{1,2,0:T(8,128)(2,1)S(1)}, u32[]{:S(2)}, u32[]{:S(2)}) %collective-permute-start.1) | collective-permute-done | bytes 1048608 | tf_op jit(solution)/shard_map/ppermute | solution.py:127
  125.1 0.4 fusion.4
  125.6 19.6 %all_to_all.37 = bf16[4,512,256]{1,2,0:T(8,128)(2,1)S(1)} all-to-all(bf16[4,512,256]{1,2,0:T(8,128)(2,1)S(1)} %fusion.4), channel_id=1, replica_groups={{0,2,4,6},{1,3,5,7},{8,10,12,14},{9,11,13,15},{16,18,20,22},{17,19,21,2..., dimensions={0} | all-to-all | bytes 2097152 | tf_op jit(solution)/shard_map/all_to_all | solution.py:131
  145.2 0.1 convert_reduce_fusion
  145.3 0.2 copy.58
  145.5 1.8 %select_convert_fusion = bf16[512,256]{1,0:T(8,128)(2,1)} fusion(f32[512,256]{1,0:T(8,128)S(1)} %copy.58, bf16[512,640]{1,0:T(8,128)(2,1)} %copy-done.3, pred[512]{0:T(512)(128)(4,1)S(1)} %iota_compare_fusion.3), kind=kLoop, calls=%fused_computation.47 | loop fusion | flops 524288 | bytes 1049088 | tf_op jit(solution)/shard_map/convert_element_type | solution.py:134
  (39 shorter events, 1.2 us)
Async XLA Ops:
  7.2 13.0 %copy-start = (bf16[2048,256]{1,0:T(8,128)(2,1)S(1)}, bf16[2048,256]{1,0:T(8,128)(2,1)}, u32[]{:S(2)}) copy-start(bf16[2048,256]{1,0:T(8,128)(2,1)} %param.13) | copy-start | bytes 3145732
  7.2 24.8 %copy-start.2 = (bf16[128,2048]{1,0:T(8,128)(2,1)S(1)}, bf16[128,2048]{1,0:T(8,128)(2,1)}, u32[]{:S(2)}) copy-start(bf16[128,2048]{1,0:T(8,128)(2,1)} %param.11) | copy-start | bytes 1572868
  10.1 9.7 %all-to-all-start = ((bf16[8,2,1024]{2,1,0:T(2,128)(2,1)}), bf16[8,2,1024]{2,1,0:T(2,128)(2,1)S(1)}, u32[]{:S(2)}, u32[]{:S(2)}) async-start(bf16[8,2,1024]{2,1,0:T(2,128)(2,1)} %reshape.146), calls=%async_computation | async-start | bytes 65536 | tf_op jit(solution)/shard_map/all_to_all | solution.py:28
  14.4 93.6 %all-gather.2.cloned.1.call-start = ((), (), s32[]{:S(2)}) async-start(), calls=%async_computation.7 | async-start | bytes 2662400 | tf_op jit(solution)/shard_map/all_gather | solution.py:56
  22.5 9.4 %all-to-all-start.1 = ((bf16[8,4,2048]{2,1,0:T(4,128)(2,1)}), bf16[8,4,2048]{2,1,0:T(4,128)(2,1)S(1)}, u32[]{:S(2)}, u32[]{:S(2)}) async-start(bf16[8,4,2048]{2,1,0:T(4,128)(2,1)} %reshape.127), calls=%async_computation.1 | async-start | bytes 262144 | tf_op jit(solution)/shard_map/all_to_all | solution.py:66
  25.9 17.3 %copy-start.1 = (bf16[2048,1,128]{2,0,1:T(8,128)(2,1)S(1)}, bf16[2048,1,128]{2,0,1:T(8,128)(2,1)}, u32[]{:S(2)}) copy-start(bf16[2048,1,128]{2,0,1:T(8,128)(2,1)} %param.14) | copy-start | bytes 1572868
  33.7 9.4 %all-to-all-start.2 = ((bf16[8,4,2048]{2,1,0:T(4,128)(2,1)}), bf16[8,4,2048]{2,1,0:T(4,128)(2,1)S(1)}, u32[]{:S(2)}, u32[]{:S(2)}) async-start(bf16[8,4,2048]{2,1,0:T(4,128)(2,1)} %reshape.129), calls=%async_computation.2 | async-start | bytes 262144 | tf_op jit(solution)/shard_map/all_to_all | solution.py:71
  44.7 57.9 %copy-start.6 = (bf16[2048]{0:T(1024)(128)(2,1)S(1)}, bf16[2048]{0:T(1024)(128)(2,1)}, u32[]{:S(2)}) copy-start(bf16[2048]{0:T(1024)(128)(2,1)} %param.16) | copy-start | bytes 12292
  44.7 9.0 %all-to-all-start.3 = ((f32[8,8,256]{2,1,0:T(8,128)}), f32[8,8,256]{2,1,0:T(8,128)S(1)}, u32[]{:S(2)}, u32[]{:S(2)}) async-start(f32[8,8,256]{2,1,0:T(8,128)} %convolution_bitcast_fusion), calls=%async_computation.3 | async-start | bytes 131072 | tf_op jit(solution)/shard_map/all_to_all | solution.py:76
  53.7 51.6 %copy-start.5 = (bf16[8,256]{1,0:T(8,128)(2,1)}, bf16[8,256]{1,0:T(8,128)(2,1)S(1)}, u32[]{:S(2)}) copy-start(bf16[8,256]{1,0:T(8,128)(2,1)S(1)} %fusion.44) | copy-start | bytes 12292
  100.7 4.5 %collective-permute-start = (bf16[4,512,256]{1,2,0:T(8,128)(2,1)S(1)}, bf16[4,512,256]{1,2,0:T(8,128)(2,1)S(1)}, u32[]{:S(2)}, u32[]{:S(2)}) collective-permute-start(bf16[4,512,256]{1,2,0:T(8,128)(2,1)S(1)} %all_to_all.36), channel_id=1, source_target_pairs={{0,1},{1,0},{2,3},{3,2},{4,5},{5,4},{6,7},{7,6},{8,9},{9,8},{10,11... | collective-permute-start | bytes 3145736 | tf_op jit(solution)/shard_map/ppermute | solution.py:82
  106.6 3.8 %copy-start.7 = (s32[1,512]{1,0:T(1,128)S(1)}, s32[1,512]{1,0:T(1,128)}, u32[]{:S(2)}) copy-start(s32[1,512]{1,0:T(1,128)} %param.20) | copy-start | bytes 6148
  110.4 1.0 copy-start.4
  111.1 3.8 %copy-start.3 = (bf16[512,640]{1,0:T(8,128)(2,1)}, bf16[512,640]{1,0:T(8,128)(2,1)S(1)}, u32[]{:S(2)}) copy-start(bf16[512,640]{1,0:T(8,128)(2,1)S(1)} %convolution_convert_fusion.3) | copy-start | bytes 1966084
  120.4 4.8 %collective-permute-start.1 = (bf16[4,512,256]{1,2,0:T(8,128)(2,1)}, bf16[4,512,256]{1,2,0:T(8,128)(2,1)S(1)}, u32[]{:S(2)}, u32[]{:S(2)}) collective-permute-start(bf16[4,512,256]{1,2,0:T(8,128)(2,1)} %fusion.11), channel_id=1, source_target_pairs={{0,1},{1,0},{2,3},{3,2},{4,5},{5,4},{6,7},{7,6},{8,9},{9,8},{10,11... | collective-permute-start | bytes 3145736 | tf_op jit(solution)/shard_map/ppermute | solution.py:127
Sparse Core Ops, SparseCore 0:
  18.3 89.6 all-gather.1

commit v2 on v1

--- a/solution.py
+++ b/solution.py
@@ -50,10 +50,15 @@
     same_core = [[2 * x + c for x in range(n_x)] for c in range(2)]
     scale = 1.0 / math.sqrt(HEAD_DIM)
 
-    parts = jnp.concatenate(
-        [wq_user, wkv_user.reshape(wkv_user.shape[0], -1), wo_user.T], axis=1
-    )
-    weights_all = lax.all_gather(parts, "wide", axis=0, tiled=True)
+    wo_all = lax.all_gather(wo_user.T, "wide", axis=0, tiled=True)
+    size = math.isqrt(lax.axis_size("wide"))
+    same_y = [[y * size + z for z in range(size)] for y in range(size)]
+    same_z = [[y * size + z for y in range(size)] for z in range(size)]
+    depth = wq_user.shape[0]
+    wq_all = spread(wq_user, "wide", same_y).reshape(-1, wq_user.shape[1])
+    wq_all = spread(wq_all, "wide", same_z).reshape(width, -1)
+    wkv_all = spread(wkv_user.reshape(depth, -1), "wide", same_z).reshape(size * depth, -1)
+    wkv_all = spread(wkv_all, "wide", same_y).reshape(width, -1)
 
     last_raw = spread(item_states[TXT - 1 :], "narrow").reshape(n_narrow, width)
     last_normed = rms_scale(last_raw, item_gain)
@@ -72,39 +77,41 @@
     mixed = jnp.dot(pooled.reshape(-1, width), wv, preferred_element_type=jnp.float32)
     mixed = mixed.astype(jnp.bfloat16).reshape(n_narrow, -1)
     partial_sum = jnp.dot(mixed, wo_item, preferred_element_type=jnp.float32)
-    pieces = partial_sum.reshape(n_narrow, n_narrow, share).transpose(1, 0, 2)
-    total = jnp.sum(lax.all_to_all(pieces, "narrow", 0, 0), axis=0)
-    last_share = lax.dynamic_slice_in_dim(last_raw, me * share, share, 1)
-    item_part = (last_share.astype(jnp.float32) + total).astype(jnp.bfloat16)
-
-    catalog_part = spread(item_part, "wide").reshape(-1, share)
-    mine = spread(catalog_part, "narrow", same_core)
-    other = lax.ppermute(mine, "narrow", [(i, i ^ 1) for i in range(n_narrow)])
-    low = jnp.where(core == 0, mine, other)
-    high = jnp.where(core == 0, other, mine)
-    catalog = jnp.stack([low, high], axis=1).transpose(2, 0, 1, 3).reshape(-1, width)
-    user_normed = rms_scale(catalog, user_gain)
+    total = jnp.sum(spread(partial_sum.astype(jnp.bfloat16), "narrow").astype(jnp.float32), axis=0)
+    embedded = (last_raw.astype(jnp.float32) + total).astype(jnp.bfloat16)
+    item_part = lax.dynamic_slice_in_dim(embedded, me * share, share, 1)
+    user_normed = rms_scale(embedded, user_gain)
+    turned = user_normed.reshape(-1, size, size, depth).swapaxes(1, 2).reshape(-1, width)
 
     q_width = wq_user.shape[1]
     kv_width = 2 * HEAD_DIM
-    projected = jnp.dot(
-        user_normed, weights_all[:, : q_width + kv_width], preferred_element_type=jnp.float32
+    projected = jnp.concatenate(
+        [
+            jnp.dot(user_normed, wq_all, preferred_element_type=jnp.float32),
+            jnp.dot(turned, wkv_all, preferred_element_type=jnp.float32),
+        ],
+        axis=1,
     ).astype(jnp.bfloat16)
+    group = projected.shape[0]
+    catalog = spread(projected, "wide", same_y).reshape(size * group, -1)
+    catalog = spread(catalog, "wide", same_z).reshape(size * size * group, -1)
+    features = spread(item_part, "wide", same_z).reshape(size * group, -1)
+    features = spread(features, "wide", same_y).reshape(size * size * group, -1)
+
     item_ids = history_items[0]
     slots = item_ids.shape[0]
-    picks = (item_ids[:, None] == jnp.arange(catalog.shape[0], dtype=jnp.int32)[None, :]).astype(
-        jnp.bfloat16
-    )
-    rows = jnp.dot(
-        picks,
-        jnp.concatenate([projected, catalog_part], axis=1),
-        preferred_element_type=jnp.float32,
-    ).astype(jnp.bfloat16)
+    every = jnp.arange(catalog.shape[0], dtype=jnp.int32)[None, :]
+    picks = (item_ids[:, None] == every).astype(jnp.bfloat16)
+    rows = jnp.dot(picks, catalog, preferred_element_type=jnp.float32).astype(jnp.bfloat16)
+    y_of = item_ids // (size * group)
+    z_of = item_ids // group % size
+    turned_ids = (z_of * size + y_of) * group + item_ids % group
+    turned_picks = (turned_ids[:, None] == every).astype(jnp.bfloat16)
+    residual = jnp.dot(turned_picks, features, preferred_element_type=jnp.float32)
     heads = q_width // HEAD_DIM
     user_queries = rows[:, :q_width].reshape(slots, heads, HEAD_DIM)
     keys = rows[:, q_width : q_width + HEAD_DIM]
-    values = rows[:, q_width + HEAD_DIM : q_width + kv_width]
-    residual = rows[:, q_width + kv_width :]
+    values = rows[:, q_width + HEAD_DIM :]
     length = history_lengths[0]
     user_scores = jnp.einsum(
         "ird,jd->rij", user_queries, keys, preferred_element_type=jnp.float32
@@ -117,7 +124,7 @@
         "rij,jd->ird", user_attn, values, preferred_element_type=jnp.float32
     ).astype(jnp.bfloat16).reshape(slots, -1)
 
-    wo_t = weights_all[:, q_width + kv_width :].reshape(n_x, 2, share, -1)
+    wo_t = wo_all.reshape(n_x, 2, share, -1)
     wo_mine = lax.dynamic_index_in_dim(wo_t, core, 1, keepdims=False)
     wo_other = lax.dynamic_index_in_dim(wo_t, 1 - core, 1, keepdims=False)
 
@@ -131,7 +138,7 @@
     shares = lax.all_to_all(pair, "narrow", 0, 0, axis_index_groups=same_core)
     summed = jnp.sum(shares.astype(jnp.float32), axis=0)
     live = (index < length)[:, None]
-    user_states = jnp.where(live, residual.astype(jnp.float32) + summed, 0.0).astype(jnp.bfloat16)
+    user_states = jnp.where(live, residual + summed, 0.0).astype(jnp.bfloat16)
     return (item_part, user_states)
 
 

time: 155 us -> 255 us (1.65)
  the two profiles are of different devices: /device:TPU:16 before, /device:TPU:2 now
where the time goes in v2:
time: 255 us; the launch traced here: 253 us
  waiting for transfers between devices  100 us (39%)
  blocking collectives  62.8 us (25%)
  starting transfers between devices  44.9 us (18%)
  matrix products  17.8 us (7%)
  between operations  15 us (6%)
  local copies, waits for them, and re-layouts  7.92 us (3%)
  other arithmetic  4.53 us (2%)
    all_to_all x6, waiting for transfers between devices, spread(): return lax.all_to_all(copies, axis, 0, 0, axis_index_groups=groups)  65.6 us
    all_to_all x4, blocking collectives, spread(): return lax.all_to_all(copies, axis, 0, 0, axis_index_groups=groups)  54.3 us
    all_to_all x6, starting transfers between devices, spread(): return lax.all_to_all(copies, axis, 0, 0, axis_index_groups=groups)  33.4 us
    all_gather x1, waiting for transfers between devices, local(): wo_all = lax.all_gather(wo_user.T, 'wide', axis=0, tiled=True)  18.6 us
    all_to_all x1, waiting for transfers between devices, local(): shares = lax.all_to_all(pair, 'narrow', 0, 0, axis_index_groups=same_core)  10.8 us
    all_to_all x1, blocking collectives, local(): lax.all_to_all(pooled.reshape(n_narrow, per, width), 'narrow', 0, 0)  8.51 us
  transfers between devices with their start and end apart: 10, of which 9 were waited for; matrix products, arithmetic and copies ran while one was open for 6% of the time, Pallas kernels for 0%

profile of v2, /device:TPU:2, one launch (start us, length us, event | category | flops | bytes accessed | tf_op | source)
XLA Modules:
  0.0 253.3 jit_solution(9961872457947225013)
XLA Ops:
  7.2 0.9 slice_reduce_fusion
  8.2 0.5 broadcast.212
  8.7 0.8 reduce.2
  9.5 0.6 reshape.263
  10.2 9.2 %all-to-all-start = ((bf16[8,2,1024]{2,1,0:T(2,128)(2,1)}), bf16[8,2,1024]{2,1,0:T(2,128)(2,1)S(1)}, u32[]{:S(2)}, u32[]{:S(2)}) async-start(bf16[8,2,1024]{2,1,0:T(2,128)(2,1)} %reshape.263), calls=%async_computation | async-start | bytes 65536 | tf_op jit(solution)/shard_map/all_to_all | solution.py:28
  19.3 1.2 fusion.9
  20.6 0.7 convert_element_type.119
  21.3 2.1 all-to-all-done
  23.5 1.5 convolution_convert_fusion.7
  25.1 1.3 convolution_convert_fusion.1
  26.4 0.7 reshape.243
  27.2 4.7 %all-to-all-start.1 = ((bf16[8,4,2048]{2,1,0:T(4,128)(2,1)}), bf16[8,4,2048]{2,1,0:T(4,128)(2,1)S(1)}, u32[]{:S(2)}, u32[]{:S(2)}) async-start(bf16[8,4,2048]{2,1,0:T(4,128)(2,1)} %reshape.243), calls=%async_computation.1 | async-start | bytes 262144 | tf_op jit(solution)/shard_map/all_to_all | solution.py:71
  31.9 4.7 %all-to-all-done.1 = bf16[8,4,2048]{2,1,0:T(4,128)(2,1)S(1)} async-done(((bf16[8,4,2048]{2,1,0:T(4,128)(2,1)}), bf16[8,4,2048]{2,1,0:T(4,128)(2,1)S(1)}, u32[]{:S(2)}, u32[]{:S(2)}) %all-to-all-start.1) | async-done | bytes 131104 | tf_op jit(solution)/shard_map/all_to_all | solution.py:71
  36.6 1.5 fusion.59
  38.4 0.3 convolution_convert_fusion
  38.8 8.5 %all_to_all.65 = bf16[8,4,2048]{2,1,0:T(4,128)(2,1)S(1)} all-to-all(bf16[8,4,2048]{2,1,0:T(4,128)(2,1)S(1)} %reshape.245), channel_id=1, replica_groups=mesh['wide'=64,'narrow'=8] {'narrow'}, dimensions={0} | all-to-all | bytes 262144 | tf_op jit(solution)/shard_map/all_to_all | solution.py:76
  47.3 0.6 broadcast_in_dim.63
  47.9 3.4 %all-to-all-start.8 = ((bf16[8,32,128]{2,1,0:T(8,128)(2,1)}), bf16[8,32,128]{2,1,0:T(8,128)(2,1)S(1)}, u32[]{:S(2)}, u32[]{:S(2)}) async-start(bf16[8,32,128]{2,1,0:T(8,128)(2,1)} %broadcast_in_dim.63), calls=%async_computation.8 | async-start | bytes 131072 | tf_op jit(solution)/shard_map/all_to_all | solution.py:28
  51.3 0.3 convolution_convert_fusion.5
  51.8 7.8 %all-to-all-done.8 = bf16[8,32,128]{2,1,0:T(8,128)(2,1)S(1)} async-done(((bf16[8,32,128]{2,1,0:T(8,128)(2,1)}), bf16[8,32,128]{2,1,0:T(8,128)(2,1)S(1)}, u32[]{:S(2)}, u32[]{:S(2)}) %all-to-all-start.8) | async-done | bytes 65568 | tf_op jit(solution)/shard_map/all_to_all | solution.py:28
  59.6 0.7 broadcast_in_dim.59
  60.2 9.8 %all-to-all-start.6 = ((bf16[8,32,256]{2,1,0:T(8,128)(2,1)}), bf16[8,32,256]{2,1,0:T(8,128)(2,1)S(1)}, u32[]{:S(2)}, u32[]{:S(2)}) async-start(bf16[8,32,256]{2,1,0:T(8,128)(2,1)} %broadcast_in_dim.59), calls=%async_computation.6 | async-start | bytes 262144 | tf_op jit(solution)/shard_map/all_to_all | solution.py:28
  70.3 8.8 %all-to-all-done.6 = bf16[8,32,256]{2,1,0:T(8,128)(2,1)S(1)} async-done(((bf16[8,32,256]{2,1,0:T(8,128)(2,1)}), bf16[8,32,256]{2,1,0:T(8,128)(2,1)S(1)}, u32[]{:S(2)}, u32[]{:S(2)}) %all-to-all-start.6) | async-done | bytes 131104 | tf_op jit(solution)/shard_map/all_to_all | solution.py:28
  79.1 9.9 %all_to_all.66 = bf16[8,8,2048]{2,1,0:T(8,128)(2,1)S(1)} all-to-all(bf16[8,8,2048]{2,1,0:T(8,128)(2,1)S(1)} %broadcast_in_dim.50), channel_id=1, replica_groups=mesh['wide'=64,'narrow'=8] {'narrow'}, dimensions={0} | all-to-all | bytes 524288 | tf_op jit(solution)/shard_map/all_to_all | solution.py:28
  89.2 19.8 %all_to_all.67 = bf16[8,256,128]{2,1,0:T(8,128)(2,1)S(1)} all-to-all(bf16[8,256,128]{2,1,0:T(8,128)(2,1)S(1)} %broadcast_in_dim.121), channel_id=1, replica_groups={{0,8,16,24,32,40,48,56},{64,72,80,88,96,104,112,120},{128,136,144,152,1..., dimensions={0} | all-to-all | bytes 1048576 | tf_op jit(solution)/shard_map/all_to_all | solution.py:28
  109.0 1.1 broadcast_in_dim.61
  110.0 3.6 %all-to-all-start.7 = ((bf16[8,256,256]{2,1,0:T(8,128)(2,1)}), bf16[8,256,256]{2,1,0:T(8,128)(2,1)S(1)}, u32[]{:S(2)}, u32[]{:S(2)}) async-start(bf16[8,256,256]{2,1,0:T(8,128)(2,1)} %broadcast_in_dim.61), calls=%async_computation.7 | async-start | bytes 2097152 | tf_op jit(solution)/shard_map/all_to_all | solution.py:28
  113.6 0.7 all-gather.2.cloned.1.call-update
  115.4 25.4 %all-to-all-done.7 = bf16[8,256,256]{2,1,0:T(8,128)(2,1)S(1)} async-done(((bf16[8,256,256]{2,1,0:T(8,128)(2,1)}), bf16[8,256,256]{2,1,0:T(8,128)(2,1)S(1)}, u32[]{:S(2)}, u32[]{:S(2)}) %all-to-all-start.7) | async-done | bytes 1048608 | tf_op jit(solution)/shard_map/all_to_all | solution.py:28
  141.1 11.1 %all_to_all.68 = bf16[8,8,384]{2,1,0:T(8,128)(2,1)S(1)} all-to-all(bf16[8,8,384]{2,1,0:T(8,128)(2,1)S(1)} %broadcast_in_dim.122), channel_id=1, replica_groups={{0,8,16,24,32,40,48,56},{64,72,80,88,96,104,112,120},{128,136,144,152,1..., dimensions={0} | all-to-all | bytes 98304 | tf_op jit(solution)/shard_map/all_to_all | solution.py:28
  152.1 0.8 broadcast_in_dim.124
  152.9 3.5 %all-to-all-start.11 = ((bf16[8,64,384]{2,1,0:T(8,128)(2,1)}), bf16[8,64,384]{2,1,0:T(8,128)(2,1)S(1)}, u32[]{:S(2)}, u32[]{:S(2)}) async-start(bf16[8,64,384]{2,1,0:T(8,128)(2,1)} %broadcast_in_dim.124), calls=%async_computation.11 | async-start | bytes 786432 | tf_op jit(solution)/shard_map/all_to_all | solution.py:28
  157.2 12.8 %all-to-all-done.11 = bf16[8,64,384]{2,1,0:T(8,128)(2,1)S(1)} async-done(((bf16[8,64,384]{2,1,0:T(8,128)(2,1)}), bf16[8,64,384]{2,1,0:T(8,128)(2,1)S(1)}, u32[]{:S(2)}, u32[]{:S(2)}) %all-to-all-start.11) | async-done | bytes 393248 | tf_op jit(solution)/shard_map/all_to_all | solution.py:28
  170.0 0.6 convolution_convert_fusion.4
  170.6 3.6 %fusion.60 = (f32[4,512]{1,0:T(4,128)S(1)}, f32[4,512,512]{1,2,0:T(8,128)}) fusion(pred[512,512]{0,1:T(8,128)(4,1)S(1)} %fusion.13, bf16[512,4,64]{0,2,1:T(8,128)(2,1)S(1)} %bitcast.124, bf16[512,384]{0,1:T(8,128)(2,1)S(1)} %convolution_convert_fusion.4), kind=kOutput, calls=%fused_computation.106 | convolution fusion | flops 138412544 | bytes 4792320 | tf_op jit(solution)/shard_map/sub | solution.py:122
  174.2 2.7 %fusion.8 = bf16[64,4,512]{2,0,1:T(8,128)(2,1)S(1)} fusion(f32[4,512,512]{1,2,0:T(8,128)} %get-tuple-element.9, f32[4,512]{1,0:T(4,128)S(1)} %get-tuple-element.8, bf16[512,384]{0,1:T(8,128)(2,1)S(1)} %convolution_convert_fusion.4), kind=kOutput, calls=%fused_computation.20 | convolution fusion | flops 136445952 | bytes 4530176 | tf_op jit(solution)/shard_map/rij,jd->ird/dot_general | solution.py:123
  176.8 18.6 %all-gather.2.cloned.1.call-done = bf16[2048,256]{1,0:T(8,128)(2,1)} async-done(((bf16[32,256]{1,0:T(8,128)(2,1)}), bf16[2048,256]{1,0:T(8,128)(2,1)}) %all-gather.2.cloned.1.call-update) | async-done | bytes 1048592 | tf_op jit(solution)/shard_map/all_gather | solution.py:53
  195.4 2.5 fusion.7
  197.9 1.9 collective-permute-start
  199.9 13.5 %all_to_all.69 = bf16[8,8,256]{2,1,0:T(8,128)(2,1)S(1)} all-to-all(bf16[8,8,256]{2,1,0:T(8,128)(2,1)S(1)} %broadcast_in_dim.52), channel_id=1, replica_groups={{0,64,128,192,256,320,384,448},{8,72,136,200,264,328,392,456},{16,80,14..., dimensions={0} | all-to-all | bytes 65536 | tf_op jit(solution)/shard_map/all_to_all | solution.py:28
  213.4 0.7 broadcast_in_dim.58
  214.1 4.1 %all-to-all-start.5 = ((bf16[8,64,256]{2,1,0:T(8,128)(2,1)}), bf16[8,64,256]{2,1,0:T(8,128)(2,1)S(1)}, u32[]{:S(2)}, u32[]{:S(2)}) async-start(bf16[8,64,256]{2,1,0:T(8,128)(2,1)} %broadcast_in_dim.58), calls=%async_computation.5 | async-start | bytes 524288 | tf_op jit(solution)/shard_map/all_to_all | solution.py:28
  218.2 2.5 fusion.2
  220.7 8.6 %all-to-all-done.5 = bf16[8,64,256]{2,1,0:T(8,128)(2,1)S(1)} async-done(((bf16[8,64,256]{2,1,0:T(8,128)(2,1)}), bf16[8,64,256]{2,1,0:T(8,128)(2,1)S(1)}, u32[]{:S(2)}, u32[]{:S(2)}) %all-to-all-start.5) | async-done | bytes 262176 | tf_op jit(solution)/shard_map/all_to_all | solution.py:28
  229.3 4.8 %all-to-all-start.12 = ((bf16[4,512,256]{1,2,0:T(8,128)(2,1)}), bf16[4,512,256]{1,2,0:T(8,128)(2,1)S(1)}, u32[]{:S(2)}, u32[]{:S(2)}) async-start(bf16[4,512,256]{1,2,0:T(8,128)(2,1)} %fusion.2), calls=%async_computation.12 | async-start | bytes 2097152 | tf_op jit(solution)/shard_map/all_to_all | solution.py:138
  234.2 0.4 fusion.12
  234.5 10.8 %all-to-all-done.12 = bf16[4,512,256]{1,2,0:T(8,128)(2,1)S(1)} async-done(((bf16[4,512,256]{1,2,0:T(8,128)(2,1)}), bf16[4,512,256]{1,2,0:T(8,128)(2,1)S(1)}, u32[]{:S(2)}, u32[]{:S(2)}) %all-to-all-start.12) | async-done | bytes 1048608 | tf_op jit(solution)/shard_map/all_to_all | solution.py:138
  245.7 0.8 select_convert_fusion
  (54 shorter events, 2.9 us)
Async XLA Ops:
  7.2 62.9 %copy-start = (bf16[256,2048]{1,0:T(8,128)(2,1)S(1)}, bf16[256,2048]{1,0:T(8,128)(2,1)}, u32[]{:S(2)}) copy-start(bf16[256,2048]{1,0:T(8,128)(2,1)} %param.15) | copy-start | bytes 3145732
  7.2 31.2 %copy-start.2 = (bf16[128,2048]{1,0:T(8,128)(2,1)S(1)}, bf16[128,2048]{1,0:T(8,128)(2,1)}, u32[]{:S(2)}) copy-start(bf16[128,2048]{1,0:T(8,128)(2,1)} %param.11) | copy-start | bytes 1572868
  7.2 44.1 %copy-start.1 = (bf16[2048,1,128]{2,0,1:T(8,128)(2,1)S(1)}, bf16[2048,1,128]{2,0,1:T(8,128)(2,1)}, u32[]{:S(2)}) copy-start(bf16[2048,1,128]{2,0,1:T(8,128)(2,1)} %param.14) | copy-start | bytes 1572868
  7.2 40.1 %copy-start.6 = (bf16[32,1,128]{2,0,1:T(8,128)(2,1)S(1)}, bf16[32,1,128]{2,0,1:T(8,128)(2,1)}, u32[]{:S(2)}) copy-start(bf16[32,1,128]{2,0,1:T(8,128)(2,1)} %param.18) | copy-start | bytes 24580
  7.2 52.4 %copy-start.3 = (bf16[32,256]{1,0:T(8,128)(2,1)S(1)}, bf16[32,256]{1,0:T(8,128)(2,1)}, u32[]{:S(2)}) copy-start(bf16[32,256]{1,0:T(8,128)(2,1)} %param.17) | copy-start | bytes 49156
  10.2 13.2 %all-to-all-start = ((bf16[8,2,1024]{2,1,0:T(2,128)(2,1)}), bf16[8,2,1024]{2,1,0:T(2,128)(2,1)S(1)}, u32[]{:S(2)}, u32[]{:S(2)}) async-start(bf16[8,2,1024]{2,1,0:T(2,128)(2,1)} %reshape.263), calls=%async_computation | async-start | bytes 65536 | tf_op jit(solution)/shard_map/all_to_all | solution.py:28
  27.2 9.4 %all-to-all-start.1 = ((bf16[8,4,2048]{2,1,0:T(4,128)(2,1)}), bf16[8,4,2048]{2,1,0:T(4,128)(2,1)S(1)}, u32[]{:S(2)}, u32[]{:S(2)}) async-start(bf16[8,4,2048]{2,1,0:T(4,128)(2,1)} %reshape.243), calls=%async_computation.1 | async-start | bytes 262144 | tf_op jit(solution)/shard_map/all_to_all | solution.py:71
  47.3 67.1 %copy-start.4 = (bf16[2048]{0:T(1024)(128)(2,1)S(1)}, bf16[2048]{0:T(1024)(128)(2,1)}, u32[]{:S(2)}) copy-start(bf16[2048]{0:T(1024)(128)(2,1)} %param.16) | copy-start | bytes 12292
  47.9 11.7 %all-to-all-start.8 = ((bf16[8,32,128]{2,1,0:T(8,128)(2,1)}), bf16[8,32,128]{2,1,0:T(8,128)(2,1)S(1)}, u32[]{:S(2)}, u32[]{:S(2)}) async-start(bf16[8,32,128]{2,1,0:T(8,128)(2,1)} %broadcast_in_dim.63), calls=%async_computation.8 | async-start | bytes 131072 | tf_op jit(solution)/shard_map/all_to_all | solution.py:28
  60.2 18.9 %all-to-all-start.6 = ((bf16[8,32,256]{2,1,0:T(8,128)(2,1)}), bf16[8,32,256]{2,1,0:T(8,128)(2,1)S(1)}, u32[]{:S(2)}, u32[]{:S(2)}) async-start(bf16[8,32,256]{2,1,0:T(8,128)(2,1)} %broadcast_in_dim.59), calls=%async_computation.6 | async-start | bytes 262144 | tf_op jit(solution)/shard_map/all_to_all | solution.py:28
  109.0 61.0 %copy-start.7 = (s32[1,512]{1,0:T(1,128)S(1)}, s32[1,512]{1,0:T(1,128)}, u32[]{:S(2)}) copy-start(s32[1,512]{1,0:T(1,128)} %param.20) | copy-start | bytes 6148
  110.0 30.7 %all-to-all-start.7 = ((bf16[8,256,256]{2,1,0:T(8,128)(2,1)}), bf16[8,256,256]{2,1,0:T(8,128)(2,1)S(1)}, u32[]{:S(2)}, u32[]{:S(2)}) async-start(bf16[8,256,256]{2,1,0:T(8,128)(2,1)} %broadcast_in_dim.61), calls=%async_computation.7 | async-start | bytes 2097152 | tf_op jit(solution)/shard_map/all_to_all | solution.py:28
  113.6 81.9 %all-gather.2.cloned.1.call-start = ((), (), s32[]{:S(2)}) async-start(), calls=%async_computation.13 | async-start | bytes 1064960 | tf_op jit(solution)/shard_map/all_gather | solution.py:53
  152.9 17.1 %all-to-all-start.11 = ((bf16[8,64,384]{2,1,0:T(8,128)(2,1)}), bf16[8,64,384]{2,1,0:T(8,128)(2,1)S(1)}, u32[]{:S(2)}, u32[]{:S(2)}) async-start(bf16[8,64,384]{2,1,0:T(8,128)(2,1)} %broadcast_in_dim.124), calls=%async_computation.11 | async-start | bytes 786432 | tf_op jit(solution)/shard_map/all_to_all | solution.py:28
  197.9 20.3 %collective-permute-start = (bf16[4,512,256]{1,2,0:T(8,128)(2,1)}, bf16[4,512,256]{1,2,0:T(8,128)(2,1)S(1)}, u32[]{:S(2)}, u32[]{:S(2)}) collective-permute-start(bf16[4,512,256]{1,2,0:T(8,128)(2,1)} %fusion.7), channel_id=1, source_target_pairs={{0,1},{1,0},{2,3},{3,2},{4,5},{5,4},{6,7},{7,6},{8,9},{9,8},{10,11... | collective-permute-start | bytes 3145736 | tf_op jit(solution)/shard_map/ppermute | solution.py:134
  199.9 45.8 %copy-start.5 = (bf16[8,256]{1,0:T(8,128)(2,1)}, bf16[8,256]{1,0:T(8,128)(2,1)S(1)}, u32[]{:S(2)}) copy-start(bf16[8,256]{1,0:T(8,128)(2,1)S(1)} %constant_dynamic-slice_fusion) | copy-start | bytes 12292
  214.1 15.2 %all-to-all-start.5 = ((bf16[8,64,256]{2,1,0:T(8,128)(2,1)}), bf16[8,64,256]{2,1,0:T(8,128)(2,1)S(1)}, u32[]{:S(2)}, u32[]{:S(2)}) async-start(bf16[8,64,256]{2,1,0:T(8,128)(2,1)} %broadcast_in_dim.58), calls=%async_computation.5 | async-start | bytes 524288 | tf_op jit(solution)/shard_map/all_to_all | solution.py:28
  229.3 16.0 %all-to-all-start.12 = ((bf16[4,512,256]{1,2,0:T(8,128)(2,1)}), bf16[4,512,256]{1,2,0:T(8,128)(2,1)S(1)}, u32[]{:S(2)}, u32[]{:S(2)}) async-start(bf16[4,512,256]{1,2,0:T(8,128)(2,1)} %fusion.2), calls=%async_computation.12 | async-start | bytes 2097152 | tf_op jit(solution)/shard_map/all_to_all | solution.py:138
Sparse Core Ops, SparseCore 0:
  117.4 77.9 all-gather.1

commit v3 on v1

v3 whole, which is shorter than its diff:
```python
import math

import jax
import jax.numpy as jnp
from jax import lax
from jax.experimental import pallas as pl
from jax.experimental.pallas import tpu as pltpu
from jax.sharding import Mesh
from jax.sharding import PartitionSpec as P

HEAD_DIM = 64
TXT = 128
epsilon = 1e-05
VMEM_LIMIT = 40 * 1024 * 1024
WIDE = ("yh", "yl", "z")
NARROW = ("x", "core")


def rms_scale(values, gain):
    wide = values.astype(jnp.float32)
    power = jnp.mean(wide * wide, axis=-1, keepdims=True)
    return (wide * lax.rsqrt(power + epsilon) * gain.astype(jnp.float32)).astype(jnp.bfloat16)


def dot_t(left, right):
    return lax.dot_general(
        left, right, (((1,), (1,)), ((), ())), preferred_element_type=jnp.float32
    )


def spread(values, axis):
    copies = jnp.broadcast_to(values[None], (lax.axis_size(axis),) + values.shape)
    return lax.all_to_all(copies, axis, 0, 0)


def swap_cores(values):
    return lax.ppermute(values, "core", [(0, 1), (1, 0)])


def norm_kernel(core_ref, mine_ref, other_ref, gain_ref, out_ref):
    core = core_ref[0]
    pairs, n_x, rows, share = mine_ref.shape
    width = 2 * n_x * share
    for p in range(pairs):
        power = jnp.zeros((rows, share), jnp.float32)
        for x in range(n_x):
            for ref in (mine_ref, other_ref):
                block = ref[p, x].astype(jnp.float32)
                power = power + block * block
        factor = lax.rsqrt(jnp.sum(power, axis=1, keepdims=True) / width + epsilon)
        for x in range(n_x):
            for ref, where in ((mine_ref, 2 * x + core), (other_ref, 2 * x + 1 - core)):
                columns = pl.ds(pl.multiple_of(where * share, share), share)
                gain = gain_ref[:, columns].astype(jnp.float32)
                block = ref[p, x].astype(jnp.float32) * factor * gain
                out_ref[p * rows : (p + 1) * rows, columns] = block.astype(jnp.bfloat16)


def user_kernel(scalar_ref, normed_ref, weights_ref, places_ref, mixed_ref, terms_ref, picked_ref):
    length, core = scalar_ref[0], scalar_ref[1]
    slots, q_width = mixed_ref.shape
    share = terms_ref.shape[2]
    kv_at = q_width + 2 * HEAD_DIM
    projected = jnp.dot(
        normed_ref[...], weights_ref[:, :kv_at], preferred_element_type=jnp.float32
    ).astype(jnp.bfloat16)
    catalog = normed_ref.shape[0]
    every = lax.broadcasted_iota(jnp.int32, (slots, catalog), 1)
    picks = jnp.where(places_ref[...] == every, 1.0, 0.0).astype(jnp.bfloat16)
    picked_ref[...] = jnp.dot(picks, projected, preferred_element_type=jnp.float32).astype(
        jnp.bfloat16
    )
    scale = 1.0 / math.sqrt(HEAD_DIM)
    chunk = min(slots, 256)
    for start in range(0, slots, chunk):
        upto = start + chunk
        keys = picked_ref[:upto, q_width : q_width + HEAD_DIM]
        values = picked_ref[:upto, q_width + HEAD_DIM : kv_at]
        row = start + lax.broadcasted_iota(jnp.int32, (chunk, upto), 0)
        column = lax.broadcasted_iota(jnp.int32, (chunk, upto), 1)
        allowed = (column <= row) & (column < length)
        for head in range(q_width // HEAD_DIM):
            lanes = slice(head * HEAD_DIM, (head + 1) * HEAD_DIM)
            scores = dot_t(picked_ref[start:upto, lanes], keys) * scale
            scores = jnp.where(allowed, scores, -1e30)
            top = jnp.max(scores, axis=1, keepdims=True)
            parts = jnp.exp(scores - top)
            total = jnp.sum(parts, axis=1, keepdims=True)
            mixed = jnp.dot(parts.astype(jnp.bfloat16), values, preferred_element_type=jnp.float32)
            mixed_ref[start:upto, lanes] = (mixed / total).astype(jnp.bfloat16)
    for x in range(terms_ref.shape[0]):
        rows = pl.ds(pl.multiple_of((2 * x + 1 - core) * share, share), share)
        terms = dot_t(mixed_ref[...], weights_ref[rows, kv_at:])
        terms_ref[x] = terms.astype(jnp.bfloat16)


def pair_kernel(core_ref, mixed_ref, weights_ref, theirs_ref, pair_ref):
    core = core_ref[0]
    share = pair_ref.shape[2]
    for x in range(pair_ref.shape[0]):
        rows = pl.ds(pl.multiple_of((2 * x + core) * share, share), share)
        terms = dot_t(mixed_ref[...], weights_ref[rows, -mixed_ref.shape[1] :])
        pair_ref[x] = (terms + theirs_ref[x].astype(jnp.float32)).astype(jnp.bfloat16)


SMEM = pl.BlockSpec(memory_space=pltpu.SMEM)
VMEM = pl.BlockSpec(memory_space=pltpu.VMEM)


def call(kernel, name, outs, ins, scratch=()):
    return pl.pallas_call(
        kernel,
        name=name,
        out_shape=outs,
        in_specs=[SMEM] + [VMEM] * (len(ins) - 1),
        out_specs=jax.tree.map(lambda _: VMEM, outs),
        scratch_shapes=scratch,
        compiler_params=pltpu.CompilerParams(vmem_limit_bytes=VMEM_LIMIT),
    )(*ins)


def local(
    item_states,
    item_gain,
    wq_item,
    wkv_item,
    wo_item,
    user_gain,
    wq_user,
    wkv_user,
    wo_user,
    history_items,
    history_lengths,
):
    width = item_states.shape[1]
    n_x = lax.axis_size("x")
    n_narrow = 2 * n_x
    share = width // n_narrow
    core = lax.axis_index("core")
    me = lax.axis_index("x") * 2 + core
    scale = 1.0 / math.sqrt(HEAD_DIM)

    parts = jnp.concatenate(
        [wq_user, wkv_user.reshape(wkv_user.shape[0], -1), wo_user.T], axis=1
    )
    parts, last_row = lax.optimization_barrier((parts, item_states[TXT - 1 :]))
    weights_all = lax.all_gather(parts, WIDE, axis=0, tiled=True)

    last_raw = spread(last_row, NARROW).reshape(n_narrow, width)
    last_normed = rms_scale(last_raw, item_gain)
    queries = jnp.dot(last_normed, wq_item, preferred_element_type=jnp.float32)
    queries = queries.astype(jnp.bfloat16)
    per = queries.shape[1] // HEAD_DIM
    wk = wkv_item[:, 0, :HEAD_DIM]
    wv = wkv_item[:, 0, HEAD_DIM:]
    probes = dot_t(queries.reshape(-1, HEAD_DIM), wk).astype(jnp.bfloat16)
    probes = lax.all_to_all(probes.reshape(n_narrow, per, width), NARROW, 0, 0)
    normed = rms_scale(item_states, item_gain)
    scores = dot_t(probes.reshape(-1, width), normed) * scale
    attn = jax.nn.softmax(scores, axis=-1).astype(jnp.bfloat16)
    pooled = jnp.dot(attn, normed, preferred_element_type=jnp.float32).astype(jnp.bfloat16)
    pooled = lax.all_to_all(pooled.reshape(n_narrow, per, width), NARROW, 0, 0)
    mixed = jnp.dot(pooled.reshape(-1, width), wv, preferred_element_type=jnp.float32)
    mixed = mixed.astype(jnp.bfloat16).reshape(n_narrow, -1)
    partial_sum = jnp.dot(mixed, wo_item, preferred_element_type=jnp.float32)
    pieces = partial_sum.reshape(n_narrow, n_narrow, share).transpose(1, 0, 2)
    total = jnp.sum(lax.all_to_all(pieces, NARROW, 0, 0), axis=0)
    last_share = lax.dynamic_slice_in_dim(last_raw, me * share, share, 1)
    item_part = (last_share.astype(jnp.float32) + total).astype(jnp.bfloat16)

    n_z, n_pair, n_far = lax.axis_size("z"), lax.axis_size("yl"), lax.axis_size("yh")
    group = item_part.shape[0]
    block = spread(item_part, "z").reshape(n_z * group, share)
    block = spread(block, "yh").reshape(n_far * n_z * group, share)
    mine = spread(block, ("yl", "x")).reshape(n_pair, n_x, -1, share)
    other = swap_cores(mine)
    core_one = core[None].astype(jnp.int32)
    catalog = n_pair * mine.shape[2]
    user_normed = call(
        norm_kernel,
        "norm_catalog",
        jax.ShapeDtypeStruct((catalog, width), jnp.bfloat16),
        (core_one, mine, other, user_gain[None]),
    )

    item_ids = history_items[0]
    slots = item_ids.shape[0]
    length = history_lengths[0]
    of_y, in_y = item_ids // (n_z * group), item_ids % (n_z * group)
    places = ((of_y % n_pair) * n_far + of_y // n_pair) * (n_z * group) + in_y
    user_mixed, theirs = call(
        user_kernel,
        "user_attention",
        (
            jax.ShapeDtypeStruct((slots, wq_user.shape[1]), jnp.bfloat16),
            jax.ShapeDtypeStruct((n_x, slots, share), jnp.bfloat16),
        ),
        (
            jnp.stack([length, core]).astype(jnp.int32),
            user_normed,
            weights_all,
            places[:, None],
        ),
        [pltpu.VMEM((slots, wq_user.shape[1] + 2 * HEAD_DIM), jnp.bfloat16)],
    )

    theirs = swap_cores(theirs)
    pair = call(
        pair_kernel,
        "pair_sum",
        jax.ShapeDtypeStruct(theirs.shape, jnp.bfloat16),
        (core_one, user_mixed, weights_all, theirs),
    )
    shares = lax.all_to_all(pair, "x", 0, 0)
    own = lax.dynamic_index_in_dim(mine, lax.axis_index("x"), 1, keepdims=False)
    picks = (places[:, None] == jnp.arange(catalog, dtype=jnp.int32)[None, :]).astype(jnp.bfloat16)
    residual = jnp.dot(picks, own.reshape(-1, share), preferred_element_type=jnp.float32)
    summed = jnp.sum(shares.astype(jnp.float32), axis=0)
    live = (jnp.arange(slots, dtype=jnp.int32) < length)[:, None]
    user_states = jnp.where(live, residual + summed, 0.0).astype(jnp.bfloat16)
    return (item_part, user_states)


def solution(mesh):
    n_wide, n_narrow = mesh.shape["wide"], mesh.shape["narrow"]
    side = math.isqrt(n_wide)
    fine = Mesh(
        mesh.devices.reshape(side // 2, 2, n_wide // side, n_narrow // 2, 2), WIDE + NARROW
    )
    return jax.shard_map(
        local,
        mesh=fine,
        in_specs=(
            P(WIDE + NARROW, None),
            P(),
            P(None, NARROW),
            P(None, NARROW, None),
            P(NARROW, None),
            P(),
            P(WIDE, NARROW),
            P(WIDE, NARROW, None),
            P(NARROW, WIDE),
            P(WIDE, None),
            P(WIDE),
        ),
        out_specs=(P(WIDE, NARROW), P(WIDE, NARROW)),
        check_vma=False,
    )
```

time: 155 us -> 163 us (1.052)
  the two profiles are of different devices: /device:TPU:16 before, /device:TPU:1 now
where the time goes in v3:
time: 163 us; the launch traced here: 162 us
  blocking collectives  46.9 us (29%)
  starting transfers between devices  36.3 us (22%)
  waiting for transfers between devices  33.4 us (20%)
  between operations  14.9 us (9%)
  local copies, waits for them, and re-layouts  13.4 us (8%)
  Pallas kernels  7.06 us (4%)
  other arithmetic  6.26 us (4%)
  matrix products  3.77 us (2%)
    all_to_all x3, blocking collectives, spread(): return lax.all_to_all(copies, axis, 0, 0)  46.9 us
    all_to_all x1, waiting for transfers between devices, local(): shares = lax.all_to_all(pair, 'x', 0, 0)  14 us
    ppermute x2, starting transfers between devices, swap_cores(): return lax.ppermute(values, 'core', [(0, 1), (1, 0)])  10.2 us
    all_to_all x1, starting transfers between devices, spread(): return lax.all_to_all(copies, axis, 0, 0)  10.1 us
    pallas_call x3, Pallas kernels, call(): pl.pallas_call(kernel, name=name, out_shape=outs, in_specs=[SMEM] + [VMEM...  7.06 us
    unnamed x26, local copies, waits for them, and re-layouts  6.85 us
    all_to_all x1, waiting for transfers between devices, local(): probes = lax.all_to_all(probes.reshape(n_narrow, per, width), NARROW, 0, 0)  5.29 us
    all_to_all x1, waiting for transfers between devices, local(): total = jnp.sum(lax.all_to_all(pieces, NARROW, 0, 0), axis=0)  4.86 us
  transfers between devices with their start and end apart: 8, of which 6 were waited for; matrix products, arithmetic and copies ran while one was open for 7% of the time, Pallas kernels for 1%

profile of v3, /device:TPU:1, one launch (start us, length us, event | category | flops | bytes accessed | tf_op | source)
XLA Modules:
  0.0 162.0 jit_solution(11462662548517930225)
XLA Ops:
  7.2 0.9 slice.9
  8.1 1.4 pad_maximum_fusion
  9.6 0.5 broadcast.234
  10.1 0.8 reduce.1
  10.9 0.6 reshape.269
  11.5 10.1 %all-to-all-start = ((bf16[8,2,1024]{2,1,0:T(2,128)(2,1)}), bf16[8,2,1024]{2,1,0:T(2,128)(2,1)S(1)}, u32[]{:S(2)}, u32[]{:S(2)}) async-start(bf16[8,2,1024]{2,1,0:T(2,128)(2,1)} %reshape.269), calls=%async_computation | async-start | bytes 65536 | tf_op jit(solution)/shard_map/all_to_all | solution.py:33
  21.7 0.7 all-gather.2.cloned.1.call-update
  22.4 1.2 fusion.2
  23.6 0.7 convert_element_type.62
  24.3 2.1 %all-to-all-done = bf16[8,2,1024]{2,1,0:T(2,128)(2,1)S(1)} async-done(((bf16[8,2,1024]{2,1,0:T(2,128)(2,1)}), bf16[8,2,1024]{2,1,0:T(2,128)(2,1)S(1)}, u32[]{:S(2)}, u32[]{:S(2)}) %all-to-all-start) | async-done | bytes 32800 | tf_op jit(solution)/shard_map/all_to_all | solution.py:33
  26.5 0.1 fusion.22
  26.7 0.3 convolution_convert_fusion.3
  27.0 0.3 convolution_convert_fusion.1
  27.3 0.7 reshape.257
  28.0 4.0 %all-to-all-start.1 = ((bf16[8,4,2048]{2,1,0:T(4,128)(2,1)}), bf16[8,4,2048]{2,1,0:T(4,128)(2,1)S(1)}, u32[]{:S(2)}, u32[]{:S(2)}) async-start(bf16[8,4,2048]{2,1,0:T(4,128)(2,1)} %reshape.257), calls=%async_computation.1 | async-start | bytes 262144 | tf_op jit(solution)/shard_map/all_to_all | solution.py:157
  32.1 5.3 %all-to-all-done.1 = bf16[8,4,2048]{2,1,0:T(4,128)(2,1)S(1)} async-done(((bf16[8,4,2048]{2,1,0:T(4,128)(2,1)}), bf16[8,4,2048]{2,1,0:T(4,128)(2,1)S(1)}, u32[]{:S(2)}, u32[]{:S(2)}) %all-to-all-start.1) | async-done | bytes 131104 | tf_op jit(solution)/shard_map/all_to_all | solution.py:157
  37.4 0.5 fusion.39
  37.9 0.2 fusion.28
  38.1 0.3 convolution_convert_fusion
  38.4 0.7 reshape.259
  39.1 4.1 %all-to-all-start.2 = ((bf16[8,4,2048]{2,1,0:T(4,128)(2,1)}), bf16[8,4,2048]{2,1,0:T(4,128)(2,1)S(1)}, u32[]{:S(2)}, u32[]{:S(2)}) async-start(bf16[8,4,2048]{2,1,0:T(4,128)(2,1)} %reshape.259), calls=%async_computation.2 | async-start | bytes 262144 | tf_op jit(solution)/shard_map/all_to_all | solution.py:162
  43.2 1.5 copy.24
  44.7 3.8 %all-to-all-done.2 = bf16[8,4,2048]{2,1,0:T(4,128)(2,1)S(1)} async-done(((bf16[8,4,2048]{2,1,0:T(4,128)(2,1)}), bf16[8,4,2048]{2,1,0:T(4,128)(2,1)S(1)}, u32[]{:S(2)}, u32[]{:S(2)}) %all-to-all-start.2) | async-done | bytes 131104 | tf_op jit(solution)/shard_map/all_to_all | solution.py:162
  48.6 0.3 convolution_convert_fusion.2
  49.0 1.0 convolution_bitcast_fusion
  50.0 4.3 %all-to-all-start.3 = ((f32[8,8,256]{2,1,0:T(8,128)}), f32[8,8,256]{2,1,0:T(8,128)S(1)}, u32[]{:S(2)}, u32[]{:S(2)}) async-start(f32[8,8,256]{2,1,0:T(8,128)} %convolution_bitcast_fusion), calls=%async_computation.3 | async-start | bytes 131072 | tf_op jit(solution)/shard_map/all_to_all | solution.py:167
  54.3 4.9 %all-to-all-done.3 = f32[8,8,256]{2,1,0:T(8,128)S(1)} async-done(((f32[8,8,256]{2,1,0:T(8,128)}), f32[8,8,256]{2,1,0:T(8,128)S(1)}, u32[]{:S(2)}, u32[]{:S(2)}) %all-to-all-start.3) | async-done | bytes 65568 | tf_op jit(solution)/shard_map/all_to_all | solution.py:167
  59.2 12.4 %all_to_all.40 = bf16[8,8,256]{2,1,0:T(8,128)(2,1)S(1)} all-to-all(bf16[8,8,256]{2,1,0:T(8,128)(2,1)S(1)} %broadcast_in_dim.29), channel_id=1, replica_groups=mesh['yh'=4,'yl'=2,'z'=8,'x'=4,'core'=2] {'z'}, dimensions={0} | all-to-all | bytes 65536 | tf_op jit(solution)/shard_map/all_to_all | solution.py:33
  71.6 13.9 %all_to_all.41 = bf16[4,64,256]{2,1,0:T(8,128)(2,1)S(1)} all-to-all(bf16[4,64,256]{2,1,0:T(8,128)(2,1)S(1)} %broadcast_in_dim.61), channel_id=1, replica_groups=mesh['yh'=4,'yl'=2,'z'=8,'x'=4,'core'=2] {'yh'}, dimensions={0} | all-to-all | bytes 262144 | tf_op jit(solution)/shard_map/all_to_all | solution.py:33
  85.6 20.5 %all_to_all.42 = bf16[8,256,256]{2,1,0:T(8,128)(2,1)S(1)} all-to-all(bf16[8,256,256]{2,1,0:T(8,128)(2,1)S(1)} %broadcast_in_dim.63), channel_id=1, replica_groups=mesh['yh'=4,'yl'=2,'z'=8,'x'=4,'core'=2] {'yl','x'}, dimensions={0} | all-to-all | bytes 2097152 | tf_op jit(solution)/shard_map/all_to_all | solution.py:33
  106.2 8.3 %collective-permute-start = (bf16[2,4,256,256]{3,2,1,0:T(8,128)(2,1)S(1)}, bf16[2,4,256,256]{3,2,1,0:T(8,128)(2,1)S(1)}, u32[]{:S(2)}, u32[]{:S(2)}) collective-permute-start(bf16[2,4,256,256]{3,2,1,0:T(8,128)(2,1)S(1)} %bitcast.42), channel_id=1, source_target_pairs={{0,1},{1,0},{2,3},{3,2},{4,5},{5,4},{6,7},{7,6},{8,9},{9,8},{10,11... | collective-permute-start | bytes 3145736 | tf_op jit(solution)/shard_map/ppermute | solution.py:37
  114.5 1.0 copy-done.3
  116.1 0.9 copy.20
  117.1 1.4 fusion.13.places_ref
  118.5 1.0 copy-done.5
  119.5 1.2 copy-done.4
  120.7 1.2 copy-done.6
  122.0 1.1 norm_catalog.1.normed_ref
  123.1 1.7 %copy-done.1 = bf16[2048,640]{1,0:T(8,128)(2,1)S(1)} copy-done((bf16[2048,640]{1,0:T(8,128)(2,1)S(1)}, bf16[2048,640]{1,0:T(8,128)(2,1)}, u32[]{:S(2)}) %copy-start.1) | copy-done | bytes 2621464
  124.8 4.5 %user_attention.1 = (bf16[512,256]{1,0:T(8,128)(2,1)S(1)}, bf16[4,512,256]{2,1,0:T(8,128)(2,1)S(1)}) custom-call(s32[2]{0:T(128)S(1)} %pad_add_fusion.scalar_ref, bf16[512,2048]{1,0:T(8,128)(2,1)S(1)} %norm_catalog.1.normed_ref, bf16[2048,640]{1,0:T(8,128)(2,1)S(1)} %copy-done.1, s32[512,1]{1,0:T(8,128)S(1)} %fusion.13.places_ref), custom_call_target="tpu_custom_call" | custom-call | tf_op jit(solution)/shard_map/user_attention/pallas_call | solution.py:111
  129.3 1.9 %collective-permute-start.1 = (bf16[4,512,256]{2,1,0:T(8,128)(2,1)S(1)}, bf16[4,512,256]{2,1,0:T(8,128)(2,1)S(1)}, u32[]{:S(2)}, u32[]{:S(2)}) collective-permute-start(bf16[4,512,256]{2,1,0:T(8,128)(2,1)S(1)} %get-tuple-element.9), channel_id=1, source_target_pairs={{0,1},{1,0},{2,3},{3,2},{4,5},{5,4},{6,7},{7,6},{8,9},{9,8},{10,11... | collective-permute-start | bytes 3145736 | tf_op jit(solution)/shard_map/ppermute | solution.py:37
  131.3 2.6 %collective-permute-done.1.theirs_ref = bf16[4,512,256]{2,1,0:T(8,128)(2,1)S(1)} collective-permute-done((bf16[4,512,256]{2,1,0:T(8,128)(2,1)S(1)}, bf16[4,512,256]{2,1,0:T(8,128)(2,1)S(1)}, u32[]{:S(2)}, u32[]{:S(2)}) %collective-permute-start.1) | collective-permute-done | bytes 1048608 | tf_op jit(solution)/shard_map/ppermute | solution.py:37
  133.9 1.4 pair_sum.1
  135.4 3.5 %all-to-all-start.7 = ((bf16[4,512,256]{2,1,0:T(8,128)(2,1)}), bf16[4,512,256]{2,1,0:T(8,128)(2,1)S(1)}, u32[]{:S(2)}, u32[]{:S(2)}) async-start(bf16[4,512,256]{2,1,0:T(8,128)(2,1)} %pair_sum.1), calls=%async_computation.7 | async-start | bytes 2097152 | tf_op jit(solution)/shard_map/all_to_all | solution.py:214
  138.9 1.0 constant_dynamic-slice_fusion
  139.9 14.0 %all-to-all-done.7 = bf16[4,512,256]{2,1,0:T(8,128)(2,1)S(1)} async-done(((bf16[4,512,256]{2,1,0:T(8,128)(2,1)}), bf16[4,512,256]{2,1,0:T(8,128)(2,1)S(1)}, u32[]{:S(2)}, u32[]{:S(2)}) %all-to-all-start.7) | async-done | bytes 1048608 | tf_op jit(solution)/shard_map/all_to_all | solution.py:214
  153.9 0.1 convert_reduce_fusion
  154.1 1.1 fusion.1
  (42 shorter events, 0.7 us)
Async XLA Ops:
  7.2 19.5 %copy-start = (bf16[2048,256]{1,0:T(8,128)(2,1)S(1)}, bf16[2048,256]{1,0:T(8,128)(2,1)}, u32[]{:S(2)}) copy-start(bf16[2048,256]{1,0:T(8,128)(2,1)} %param.13) | copy-start | bytes 3145732
  7.2 30.2 %copy-start.8 = (bf16[128,2048]{1,0:T(8,128)(2,1)S(1)}, bf16[128,2048]{1,0:T(8,128)(2,1)}, u32[]{:S(2)}) copy-start(bf16[128,2048]{1,0:T(8,128)(2,1)} %param.11) | copy-start | bytes 1572868
  7.2 19.8 %copy-start.7 = (bf16[2048,1,128]{2,0,1:T(8,128)(2,1)S(1)}, bf16[2048,1,128]{2,0,1:T(8,128)(2,1)}, u32[]{:S(2)}) copy-start(bf16[2048,1,128]{2,0,1:T(8,128)(2,1)} %param.14) | copy-start | bytes 1572868
  11.5 14.9 %all-to-all-start = ((bf16[8,2,1024]{2,1,0:T(2,128)(2,1)}), bf16[8,2,1024]{2,1,0:T(2,128)(2,1)S(1)}, u32[]{:S(2)}, u32[]{:S(2)}) async-start(bf16[8,2,1024]{2,1,0:T(2,128)(2,1)} %reshape.269), calls=%async_computation | async-start | bytes 65536 | tf_op jit(solution)/shard_map/all_to_all | solution.py:33
  21.7 101.4 %all-gather.2.cloned.1.call-start = ((), (), s32[]{:S(2)}) async-start(), calls=%async_computation.8 | async-start | bytes 2662400 | tf_op jit(solution)/shard_map/all_gather | solution.py:147
  28.0 9.3 %all-to-all-start.1 = ((bf16[8,4,2048]{2,1,0:T(4,128)(2,1)}), bf16[8,4,2048]{2,1,0:T(4,128)(2,1)S(1)}, u32[]{:S(2)}, u32[]{:S(2)}) async-start(bf16[8,4,2048]{2,1,0:T(4,128)(2,1)} %reshape.257), calls=%async_computation.1 | async-start | bytes 262144 | tf_op jit(solution)/shard_map/all_to_all | solution.py:157
  39.1 9.4 %all-to-all-start.2 = ((bf16[8,4,2048]{2,1,0:T(4,128)(2,1)}), bf16[8,4,2048]{2,1,0:T(4,128)(2,1)S(1)}, u32[]{:S(2)}, u32[]{:S(2)}) async-start(bf16[8,4,2048]{2,1,0:T(4,128)(2,1)} %reshape.259), calls=%async_computation.2 | async-start | bytes 262144 | tf_op jit(solution)/shard_map/all_to_all | solution.py:162
  50.0 65.4 %copy-start.11 = (bf16[2048]{0:T(1024)(128)(2,1)S(1)}, bf16[2048]{0:T(1024)(128)(2,1)}, u32[]{:S(2)}) copy-start(bf16[2048]{0:T(1024)(128)(2,1)} %param.16) | copy-start | bytes 12292
  50.0 66.1 %copy-start.10 = (s32[1,512]{1,0:T(1,128)S(1)}, s32[1,512]{1,0:T(1,128)}, u32[]{:S(2)}) copy-start(s32[1,512]{1,0:T(1,128)} %param.20) | copy-start | bytes 6148
  50.0 9.1 %all-to-all-start.3 = ((f32[8,8,256]{2,1,0:T(8,128)}), f32[8,8,256]{2,1,0:T(8,128)S(1)}, u32[]{:S(2)}, u32[]{:S(2)}) async-start(f32[8,8,256]{2,1,0:T(8,128)} %convolution_bitcast_fusion), calls=%async_computation.3 | async-start | bytes 131072 | tf_op jit(solution)/shard_map/all_to_all | solution.py:167
  59.2 59.3 %copy-start.9 = (bf16[8,256]{1,0:T(8,128)(2,1)}, bf16[8,256]{1,0:T(8,128)(2,1)S(1)}, u32[]{:S(2)}) copy-start(bf16[8,256]{1,0:T(8,128)(2,1)S(1)} %fusion.29) | copy-start | bytes 12292
  106.2 12.4 %collective-permute-start = (bf16[2,4,256,256]{3,2,1,0:T(8,128)(2,1)S(1)}, bf16[2,4,256,256]{3,2,1,0:T(8,128)(2,1)S(1)}, u32[]{:S(2)}, u32[]{:S(2)}) collective-permute-start(bf16[2,4,256,256]{3,2,1,0:T(8,128)(2,1)S(1)} %bitcast.42), channel_id=1, source_target_pairs={{0,1},{1,0},{2,3},{3,2},{4,5},{5,4},{6,7},{7,6},{8,9},{9,8},{10,11... | collective-permute-start | bytes 3145736 | tf_op jit(solution)/shard_map/ppermute | solution.py:37
  114.5 1.0 copy-start.3
  118.5 1.0 copy-start.5
  119.5 1.2 copy-start.4
  120.7 1.2 copy-start.6
  123.1 1.7 %copy-start.1 = (bf16[2048,640]{1,0:T(8,128)(2,1)S(1)}, bf16[2048,640]{1,0:T(8,128)(2,1)}, u32[]{:S(2)}) copy-start(bf16[2048,640]{1,0:T(8,128)(2,1)} %all-gather.2.cloned.1.call-done.weights_ref) | copy-start | bytes 7864324
  124.8 9.1 %copy-start.2 = (bf16[2048,640]{1,0:T(8,128)(2,1)S(1)}, bf16[2048,640]{1,0:T(8,128)(2,1)}, u32[]{:S(2)}) copy-start(bf16[2048,640]{1,0:T(8,128)(2,1)} %all-gather.2.cloned.1.call-done.weights_ref) | copy-start | bytes 7864324
  129.3 4.6 %collective-permute-start.1 = (bf16[4,512,256]{2,1,0:T(8,128)(2,1)S(1)}, bf16[4,512,256]{2,1,0:T(8,128)(2,1)S(1)}, u32[]{:S(2)}, u32[]{:S(2)}) collective-permute-start(bf16[4,512,256]{2,1,0:T(8,128)(2,1)S(1)} %get-tuple-element.9), channel_id=1, source_target_pairs={{0,1},{1,0},{2,3},{3,2},{4,5},{5,4},{6,7},{7,6},{8,9},{9,8},{10,11... | collective-permute-start | bytes 3145736 | tf_op jit(solution)/shard_map/ppermute | solution.py:37
  135.4 18.6 %all-to-all-start.7 = ((bf16[4,512,256]{2,1,0:T(8,128)(2,1)}), bf16[4,512,256]{2,1,0:T(8,128)(2,1)S(1)}, u32[]{:S(2)}, u32[]{:S(2)}) async-start(bf16[4,512,256]{2,1,0:T(8,128)(2,1)} %pair_sum.1), calls=%async_computation.7 | async-start | bytes 2097152 | tf_op jit(solution)/shard_map/all_to_all | solution.py:214
Sparse Core Ops, SparseCore 0:
  25.5 83.1 all-gather.1

commit v4 on v3

v4 whole, which is shorter than its diff:
```python
import math

import jax
import jax.numpy as jnp
from jax import lax
from jax.experimental import pallas as pl
from jax.experimental.pallas import tpu as pltpu
from jax.sharding import Mesh
from jax.sharding import PartitionSpec as P

HEAD_DIM = 64
TXT = 128
epsilon = 1e-05
MIB = 1024 * 1024
WIDE = ("y", "z")
NARROW = ("x", "core")


def rms_scale(values, gain):
    wide = values.astype(jnp.float32)
    power = jnp.mean(wide * wide, axis=-1, keepdims=True)
    return (wide * lax.rsqrt(power + epsilon) * gain.astype(jnp.float32)).astype(jnp.bfloat16)


def dot_t(left, right):
    return lax.dot_general(
        left, right, (((1,), (1,)), ((), ())), preferred_element_type=jnp.float32
    )


def spread(values, axis):
    copies = jnp.broadcast_to(values[None], (lax.axis_size(axis),) + values.shape)
    return lax.all_to_all(copies, axis, 0, 0)


def swap_cores(values):
    return lax.ppermute(values, "core", [(0, 1), (1, 0)])


def along_x(values, step):
    n_x = lax.axis_size("x")
    pairs = [
        (2 * x + core, 2 * ((x + step * (1 - 2 * core)) % n_x) + core)
        for x in range(n_x)
        for core in range(2)
    ]
    return lax.ppermute(values, NARROW, pairs)


def load(source, target, sem):
    copy = pltpu.make_async_copy(source, target, sem)
    copy.start()
    return copy


def first_kernel(wq_ref, wkv_ref, wo_ref, parts_ref, sems):
    at, loads = 0, []
    for k, ref in enumerate((wq_ref, wkv_ref, wo_ref)):
        columns = ref.shape[1]
        loads.append(load(ref, parts_ref.at[:, pl.ds(at, columns)], sems.at[k]))
        at += columns
    for copy in loads:
        copy.wait()


def message_kernel(parts_ref, states_ref, message_ref, tail_ref, sem):
    del parts_ref
    tail = tail_ref.shape[0]
    load(states_ref.at[pl.ds(TXT - tail, tail)], tail_ref, sem).wait()
    row = tail_ref[...].astype(jnp.float32)[-1:]
    pieces, share = message_ref.shape[1:]
    tile = jnp.concatenate([row[:, j * share : (j + 1) * share] for j in range(pieces)], axis=0)
    for k in range(message_ref.shape[0]):
        message_ref[k] = tile


def user_kernel(
    scalar_ref,
    gain_ref,
    places_ref,
    mine_ref,
    other_ref,
    weights_ref,
    mixed_ref,
    terms_ref,
    wo_ref,
    normed_ref,
    picked_ref,
):
    length, core, place = scalar_ref[0], scalar_ref[1], scalar_ref[2]
    slots, q_width = mixed_ref.shape
    n_x, share = wo_ref.shape[:2]
    blocks = 2 * n_x
    kv_at = weights_ref.shape[1] - q_width
    catalog = normed_ref.shape[1]
    raw = [ref[x] for x in range(n_x) for ref in (mine_ref, other_ref)]
    power = jnp.zeros((catalog, share), jnp.float32)
    for k in range(blocks):
        block = raw[k].astype(jnp.float32)
        power = power + block * block
    factor = lax.rsqrt(jnp.sum(power, axis=1, keepdims=True) / (blocks * share) + epsilon)
    for k in range(blocks):
        where = k + core if k % 2 == 0 else k - core
        columns = pl.ds(pl.multiple_of(where * share, share), share)
        gain = gain_ref[:, columns].astype(jnp.float32)
        normed_ref[where] = (raw[k].astype(jnp.float32) * factor * gain).astype(jnp.bfloat16)
    every = lax.broadcasted_iota(jnp.int32, (slots, catalog), 1)
    picks = jnp.where(places_ref[...] == every, 1.0, 0.0).astype(jnp.bfloat16)
    projected = jnp.zeros((catalog, kv_at), jnp.float32)
    for k in range(blocks):
        projected += jnp.dot(
            normed_ref[k],
            weights_ref[k * share : (k + 1) * share, :kv_at],
            preferred_element_type=jnp.float32,
        )
    picked_ref[...] = jnp.dot(
        picks, projected.astype(jnp.bfloat16), preferred_element_type=jnp.float32
    ).astype(jnp.bfloat16)
    scale = 1.0 / math.sqrt(HEAD_DIM)
    chunk = min(slots, 256)
    for start in range(0, slots, chunk):
        upto = start + chunk
        keys = picked_ref[:upto, q_width : q_width + HEAD_DIM]
        values = picked_ref[:upto, q_width + HEAD_DIM : kv_at]
        row = start + lax.broadcasted_iota(jnp.int32, (chunk, upto), 0)
        column = lax.broadcasted_iota(jnp.int32, (chunk, upto), 1)
        allowed = (column <= row) & (column < length)
        for head in range(q_width // HEAD_DIM):
            lanes = slice(head * HEAD_DIM, (head + 1) * HEAD_DIM)
            scores = dot_t(picked_ref[start:upto, lanes], keys) * scale
            scores = jnp.where(allowed, scores, -1e30)
            top = jnp.max(scores, axis=1, keepdims=True)
            parts = jnp.exp(scores - top)
            total = jnp.sum(parts, axis=1, keepdims=True)
            mixed = jnp.dot(parts.astype(jnp.bfloat16), values, preferred_element_type=jnp.float32)
            mixed_ref[start:upto, lanes] = (mixed / total).astype(jnp.bfloat16)
    step = 1 - 2 * core
    for k, (theirs, mine) in enumerate(((2, 2), (step, -step), (-step, step), (0, 0))):
        rows = (2 * lax.rem(place + n_x + theirs, n_x) + 1 - core) * share
        rows = pl.ds(pl.multiple_of(rows, share), share)
        terms_ref[k] = dot_t(mixed_ref[...], weights_ref[rows, kv_at:]).astype(jnp.bfloat16)
        rows = (2 * lax.rem(place + n_x + mine, n_x) + core) * share
        rows = pl.ds(pl.multiple_of(rows, share), share)
        wo_ref[k] = weights_ref[rows, kv_at:]


def pair_kernel(mixed_ref, wo_ref, theirs_ref, *pair_refs):
    for x, ref in enumerate(pair_refs):
        terms = dot_t(mixed_ref[...], wo_ref[x])
        ref[...] = (terms + theirs_ref[x].astype(jnp.float32)).astype(jnp.bfloat16)


SMEM = pl.BlockSpec(memory_space=pltpu.SMEM)
VMEM = pl.BlockSpec(memory_space=pltpu.VMEM)
ANY = pl.BlockSpec(memory_space=pl.ANY)


def call(kernel, name, limit, outs, in_specs, ins, scratch=()):
    return pl.pallas_call(
        kernel,
        name=name,
        out_shape=outs,
        in_specs=in_specs,
        out_specs=jax.tree.map(lambda _: VMEM, outs),
        scratch_shapes=scratch,
        compiler_params=pltpu.CompilerParams(vmem_limit_bytes=limit * MIB),
    )(*ins)


def local(
    item_states,
    item_gain,
    wq_item,
    wkv_item,
    wo_item,
    user_gain,
    wq_user,
    wkv_user,
    wo_user,
    history_items,
    history_lengths,
):
    width = item_states.shape[1]
    n_x = lax.axis_size("x")
    n_narrow = 2 * n_x
    share = width // n_narrow
    core = lax.axis_index("core")
    me = lax.axis_index("x") * 2 + core
    scale = 1.0 / math.sqrt(HEAD_DIM)

    columns = wq_user.shape[1] + 2 * HEAD_DIM + wo_user.shape[0]
    parts = call(
        first_kernel,
        "user_weights",
        60,
        jax.ShapeDtypeStruct((wq_user.shape[0], columns), jnp.bfloat16),
        [ANY] * 3,
        (wq_user, wkv_user.reshape(wkv_user.shape[0], -1), wo_user.T),
        [pltpu.SemaphoreType.DMA((3,))],
    )
    weights_all = lax.all_gather(parts, WIDE, axis=0, tiled=True)

    messages = call(
        message_kernel,
        "last_rows",
        60,
        jax.ShapeDtypeStruct((n_narrow, n_narrow, share), jnp.float32),
        [ANY, ANY],
        (parts, item_states),
        [pltpu.VMEM((16, width), jnp.bfloat16), pltpu.SemaphoreType.DMA],
    )
    last_raw = lax.all_to_all(messages, NARROW, 0, 0)
    last_share = lax.dynamic_index_in_dim(last_raw, me, 1, keepdims=False)
    last_raw = last_raw.reshape(n_narrow, width)
    last_normed = rms_scale(last_raw, item_gain)
    queries = jnp.dot(last_normed, wq_item, preferred_element_type=jnp.float32)
    queries = queries.astype(jnp.bfloat16)
    per = queries.shape[1] // HEAD_DIM
    wk = wkv_item[:, 0, :HEAD_DIM]
    wv = wkv_item[:, 0, HEAD_DIM:]
    probes = dot_t(queries.reshape(-1, HEAD_DIM), wk).astype(jnp.bfloat16)
    probes = lax.all_to_all(probes.reshape(n_narrow, per, width), NARROW, 0, 0)
    length = history_lengths[0]
    normed, places, scalars, gain_row = lax.optimization_barrier(
        (
            rms_scale(item_states, item_gain),
            history_items[0][:, None],
            jnp.stack([length, core, lax.axis_index("x")]).astype(jnp.int32),
            user_gain[None],
        )
    )
    scores = dot_t(probes.reshape(-1, width), normed) * scale
    attn = jax.nn.softmax(scores, axis=-1).astype(jnp.bfloat16)
    pooled = jnp.dot(attn, normed, preferred_element_type=jnp.float32).astype(jnp.bfloat16)
    pooled = lax.all_to_all(pooled.reshape(n_narrow, per, width), NARROW, 0, 0)
    mixed = jnp.dot(pooled.reshape(-1, width), wv, preferred_element_type=jnp.float32)
    mixed = mixed.astype(jnp.bfloat16).reshape(n_narrow, -1)
    partial_sum = jnp.dot(mixed, wo_item, preferred_element_type=jnp.float32)
    pieces = partial_sum.reshape(n_narrow, n_narrow, share).transpose(1, 0, 2)
    total = jnp.sum(lax.all_to_all(pieces, NARROW, 0, 0), axis=0)
    item_part = (last_share + total).astype(jnp.bfloat16)

    block = spread(item_part, WIDE).reshape(-1, share)
    mine = spread(block, "x")
    other = swap_cores(mine)
    catalog = block.shape[0]
    slots = history_items.shape[1]
    heads_width = wq_user.shape[1]
    kv_at = heads_width + 2 * HEAD_DIM
    user_mixed, theirs, wo_mine = call(
        user_kernel,
        "user_attention",
        20,
        (
            jax.ShapeDtypeStruct((slots, heads_width), jnp.bfloat16),
            jax.ShapeDtypeStruct((n_x, slots, share), jnp.bfloat16),
            jax.ShapeDtypeStruct((n_x, share, heads_width), jnp.bfloat16),
        ),
        [SMEM] + [VMEM] * 5,
        (
            scalars,
            gain_row,
            places,
            mine,
            other,
            weights_all,
        ),
        [
            pltpu.VMEM((n_narrow, catalog, share), jnp.bfloat16),
            pltpu.VMEM((slots, kv_at), jnp.bfloat16),
        ],
    )

    theirs = swap_cores(theirs)
    first, direct, second, own = call(
        pair_kernel,
        "pair_sum",
        20,
        [jax.ShapeDtypeStruct((slots, share), jnp.bfloat16)] * n_x,
        [VMEM] * 3,
        (user_mixed, wo_mine, theirs),
    )
    relay = along_x(first, 1)
    direct = along_x(direct, -1)
    relay = (relay.astype(jnp.float32) + second.astype(jnp.float32)).astype(jnp.bfloat16)
    relay = along_x(relay, 1)
    picks = (places == jnp.arange(catalog, dtype=jnp.int32)[None, :]).astype(jnp.bfloat16)
    residual = jnp.dot(picks, block, preferred_element_type=jnp.float32)
    summed = own.astype(jnp.float32) + direct.astype(jnp.float32) + relay.astype(jnp.float32)
    live = (jnp.arange(slots, dtype=jnp.int32) < length)[:, None]
    user_states = jnp.where(live, residual + summed, 0.0).astype(jnp.bfloat16)
    return (item_part, user_states)


def solution(mesh):
    n_wide, n_narrow = mesh.shape["wide"], mesh.shape["narrow"]
    side = math.isqrt(n_wide)
    fine = Mesh(
        mesh.devices.reshape(side, n_wide // side, n_narrow // 2, 2), WIDE + NARROW
    )
    return jax.shard_map(
        local,
        mesh=fine,
        in_specs=(
            P(WIDE + NARROW, None),
            P(),
            P(None, NARROW),
            P(None, NARROW, None),
            P(NARROW, None),
            P(),
            P(WIDE, NARROW),
            P(WIDE, NARROW, None),
            P(NARROW, WIDE),
            P(WIDE, None),
            P(WIDE),
        ),
        out_specs=(P(WIDE, NARROW), P(WIDE, NARROW)),
        check_vma=False,
    )
```

time: 163 us -> 145 us (0.89)
  the two profiles are of different devices: /device:TPU:1 before, /device:TPU:16 now
where the time goes in v4:
time: 145 us; the launch traced here: 144 us
  blocking collectives  46.8 us (32%)
  waiting for transfers between devices  34.2 us (24%)
  starting transfers between devices  27.4 us (19%)
  between operations  15 us (10%)
  Pallas kernels  9.01 us (6%)
  local copies, waits for them, and re-layouts  5.25 us (4%)
  other arithmetic  3.47 us (2%)
  matrix products  2.92 us (2%)
    all_to_all x2, blocking collectives, spread(): return lax.all_to_all(copies, axis, 0, 0)  46.8 us
    ppermute x3, waiting for transfers between devices, along_x(): return lax.ppermute(values, NARROW, pairs)  10.3 us
    pallas_call x4, Pallas kernels, call(): pl.pallas_call(kernel, name=name, out_shape=outs, in_specs=in_specs, out_...  9.01 us
    ppermute x3, starting transfers between devices, along_x(): return lax.ppermute(values, NARROW, pairs)  8.97 us
    all_to_all x1, waiting for transfers between devices, local(): total = jnp.sum(lax.all_to_all(pieces, NARROW, 0, 0), axis=0)  5.52 us
    all_to_all x1, waiting for transfers between devices, local(): probes = lax.all_to_all(probes.reshape(n_narrow, per, width), NARROW, 0, 0)  5.09 us
    ppermute x2, waiting for transfers between devices, swap_cores(): return lax.ppermute(values, 'core', [(0, 1), (1, 0)])  4.97 us
    all_to_all x1, waiting for transfers between devices, local(): pooled = lax.all_to_all(pooled.reshape(n_narrow, per, width), NARROW, 0, 0)  4.56 us
  transfers between devices with their start and end apart: 10, of which 8 were waited for; matrix products, arithmetic and copies ran while one was open for 6% of the time, Pallas kernels for 1%

profile of v4, /device:TPU:16, one launch (start us, length us, event | category | flops | bytes accessed | tf_op | source)
XLA Modules:
  0.0 144.0 jit_solution(8563244409429565516)
XLA Ops:
  7.2 0.0 all-gather.2.cloned.1.call-start
  7.3 1.5 %user_weights.1.parts_ref = bf16[32,640]{1,0:T(8,128)(2,1)} custom-call(bf16[32,256]{1,0:T(8,128)(2,1)} %wq_ref.1, bf16[32,128]{1,0:T(8,128)(2,1)} %bitcast.43, bf16[32,256]{1,0:T(8,128)(2,1)} %bitcast.40), custom_call_target="tpu_custom_call" | custom-call | tf_op jit(solution)/shard_map/user_weights/pallas_call | solution.py:159
  8.8 0.0 all-gather.2.cloned.1.call-update
  8.8 1.5 %last_rows.1 = f32[8,8,256]{2,1,0:T(8,128)} custom-call(bf16[32,640]{1,0:T(8,128)(2,1)} %user_weights.1.parts_ref, bf16[128,2048]{1,0:T(8,128)(2,1)} %states_ref.1), custom_call_target="tpu_custom_call" | custom-call | tf_op jit(solution)/shard_map/last_rows/pallas_call | solution.py:159
  10.3 4.3 %all-to-all-start = ((f32[8,8,256]{2,1,0:T(8,128)}), f32[8,8,256]{2,1,0:T(8,128)S(1)}, u32[]{:S(2)}, u32[]{:S(2)}) async-start(f32[8,8,256]{2,1,0:T(8,128)} %last_rows.1), calls=%async_computation | async-start | bytes 131072 | tf_op jit(solution)/shard_map/all_to_all | solution.py:212
  14.6 1.2 fusion
  15.9 0.7 convert_element_type.57
  16.6 3.7 %all-to-all-done = f32[8,8,256]{2,1,0:T(8,128)S(1)} async-done(((f32[8,8,256]{2,1,0:T(8,128)}), f32[8,8,256]{2,1,0:T(8,128)S(1)}, u32[]{:S(2)}, u32[]{:S(2)}) %all-to-all-start) | async-done | bytes 65568 | tf_op jit(solution)/shard_map/all_to_all | solution.py:212
  20.3 0.1 multiply_reduce_fusion
  20.4 0.3 convolution_convert_fusion.3
  20.7 0.1 reshape.67
  20.8 0.3 convolution_convert_fusion.1
  21.1 0.7 reshape.68
  21.8 3.4 %all-to-all-start.1 = ((bf16[8,4,2048]{2,1,0:T(4,128)(2,1)}), bf16[8,4,2048]{2,1,0:T(4,128)(2,1)S(1)}, u32[]{:S(2)}, u32[]{:S(2)}) async-start(bf16[8,4,2048]{2,1,0:T(4,128)(2,1)} %reshape.68), calls=%async_computation.1 | async-start | bytes 262144 | tf_op jit(solution)/shard_map/all_to_all | solution.py:222
  25.2 0.2 fusion.2
  26.1 0.1 pad_add_fusion.scalar_ref
  26.2 5.1 %all-to-all-done.1 = bf16[8,4,2048]{2,1,0:T(4,128)(2,1)S(1)} async-done(((bf16[8,4,2048]{2,1,0:T(4,128)(2,1)}), bf16[8,4,2048]{2,1,0:T(4,128)(2,1)S(1)}, u32[]{:S(2)}, u32[]{:S(2)}) %all-to-all-start.1) | async-done | bytes 131104 | tf_op jit(solution)/shard_map/all_to_all | solution.py:222
  31.3 0.4 fusion.16
  31.7 0.2 fusion.11
  31.9 0.3 convolution_convert_fusion
  32.2 0.7 reshape.70
  32.9 3.4 %all-to-all-start.2 = ((bf16[8,4,2048]{2,1,0:T(4,128)(2,1)}), bf16[8,4,2048]{2,1,0:T(4,128)(2,1)S(1)}, u32[]{:S(2)}, u32[]{:S(2)}) async-start(bf16[8,4,2048]{2,1,0:T(4,128)(2,1)} %reshape.70), calls=%async_computation.2 | async-start | bytes 262144 | tf_op jit(solution)/shard_map/all_to_all | solution.py:235
  36.3 1.5 %copy.16 = bf16[2048,256]{1,0:T(8,128)(2,1)S(1)} copy(bf16[2048,256]{0,1:T(8,128)(2,1)} %bitcast.37) | data formatting | bytes 2097152 | tf_op jit(solution)/shard_map/dot_general | solution.py:238
  37.8 4.6 %all-to-all-done.2 = bf16[8,4,2048]{2,1,0:T(4,128)(2,1)S(1)} async-done(((bf16[8,4,2048]{2,1,0:T(4,128)(2,1)}), bf16[8,4,2048]{2,1,0:T(4,128)(2,1)S(1)}, u32[]{:S(2)}, u32[]{:S(2)}) %all-to-all-start.2) | async-done | bytes 131104 | tf_op jit(solution)/shard_map/all_to_all | solution.py:235
  42.4 0.3 convolution_convert_fusion.2
  42.7 0.1 reshape.74
  42.8 1.0 convolution_bitcast_fusion
  43.8 3.4 %all-to-all-start.3 = ((f32[8,8,256]{2,1,0:T(8,128)}), f32[8,8,256]{2,1,0:T(8,128)S(1)}, u32[]{:S(2)}, u32[]{:S(2)}) async-start(f32[8,8,256]{2,1,0:T(8,128)} %convolution_bitcast_fusion), calls=%async_computation.3 | async-start | bytes 131072 | tf_op jit(solution)/shard_map/all_to_all | solution.py:240
  47.2 5.5 %all-to-all-done.3 = f32[8,8,256]{2,1,0:T(8,128)S(1)} async-done(((f32[8,8,256]{2,1,0:T(8,128)}), f32[8,8,256]{2,1,0:T(8,128)S(1)}, u32[]{:S(2)}, u32[]{:S(2)}) %all-to-all-start.3) | async-done | bytes 65568 | tf_op jit(solution)/shard_map/all_to_all | solution.py:240
  52.8 31.6 %all_to_all.30 = bf16[64,8,256]{2,1,0:T(8,128)(2,1)S(1)} all-to-all(bf16[64,8,256]{2,1,0:T(8,128)(2,1)S(1)} %broadcast_in_dim.16), channel_id=1, replica_groups=mesh['y'=8,'z'=8,'x'=4,'core'=2] {'y','z'}, dimensions={0} | all-to-all | bytes 524288 | tf_op jit(solution)/shard_map/all_to_all | solution.py:33
  84.4 0.1 broadcast_in_dim.17
  84.4 15.2 %all_to_all.31.mine_ref = bf16[4,512,256]{2,1,0:T(8,128)(2,1)S(1)} all-to-all(bf16[4,512,256]{2,1,0:T(8,128)(2,1)S(1)} %broadcast_in_dim.17), channel_id=1, replica_groups=mesh['y'=8,'z'=8,'x'=4,'core'=2] {'x'}, dimensions={0} | all-to-all | bytes 2097152 | tf_op jit(solution)/shard_map/all_to_all | solution.py:33
  99.6 1.9 %collective-permute-start = (bf16[4,512,256]{2,1,0:T(8,128)(2,1)S(1)}, bf16[4,512,256]{2,1,0:T(8,128)(2,1)S(1)}, u32[]{:S(2)}, u32[]{:S(2)}) collective-permute-start(bf16[4,512,256]{2,1,0:T(8,128)(2,1)S(1)} %all_to_all.31.mine_ref), channel_id=1, source_target_pairs={{0,1},{1,0},{2,3},{3,2},{4,5},{5,4},{6,7},{7,6},{8,9},{9,8},{10,11... | collective-permute-start | bytes 3145736 | tf_op jit(solution)/shard_map/ppermute | solution.py:37
  101.6 0.1 copy.15.places_ref
  101.7 2.5 %collective-permute-done.other_ref = bf16[4,512,256]{2,1,0:T(8,128)(2,1)S(1)} collective-permute-done((bf16[4,512,256]{2,1,0:T(8,128)(2,1)S(1)}, bf16[4,512,256]{2,1,0:T(8,128)(2,1)S(1)}, u32[]{:S(2)}, u32[]{:S(2)}) %collective-permute-start) | collective-permute-done | bytes 1048608 | tf_op jit(solution)/shard_map/ppermute | solution.py:37
  104.2 1.7 %copy-done.1 = bf16[2048,640]{1,0:T(8,128)(2,1)S(1)} copy-done((bf16[2048,640]{1,0:T(8,128)(2,1)S(1)}, bf16[2048,640]{1,0:T(8,128)(2,1)}, u32[]{:S(2)}) %copy-start.1) | copy-done | bytes 2621464
  105.9 5.5 %user_attention.1 = (bf16[512,256]{1,0:T(8,128)(2,1)S(1)}, bf16[4,512,256]{2,1,0:T(8,128)(2,1)S(1)}, bf16[4,256,256]{2,1,0:T(8,128)(2,1)S(1)}) custom-call(s32[3]{0:T(128)S(1)} %pad_add_fusion.scalar_ref, bf16[1,2048]{1,0:T(2,128)(2,1)S(1)} %broadcast_in_dim.14.gain_ref, s32[512,1]{1,0:T(8,128)S(1)} %copy.15.places_ref, ...), custom_call_target="tpu_custom_call" | custom-call | tf_op jit(solution)/shard_map/user_attention/pallas_call | solution.py:159
  111.5 2.0 %collective-permute-start.1 = (bf16[4,512,256]{2,1,0:T(8,128)(2,1)S(1)}, bf16[4,512,256]{2,1,0:T(8,128)(2,1)S(1)}, u32[]{:S(2)}, u32[]{:S(2)}) collective-permute-start(bf16[4,512,256]{2,1,0:T(8,128)(2,1)S(1)} %get-tuple-element.19), channel_id=1, source_target_pairs={{0,1},{1,0},{2,3},{3,2},{4,5},{5,4},{6,7},{7,6},{8,9},{9,8},{10,11... | collective-permute-start | bytes 3145736 | tf_op jit(solution)/shard_map/ppermute | solution.py:37
  113.5 2.5 %collective-permute-done.1.theirs_ref = bf16[4,512,256]{2,1,0:T(8,128)(2,1)S(1)} collective-permute-done((bf16[4,512,256]{2,1,0:T(8,128)(2,1)S(1)}, bf16[4,512,256]{2,1,0:T(8,128)(2,1)S(1)}, u32[]{:S(2)}, u32[]{:S(2)}) %collective-permute-start.1) | collective-permute-done | bytes 1048608 | tf_op jit(solution)/shard_map/ppermute | solution.py:37
  116.0 0.5 pair_sum.1
  116.5 2.5 %collective-permute-start.3 = (bf16[512,256]{1,0:T(8,128)(2,1)S(1)}, bf16[512,256]{1,0:T(8,128)(2,1)S(1)}, u32[]{:S(2)}, u32[]{:S(2)}) collective-permute-start(bf16[512,256]{1,0:T(8,128)(2,1)S(1)} %get-tuple-element.22), channel_id=1, source_target_pairs={{0,2},{1,7},{2,4},{3,1},{4,6},{5,3},{6,0},{7,5},{8,10},{9,15},{10,... | collective-permute-start | bytes 786440 | tf_op jit(solution)/shard_map/ppermute | solution.py:47
  119.0 4.6 %collective-permute-start.2 = (bf16[512,256]{1,0:T(8,128)(2,1)S(1)}, bf16[512,256]{1,0:T(8,128)(2,1)S(1)}, u32[]{:S(2)}, u32[]{:S(2)}) collective-permute-start(bf16[512,256]{1,0:T(8,128)(2,1)S(1)} %get-tuple-element.21), channel_id=1, source_target_pairs={{0,6},{1,3},{2,0},{3,5},{4,2},{5,7},{6,4},{7,1},{8,14},{9,11},{10,... | collective-permute-start | bytes 786440 | tf_op jit(solution)/shard_map/ppermute | solution.py:47
  123.6 3.2 %collective-permute-done.3 = bf16[512,256]{1,0:T(8,128)(2,1)S(1)} collective-permute-done((bf16[512,256]{1,0:T(8,128)(2,1)S(1)}, bf16[512,256]{1,0:T(8,128)(2,1)S(1)}, u32[]{:S(2)}, u32[]{:S(2)}) %collective-permute-start.3) | collective-permute-done | bytes 262176 | tf_op jit(solution)/shard_map/ppermute | solution.py:47
  126.7 0.1 add_convert_fusion
  126.8 1.9 %collective-permute-start.4 = (bf16[512,256]{1,0:T(8,128)(2,1)S(1)}, bf16[512,256]{1,0:T(8,128)(2,1)S(1)}, u32[]{:S(2)}, u32[]{:S(2)}) collective-permute-start(bf16[512,256]{1,0:T(8,128)(2,1)S(1)} %add_convert_fusion), channel_id=1, source_target_pairs={{0,2},{1,7},{2,4},{3,1},{4,6},{5,3},{6,0},{7,5},{8,10},{9,15},{10,... | collective-permute-start | bytes 786440 | tf_op jit(solution)/shard_map/ppermute | solution.py:47
  128.7 0.4 fusion.3
  129.1 7.2 %collective-permute-done.4 = bf16[512,256]{1,0:T(8,128)(2,1)S(1)} collective-permute-done((bf16[512,256]{1,0:T(8,128)(2,1)S(1)}, bf16[512,256]{1,0:T(8,128)(2,1)S(1)}, u32[]{:S(2)}, u32[]{:S(2)}) %collective-permute-start.4) | collective-permute-done | bytes 262176 | tf_op jit(solution)/shard_map/ppermute | solution.py:47
  136.3 0.8 select_convert_fusion
  (30 shorter events, 0.2 us)
Async XLA Ops:
  7.2 13.3 %copy-start = (bf16[2048,256]{1,0:T(8,128)(2,1)S(1)}, bf16[2048,256]{1,0:T(8,128)(2,1)}, u32[]{:S(2)}) copy-start(bf16[2048,256]{1,0:T(8,128)(2,1)} %param.13) | copy-start | bytes 3145732
  7.2 18.0 %copy-start.2 = (bf16[128,2048]{1,0:T(8,128)(2,1)S(1)}, bf16[128,2048]{1,0:T(8,128)(2,1)}, u32[]{:S(2)}) copy-start(bf16[128,2048]{1,0:T(8,128)(2,1)} %states_ref.1) | copy-start | bytes 1572868
  7.2 13.6 %copy-start.5 = (bf16[2048,1,128]{2,0,1:T(8,128)(2,1)S(1)}, bf16[2048,1,128]{2,0,1:T(8,128)(2,1)}, u32[]{:S(2)}) copy-start(bf16[2048,1,128]{2,0,1:T(8,128)(2,1)} %param.14) | copy-start | bytes 1572868
  7.2 18.9 %copy-start.8 = (bf16[2048]{0:T(1024)(128)(2,1)S(1)}, bf16[2048]{0:T(1024)(128)(2,1)}, u32[]{:S(2)}) copy-start(bf16[2048]{0:T(1024)(128)(2,1)} %param.16) | copy-start | bytes 12292
  7.2 97.0 %all-gather.2.cloned.1.call-start = ((), (), s32[]{:S(2)}) async-start(), calls=%async_computation.6 | async-start | bytes 2662400 | tf_op jit(solution)/shard_map/all_gather | solution.py:201
  10.3 9.9 %all-to-all-start = ((f32[8,8,256]{2,1,0:T(8,128)}), f32[8,8,256]{2,1,0:T(8,128)S(1)}, u32[]{:S(2)}, u32[]{:S(2)}) async-start(f32[8,8,256]{2,1,0:T(8,128)} %last_rows.1), calls=%async_computation | async-start | bytes 131072 | tf_op jit(solution)/shard_map/all_to_all | solution.py:212
  21.8 9.4 %all-to-all-start.1 = ((bf16[8,4,2048]{2,1,0:T(4,128)(2,1)}), bf16[8,4,2048]{2,1,0:T(4,128)(2,1)S(1)}, u32[]{:S(2)}, u32[]{:S(2)}) async-start(bf16[8,4,2048]{2,1,0:T(4,128)(2,1)} %reshape.68), calls=%async_computation.1 | async-start | bytes 262144 | tf_op jit(solution)/shard_map/all_to_all | solution.py:222
  32.9 9.4 %all-to-all-start.2 = ((bf16[8,4,2048]{2,1,0:T(4,128)(2,1)}), bf16[8,4,2048]{2,1,0:T(4,128)(2,1)S(1)}, u32[]{:S(2)}, u32[]{:S(2)}) async-start(bf16[8,4,2048]{2,1,0:T(4,128)(2,1)} %reshape.70), calls=%async_computation.2 | async-start | bytes 262144 | tf_op jit(solution)/shard_map/all_to_all | solution.py:235
  42.8 58.8 %copy-start.7 = (s32[1,512]{1,0:T(1,128)S(1)}, s32[1,512]{1,0:T(1,128)}, u32[]{:S(2)}) copy-start(s32[1,512]{1,0:T(1,128)} %param.20) | copy-start | bytes 6148
  43.8 8.9 %all-to-all-start.3 = ((f32[8,8,256]{2,1,0:T(8,128)}), f32[8,8,256]{2,1,0:T(8,128)S(1)}, u32[]{:S(2)}, u32[]{:S(2)}) async-start(f32[8,8,256]{2,1,0:T(8,128)} %convolution_bitcast_fusion), calls=%async_computation.3 | async-start | bytes 131072 | tf_op jit(solution)/shard_map/all_to_all | solution.py:240
  52.7 58.7 %copy-start.6 = (bf16[8,256]{1,0:T(8,128)(2,1)}, bf16[8,256]{1,0:T(8,128)(2,1)S(1)}, u32[]{:S(2)}) copy-start(bf16[8,256]{1,0:T(8,128)(2,1)S(1)} %fusion.12) | copy-start | bytes 12292
  84.4 15.3 %copy-start.3 = (bf16[64,8,256]{2,1,0:T(8,128)(2,1)}, bf16[64,8,256]{2,1,0:T(8,128)(2,1)S(1)}, u32[]{:S(2)}) copy-start(bf16[64,8,256]{2,1,0:T(8,128)(2,1)S(1)} %all_to_all.30) | copy-start | bytes 786436
  99.6 4.5 %collective-permute-start = (bf16[4,512,256]{2,1,0:T(8,128)(2,1)S(1)}, bf16[4,512,256]{2,1,0:T(8,128)(2,1)S(1)}, u32[]{:S(2)}, u32[]{:S(2)}) collective-permute-start(bf16[4,512,256]{2,1,0:T(8,128)(2,1)S(1)} %all_to_all.31.mine_ref), channel_id=1, source_target_pairs={{0,1},{1,0},{2,3},{3,2},{4,5},{5,4},{6,7},{7,6},{8,9},{9,8},{10,11... | collective-permute-start | bytes 3145736 | tf_op jit(solution)/shard_map/ppermute | solution.py:37
  104.2 1.7 %copy-start.1 = (bf16[2048,640]{1,0:T(8,128)(2,1)S(1)}, bf16[2048,640]{1,0:T(8,128)(2,1)}, u32[]{:S(2)}) copy-start(bf16[2048,640]{1,0:T(8,128)(2,1)} %all-gather.2.cloned.1.call-done.weights_ref) | copy-start | bytes 7864324
  105.9 22.8 %copy-start.4 = (bf16[64,8,256]{2,1,0:T(8,128)(2,1)S(1)}, bf16[64,8,256]{2,1,0:T(8,128)(2,1)}, u32[]{:S(2)}) copy-start(bf16[64,8,256]{2,1,0:T(8,128)(2,1)} %copy-done.3) | copy-start | bytes 786436
  111.5 4.6 %collective-permute-start.1 = (bf16[4,512,256]{2,1,0:T(8,128)(2,1)S(1)}, bf16[4,512,256]{2,1,0:T(8,128)(2,1)S(1)}, u32[]{:S(2)}, u32[]{:S(2)}) collective-permute-start(bf16[4,512,256]{2,1,0:T(8,128)(2,1)S(1)} %get-tuple-element.19), channel_id=1, source_target_pairs={{0,1},{1,0},{2,3},{3,2},{4,5},{5,4},{6,7},{7,6},{8,9},{9,8},{10,11... | collective-permute-start | bytes 3145736 | tf_op jit(solution)/shard_map/ppermute | solution.py:37
  116.5 10.2 %collective-permute-start.3 = (bf16[512,256]{1,0:T(8,128)(2,1)S(1)}, bf16[512,256]{1,0:T(8,128)(2,1)S(1)}, u32[]{:S(2)}, u32[]{:S(2)}) collective-permute-start(bf16[512,256]{1,0:T(8,128)(2,1)S(1)} %get-tuple-element.22), channel_id=1, source_target_pairs={{0,2},{1,7},{2,4},{3,1},{4,6},{5,3},{6,0},{7,5},{8,10},{9,15},{10,... | collective-permute-start | bytes 786440 | tf_op jit(solution)/shard_map/ppermute | solution.py:47
  119.0 10.1 %collective-permute-start.2 = (bf16[512,256]{1,0:T(8,128)(2,1)S(1)}, bf16[512,256]{1,0:T(8,128)(2,1)S(1)}, u32[]{:S(2)}, u32[]{:S(2)}) collective-permute-start(bf16[512,256]{1,0:T(8,128)(2,1)S(1)} %get-tuple-element.21), channel_id=1, source_target_pairs={{0,6},{1,3},{2,0},{3,5},{4,2},{5,7},{6,4},{7,1},{8,14},{9,11},{10,... | collective-permute-start | bytes 786440 | tf_op jit(solution)/shard_map/ppermute | solution.py:47
  126.8 9.5 %collective-permute-start.4 = (bf16[512,256]{1,0:T(8,128)(2,1)S(1)}, bf16[512,256]{1,0:T(8,128)(2,1)S(1)}, u32[]{:S(2)}, u32[]{:S(2)}) collective-permute-start(bf16[512,256]{1,0:T(8,128)(2,1)S(1)} %add_convert_fusion), channel_id=1, source_target_pairs={{0,2},{1,7},{2,4},{3,1},{4,6},{5,3},{6,0},{7,5},{8,10},{9,15},{10,... | collective-permute-start | bytes 786440 | tf_op jit(solution)/shard_map/ppermute | solution.py:47
Sparse Core Ops, SparseCore 0:
  11.1 92.1 all-gather.1

commit v5 on v4

v5 whole, which is shorter than its diff:
```python
import math

import jax
import jax.numpy as jnp
from jax import lax
from jax.experimental import pallas as pl
from jax.experimental.pallas import tpu as pltpu
from jax.sharding import Mesh
from jax.sharding import PartitionSpec as P

HEAD_DIM = 64
TXT = 128
epsilon = 1e-05
MIB = 1024 * 1024
WIDE = ("y", "z")
NARROW = ("x", "core")


def rms_scale(values, gain):
    wide = values.astype(jnp.float32)
    power = jnp.mean(wide * wide, axis=-1, keepdims=True)
    return (wide * lax.rsqrt(power + epsilon) * gain.astype(jnp.float32)).astype(jnp.bfloat16)


def dot_t(left, right):
    return lax.dot_general(
        left, right, (((1,), (1,)), ((), ())), preferred_element_type=jnp.float32
    )


def spread(values, axis):
    copies = jnp.broadcast_to(values[None], (lax.axis_size(axis),) + values.shape)
    return lax.all_to_all(copies, axis, 0, 0)


def swap_cores(values):
    return lax.ppermute(values, "core", [(0, 1), (1, 0)])


def along_x(values, step):
    n_x = lax.axis_size("x")
    pairs = [
        (2 * x + core, 2 * ((x + step * (1 - 2 * core)) % n_x) + core)
        for x in range(n_x)
        for core in range(2)
    ]
    return lax.ppermute(values, NARROW, pairs)


def load(source, target, sem):
    copy = pltpu.make_async_copy(source, target, sem)
    copy.start()
    return copy


def first_kernel(wq_ref, wkv_ref, wo_ref, copies_ref, sems):
    at, loads = 0, []
    for k, ref in enumerate((wq_ref, wkv_ref, wo_ref)):
        columns = ref.shape[1]
        loads.append(load(ref, copies_ref.at[0, :, pl.ds(at, columns)], sems.at[k]))
        at += columns
    for copy in loads:
        copy.wait()
    for k in range(1, copies_ref.shape[0]):
        copies_ref[k] = copies_ref[0]


def message_kernel(states_ref, message_ref, tail_ref, sem):
    tail = tail_ref.shape[0]
    load(states_ref.at[pl.ds(TXT - tail, tail)], tail_ref, sem).wait()
    row = tail_ref[...].astype(jnp.float32)[-1:]
    pieces, share = message_ref.shape[1:]
    tile = jnp.concatenate([row[:, j * share : (j + 1) * share] for j in range(pieces)], axis=0)
    for k in range(message_ref.shape[0]):
        message_ref[k] = tile


def probe_kernel(gain_ref, last_ref, wq_ref, wkv_ref, probes_ref, raw_ref):
    raw = jnp.concatenate([last_ref[:, j, :] for j in range(last_ref.shape[1])], axis=1)
    raw_ref[...] = raw
    power = jnp.mean(raw * raw, axis=-1, keepdims=True)
    normed = raw * lax.rsqrt(power + epsilon) * gain_ref[...].astype(jnp.float32)
    queries = jnp.dot(normed.astype(jnp.bfloat16), wq_ref[...], preferred_element_type=jnp.float32)
    queries = queries.astype(jnp.bfloat16)
    keys = wkv_ref[:, :HEAD_DIM]
    for head in range(probes_ref.shape[1]):
        lanes = slice(head * HEAD_DIM, (head + 1) * HEAD_DIM)
        probes_ref[:, head, :] = dot_t(queries[:, lanes], keys).astype(jnp.bfloat16)


def pool_kernel(probes_ref, normed_ref, pooled_ref):
    items, per = probes_ref.shape[:2]
    probes = jnp.concatenate([probes_ref[k].astype(jnp.float32) for k in range(items)], axis=0)
    scores = dot_t(probes.astype(jnp.bfloat16), normed_ref[...]) * (1.0 / math.sqrt(HEAD_DIM))
    parts = jnp.exp(scores - jnp.max(scores, axis=1, keepdims=True))
    parts = parts / jnp.sum(parts, axis=1, keepdims=True)
    pooled = jnp.dot(parts.astype(jnp.bfloat16), normed_ref[...], preferred_element_type=jnp.float32)
    for k in range(items):
        pooled_ref[k] = pooled[k * per : (k + 1) * per].astype(jnp.bfloat16)


def project_kernel(
    scalar_ref,
    gain_ref,
    terms_ref,
    last_ref,
    weights_ref,
    copies_ref,
    embedded_ref,
):
    total = last_ref[...]
    for k in range(terms_ref.shape[0]):
        total = total + terms_ref[k].astype(jnp.float32)
    embedded = total.astype(jnp.bfloat16)
    embedded_ref[...] = embedded
    wide = embedded.astype(jnp.float32)
    power = jnp.mean(wide * wide, axis=-1, keepdims=True)
    normed = wide * lax.rsqrt(power + epsilon) * gain_ref[...].astype(jnp.float32)
    projected = jnp.dot(
        normed.astype(jnp.bfloat16),
        weights_ref[...],
        preferred_element_type=jnp.float32,
    ).astype(jnp.bfloat16)
    kv_at = projected.shape[1]
    share = copies_ref.shape[2] - kv_at
    columns = pl.ds(pl.multiple_of((2 * scalar_ref[2] + scalar_ref[1]) * share, share), share)
    features = embedded_ref[:, columns]
    for k in range(copies_ref.shape[0]):
        copies_ref[k, :, :kv_at] = projected
        copies_ref[k, :, kv_at:] = features


def layout_kernel(scalar_ref, weights_ref, theirs_ref, mine_ref):
    n_x, share, out_width = mine_ref.shape
    core, place = scalar_ref[1], scalar_ref[2]
    step = 1 - 2 * core
    for k, (theirs, mine) in enumerate(((2, 2), (step, -step), (-step, step), (0, 0))):
        rows = (2 * lax.rem(place + n_x + theirs, n_x) + 1 - core) * share
        rows = pl.ds(pl.multiple_of(rows, share), share)
        theirs_ref[k] = weights_ref[rows, -out_width:]
        rows = (2 * lax.rem(place + n_x + mine, n_x) + core) * share
        rows = pl.ds(pl.multiple_of(rows, share), share)
        mine_ref[k] = weights_ref[rows, -out_width:]


def user_kernel(
    scalar_ref, places_ref, catalog_ref, wo_ref, mixed_ref, terms_ref, residual_ref, picked_ref
):
    length = scalar_ref[0]
    slots, q_width = mixed_ref.shape
    catalog, kv_at = catalog_ref.shape[0], q_width + 2 * HEAD_DIM
    every = lax.broadcasted_iota(jnp.int32, (slots, catalog), 1)
    picks = jnp.where(places_ref[...] == every, 1.0, 0.0).astype(jnp.bfloat16)
    picked = jnp.dot(picks, catalog_ref[...], preferred_element_type=jnp.float32)
    picked_ref[...] = picked[:, :kv_at].astype(jnp.bfloat16)
    residual_ref[...] = picked[:, kv_at:].astype(jnp.bfloat16)
    scale = 1.0 / math.sqrt(HEAD_DIM)
    chunk = min(slots, 256)
    for start in range(0, slots, chunk):
        upto = start + chunk
        keys = picked_ref[:upto, q_width : q_width + HEAD_DIM]
        values = picked_ref[:upto, q_width + HEAD_DIM : kv_at]
        row = start + lax.broadcasted_iota(jnp.int32, (chunk, upto), 0)
        column = lax.broadcasted_iota(jnp.int32, (chunk, upto), 1)
        allowed = (column <= row) & (column < length)
        for head in range(q_width // HEAD_DIM):
            lanes = slice(head * HEAD_DIM, (head + 1) * HEAD_DIM)
            scores = dot_t(picked_ref[start:upto, lanes], keys) * scale
            scores = jnp.where(allowed, scores, -1e30)
            top = jnp.max(scores, axis=1, keepdims=True)
            parts = jnp.exp(scores - top)
            total = jnp.sum(parts, axis=1, keepdims=True)
            mixed = jnp.dot(parts.astype(jnp.bfloat16), values, preferred_element_type=jnp.float32)
            mixed_ref[start:upto, lanes] = (mixed / total).astype(jnp.bfloat16)
    for k in range(terms_ref.shape[0]):
        terms_ref[k] = dot_t(mixed_ref[...], wo_ref[k]).astype(jnp.bfloat16)


def pair_kernel(mixed_ref, wo_ref, theirs_ref, *pair_refs):
    for x, ref in enumerate(pair_refs):
        terms = dot_t(mixed_ref[...], wo_ref[x])
        ref[...] = (terms + theirs_ref[x].astype(jnp.float32)).astype(jnp.bfloat16)


SMEM = pl.BlockSpec(memory_space=pltpu.SMEM)
VMEM = pl.BlockSpec(memory_space=pltpu.VMEM)
ANY = pl.BlockSpec(memory_space=pl.ANY)


def call(kernel, name, limit, outs, in_specs, ins, scratch=()):
    return pl.pallas_call(
        kernel,
        name=name,
        out_shape=outs,
        in_specs=in_specs,
        out_specs=jax.tree.map(lambda _: VMEM, outs),
        scratch_shapes=scratch,
        compiler_params=pltpu.CompilerParams(vmem_limit_bytes=limit * MIB),
    )(*ins)


def local(
    item_states,
    item_gain,
    wq_item,
    wkv_item,
    wo_item,
    user_gain,
    wq_user,
    wkv_user,
    wo_user,
    history_items,
    history_lengths,
):
    width = item_states.shape[1]
    n_x = lax.axis_size("x")
    n_narrow = 2 * n_x
    share = width // n_narrow
    core = lax.axis_index("core")
    me = lax.axis_index("x") * 2 + core
    scale = 1.0 / math.sqrt(HEAD_DIM)

    columns = wq_user.shape[1] + 2 * HEAD_DIM + wo_user.shape[0]
    n_z = lax.axis_size("z")
    depth, heads_width = wq_user.shape
    kv_at = heads_width + 2 * HEAD_DIM
    columns = kv_at + wo_user.shape[0]
    copies = call(
        first_kernel,
        "user_weights",
        60,
        jax.ShapeDtypeStruct((n_z, depth, columns), jnp.bfloat16),
        [ANY] * 3,
        (wq_user, wkv_user.reshape(depth, -1), wo_user.T),
        [pltpu.SemaphoreType.DMA((3,))],
    )
    weights_z = lax.all_to_all(copies, "z", 0, 0).reshape(n_z * depth, columns)
    messages = call(
        message_kernel,
        "last_rows",
        20,
        jax.ShapeDtypeStruct((n_narrow, n_narrow, share), jnp.float32),
        [ANY],
        (item_states,),
        [pltpu.VMEM((16, width), jnp.bfloat16), pltpu.SemaphoreType.DMA],
    )
    length = history_lengths[0]
    weights_z, messages, normed, places, scalars, gain_row, item_gain_row = (
        lax.optimization_barrier(
            (
                weights_z,
                messages,
                rms_scale(item_states, item_gain),
                history_items[0][:, None],
                jnp.stack([length, core, lax.axis_index("x")]).astype(jnp.int32),
                user_gain[None],
                item_gain[None],
            )
        )
    )
    weights_all = lax.all_gather(weights_z, "y", axis=0, tiled=True)
    last_raw = lax.all_to_all(messages, NARROW, 0, 0)
    per = wq_item.shape[1] // HEAD_DIM
    wkv = wkv_item.reshape(width, -1)
    wv = wkv[:, HEAD_DIM:]
    probes, last_raw = call(
        probe_kernel,
        "item_probes",
        20,
        (
            jax.ShapeDtypeStruct((n_narrow, per, width), jnp.bfloat16),
            jax.ShapeDtypeStruct((n_narrow, width), jnp.float32),
        ),
        [VMEM] * 4,
        (item_gain_row, last_raw, wq_item, wkv),
    )
    probes = lax.all_to_all(probes, NARROW, 0, 0)
    pooled = call(
        pool_kernel,
        "item_attention",
        20,
        jax.ShapeDtypeStruct(probes.shape, jnp.bfloat16),
        [VMEM] * 2,
        (probes, normed),
    )
    pooled = lax.all_to_all(pooled, NARROW, 0, 0)
    mixed = jnp.dot(pooled.reshape(-1, width), wv, preferred_element_type=jnp.float32)
    mixed = mixed.astype(jnp.bfloat16).reshape(n_narrow, -1)
    partial_sum = jnp.dot(mixed, wo_item, preferred_element_type=jnp.float32)
    terms = spread(partial_sum.astype(jnp.bfloat16), NARROW)
    group = terms.shape[1]
    copies, embedded = call(
        project_kernel,
        "project_items",
        20,
        (
            jax.ShapeDtypeStruct((lax.axis_size(WIDE), group, kv_at + share), jnp.bfloat16),
            jax.ShapeDtypeStruct((group, width), jnp.bfloat16),
        ),
        [SMEM] + [VMEM] * 4,
        (scalars, gain_row, terms, last_raw, weights_all[:, :kv_at]),
    )
    item_part = lax.dynamic_slice_in_dim(embedded, me * share, share, 1)

    catalog = lax.all_to_all(copies, WIDE, 0, 0).reshape(-1, kv_at + share)

    wo_theirs, wo_mine = call(
        layout_kernel,
        "output_weights",
        20,
        [jax.ShapeDtypeStruct((n_x, share, wo_user.shape[0]), jnp.bfloat16)] * 2,
        [SMEM, VMEM],
        (scalars, weights_all),
    )
    slots = history_items.shape[1]
    user_mixed, theirs, residual = call(
        user_kernel,
        "user_attention",
        20,
        (
            jax.ShapeDtypeStruct((slots, heads_width), jnp.bfloat16),
            jax.ShapeDtypeStruct((n_x, slots, share), jnp.bfloat16),
            jax.ShapeDtypeStruct((slots, share), jnp.bfloat16),
        ),
        [SMEM] + [VMEM] * 3,
        (scalars, places, catalog, wo_theirs),
        [pltpu.VMEM((slots, kv_at), jnp.bfloat16)],
    )

    theirs = swap_cores(theirs)
    first, direct, second, own = call(
        pair_kernel,
        "pair_sum",
        20,
        [jax.ShapeDtypeStruct((slots, share), jnp.bfloat16)] * n_x,
        [VMEM] * 3,
        (user_mixed, wo_mine, theirs),
    )
    relay = along_x(first, 1)
    direct = along_x(direct, -1)
    relay = (relay.astype(jnp.float32) + second.astype(jnp.float32)).astype(jnp.bfloat16)
    relay = along_x(relay, 1)
    summed = own.astype(jnp.float32) + direct.astype(jnp.float32) + relay.astype(jnp.float32)
    live = (jnp.arange(slots, dtype=jnp.int32) < length)[:, None]
    user_states = jnp.where(live, residual.astype(jnp.float32) + summed, 0.0).astype(jnp.bfloat16)
    return (item_part, user_states)


def solution(mesh):
    n_wide, n_narrow = mesh.shape["wide"], mesh.shape["narrow"]
    side = math.isqrt(n_wide)
    fine = Mesh(
        mesh.devices.reshape(side, n_wide // side, n_narrow // 2, 2), WIDE + NARROW
    )
    return jax.shard_map(
        local,
        mesh=fine,
        in_specs=(
            P(WIDE + NARROW, None),
            P(),
            P(None, NARROW),
            P(None, NARROW, None),
            P(NARROW, None),
            P(),
            P(WIDE, NARROW),
            P(WIDE, NARROW, None),
            P(NARROW, WIDE),
            P(WIDE, None),
            P(WIDE),
        ),
        out_specs=(P(WIDE, NARROW), P(WIDE, NARROW)),
        check_vma=False,
    )
```

time: 145 us -> 143 us (0.986)
  blocking collectives: 46.8 us -> 26.8 us
  starting transfers between devices: 27.4 us -> 37.1 us
  waiting for transfers between devices: 34.2 us -> 41.3 us
  matrix products: 2.92 us -> 0.58 us
  local copies, waits for them, and re-layouts: 5.25 us -> 7.36 us
    all_to_all x2 -> x3, blocking collectives: 46.8 us -> 26.8 us  [the longest x1 9.72 us: local(): last_raw = lax.all_to_all(messages, NARROW, 0, 0)]
    all_to_all x4 -> x3, starting transfers between devices: 14.4 us -> 25.5 us  [the longest x1 11.8 us: local(): catalog = lax.all_to_all(copies, WIDE, 0, 0).reshape(-1, kv_at + share)]
    all_gather x1, waiting for transfers between devices: 0.01 us -> 6.49 us  [local(): weights_all = lax.all_gather(weights_z, 'y', axis=0, tiled=True)]
    all_to_all x4 -> x3, waiting for transfers between devices: 18.9 us -> 23.5 us  [the longest x1 16.6 us: local(): catalog = lax.all_to_all(copies, WIDE, 0, 0).reshape(-1, kv_at + share)]
    ppermute x2 -> x1, waiting for transfers between devices: 4.97 us -> 2.63 us  [swap_cores(): return lax.ppermute(values, 'core', [(0, 1), (1, 0)])]
    ppermute x2 -> x1, starting transfers between devices: 3.95 us -> 1.92 us  [swap_cores(): return lax.ppermute(values, 'core', [(0, 1), (1, 0)])]
    ppermute x3, waiting for transfers between devices: 10.3 us -> 8.66 us  [along_x(): return lax.ppermute(values, NARROW, pairs)]
    reshape x4 -> x0, local copies, waits for them, and re-layouts: 1.58 us -> none  [the longest x1 0.74 us: local(): probes = lax.all_to_all(probes.reshape(n_narrow, per, width), NARROW, 0, 0)]
  transfers between devices with their start and end apart: 10 -> 8, of which waited for: 8 -> 6; matrix products, arithmetic and copies ran while one was open for 6% -> 6% of each run, Pallas kernels for 1% -> 2%
where the time goes in v5:
time: 143 us
  waiting for transfers between devices  41.3 us (29%)
  starting transfers between devices  37.1 us (26%)
  blocking collectives  26.8 us (19%)
  between operations  14.9 us (10%)
  Pallas kernels  10.3 us (7%)
  local copies, waits for them, and re-layouts  7.36 us (5%)
  other arithmetic  4.23 us (3%)
    all_to_all x1, waiting for transfers between devices, local(): catalog = lax.all_to_all(copies, WIDE, 0, 0).reshape(-1, kv_at + share)  16.6 us
    all_to_all x1, starting transfers between devices, local(): catalog = lax.all_to_all(copies, WIDE, 0, 0).reshape(-1, kv_at + share)  11.8 us
    all_to_all x1, starting transfers between devices, local(): weights_z = lax.all_to_all(copies, 'z', 0, 0).reshape(n_z * depth, columns)  10.3 us
    pallas_call x8, Pallas kernels, call(): pl.pallas_call(kernel, name=name, out_shape=outs, in_specs=in_specs, out_...  10.3 us
    all_to_all x1, blocking collectives, local(): last_raw = lax.all_to_all(messages, NARROW, 0, 0)  9.72 us
    ppermute x3, starting transfers between devices, along_x(): return lax.ppermute(values, NARROW, pairs)  9.64 us
    ppermute x3, waiting for transfers between devices, along_x(): return lax.ppermute(values, NARROW, pairs)  8.66 us
    all_to_all x1, blocking collectives, local(): probes = lax.all_to_all(probes, NARROW, 0, 0)  8.52 us
  transfers between devices with their start and end apart: 8, of which 6 were waited for; matrix products, arithmetic and copies ran while one was open for 6% of the time, Pallas kernels for 2%

profile of v5, /device:TPU:16, one launch (start us, length us, event | category | flops | bytes accessed | tf_op | source)
XLA Modules:
  0.0 142.5 jit_solution(14984446208329832049)
XLA Ops:
  7.2 0.0 copy-start
  7.2 0.0 copy-start.3
  7.2 1.6 %user_weights.1 = bf16[8,32,640]{2,1,0:T(8,128)(2,1)} custom-call(bf16[32,256]{1,0:T(8,128)(2,1)} %wq_ref.2, bf16[32,128]{1,0:T(8,128)(2,1)} %bitcast.17, bf16[32,256]{1,0:T(8,128)(2,1)} %bitcast.16), custom_call_target="tpu_custom_call" | custom-call | tf_op jit(solution)/shard_map/user_weights/pallas_call | solution.py:191
  8.8 10.3 %all-to-all-start = ((bf16[8,32,640]{2,1,0:T(8,128)(2,1)}), bf16[8,32,640]{2,1,0:T(8,128)(2,1)}, u32[]{:S(2)}, u32[]{:S(2)}) async-start(bf16[8,32,640]{2,1,0:T(8,128)(2,1)} %user_weights.1), calls=%async_computation | async-start | bytes 655360 | tf_op jit(solution)/shard_map/all_to_all | solution.py:237
  19.2 0.0 all-gather.2.cloned.1.call-start
  19.2 1.2 fusion
  20.5 1.0 copy-done.2
  21.5 0.1 last_rows.1
  21.6 0.8 convert_element_type.40
  22.3 0.7 broadcast_in_dim.28.gain_ref
  23.7 0.7 broadcast_in_dim.27.gain_ref
  24.4 0.1 pad_add_fusion.scalar_ref
  24.5 1.2 fusion.2.normed_ref
  25.7 6.8 %all-to-all-done = bf16[8,32,640]{2,1,0:T(8,128)(2,1)} async-done(((bf16[8,32,640]{2,1,0:T(8,128)(2,1)}), bf16[8,32,640]{2,1,0:T(8,128)(2,1)}, u32[]{:S(2)}, u32[]{:S(2)}) %all-to-all-start) | async-done | bytes 327712 | tf_op jit(solution)/shard_map/all_to_all | solution.py:237
  32.6 0.0 all-gather.2.cloned.1.call-update
  32.6 9.7 %all_to_all.30.last_ref = f32[8,8,256]{2,1,0:T(8,128)S(1)} all-to-all(f32[8,8,256]{2,1,0:T(8,128)S(1)} %last_rows.1), channel_id=1, replica_groups=mesh['y'=8,'z'=8,'x'=4,'core'=2] {'x','core'}, dimensions={0} | all-to-all | bytes 131072 | tf_op jit(solution)/shard_map/all_to_all | solution.py:262
  42.3 1.3 item_probes.1
  43.6 8.5 %all_to_all.31.probes_ref = bf16[8,4,2048]{2,1,0:T(4,128)(2,1)S(1)} all-to-all(bf16[8,4,2048]{2,1,0:T(4,128)(2,1)S(1)} %get-tuple-element.26), channel_id=1, replica_groups=mesh['y'=8,'z'=8,'x'=4,'core'=2] {'x','core'}, dimensions={0} | all-to-all | bytes 262144 | tf_op jit(solution)/shard_map/all_to_all | solution.py:277
  52.1 0.7 item_attention.1
  52.8 8.5 %all_to_all.32 = bf16[8,4,2048]{2,1,0:T(4,128)(2,1)S(1)} all-to-all(bf16[8,4,2048]{2,1,0:T(4,128)(2,1)S(1)} %item_attention.1), channel_id=1, replica_groups=mesh['y'=8,'z'=8,'x'=4,'core'=2] {'x','core'}, dimensions={0} | all-to-all | bytes 262144 | tf_op jit(solution)/shard_map/all_to_all | solution.py:286
  61.4 0.3 convolution_convert_fusion.1
  61.7 0.1 reshape.40
  61.8 0.2 convolution_convert_fusion
  62.1 0.7 broadcast_in_dim.29
  62.8 3.4 %all-to-all-start.4 = ((bf16[8,8,2048]{2,1,0:T(8,128)(2,1)}), bf16[8,8,2048]{2,1,0:T(8,128)(2,1)S(1)}, u32[]{:S(2)}, u32[]{:S(2)}) async-start(bf16[8,8,2048]{2,1,0:T(8,128)(2,1)} %broadcast_in_dim.29), calls=%async_computation.4 | async-start | bytes 524288 | tf_op jit(solution)/shard_map/all_to_all | solution.py:33
  66.2 0.0 copy-start.5
  66.2 6.5 %all-gather.2.cloned.1.call-done.weights_ref = bf16[2048,640]{1,0:T(8,128)(2,1)} async-done(((bf16[256,640]{1,0:T(8,128)(2,1)}), bf16[2048,640]{1,0:T(8,128)(2,1)}) %all-gather.2.cloned.1.call-update) | async-done | bytes 2621456 | tf_op jit(solution)/shard_map/all_gather | solution.py:261
  72.7 1.6 %slice.9.weights_ref = bf16[2048,384]{1,0:T(8,128)(2,1)S(1)} slice(bf16[2048,640]{1,0:T(8,128)(2,1)} %all-gather.2.cloned.1.call-done.weights_ref), slice={[0:2048], [0:384]} | slice | bytes 3145728 | tf_op jit(solution)/shard_map/slice | solution.py:301
  74.3 0.0 all-to-all-done.4.terms_ref
  74.3 1.8 %project_items.1 = (bf16[64,8,640]{2,1,0:T(8,128)(2,1)}, bf16[8,2048]{1,0:T(8,128)(2,1)S(1)}) custom-call(s32[3]{0:T(128)S(1)} %pad_add_fusion.scalar_ref, bf16[1,2048]{1,0:T(2,128)(2,1)S(1)} %broadcast_in_dim.27.gain_ref, bf16[8,8,2048]{2,1,0:T(8,128)(2,1)S(1)} %all-to-all-done.4.terms_ref, f32[8,2048]{1,0:T(8,128)S(1)} %get-tuple-element.28.last_ref, ...), custom_call_target="tpu_custom_call" | custom-call | tf_op jit(solution)/shard_map/project_items/pallas_call | solution.py:191
  76.1 11.8 %all-to-all-start.5 = ((bf16[64,8,640]{2,1,0:T(8,128)(2,1)}), bf16[64,8,640]{2,1,0:T(8,128)(2,1)S(1)}, u32[]{:S(2)}, u32[]{:S(2)}) async-start(bf16[64,8,640]{2,1,0:T(8,128)(2,1)} %get-tuple-element.32), calls=%async_computation.5 | async-start | bytes 1310720 | tf_op jit(solution)/shard_map/all_to_all | solution.py:305
  88.0 0.1 copy.13.places_ref
  88.1 1.7 %copy-done.1 = bf16[2048,640]{1,0:T(8,128)(2,1)S(1)} copy-done((bf16[2048,640]{1,0:T(8,128)(2,1)S(1)}, bf16[2048,640]{1,0:T(8,128)(2,1)}, u32[]{:S(2)}) %copy-start.1) | copy-done | bytes 2621464
  89.9 0.6 output_weights.1
  90.5 16.6 %all-to-all-done.5 = bf16[64,8,640]{2,1,0:T(8,128)(2,1)S(1)} async-done(((bf16[64,8,640]{2,1,0:T(8,128)(2,1)}), bf16[64,8,640]{2,1,0:T(8,128)(2,1)S(1)}, u32[]{:S(2)}, u32[]{:S(2)}) %all-to-all-start.5) | async-done | bytes 655392 | tf_op jit(solution)/shard_map/all_to_all | solution.py:305
  107.1 3.6 %user_attention.1 = (bf16[512,256]{1,0:T(8,128)(2,1)S(1)}, bf16[4,512,256]{2,1,0:T(8,128)(2,1)S(1)}, bf16[512,256]{1,0:T(8,128)(2,1)S(1)}) custom-call(s32[3]{0:T(128)S(1)} %pad_add_fusion.scalar_ref, s32[512,1]{1,0:T(8,128)S(1)} %copy.13.places_ref, bf16[512,640]{1,0:T(8,128)(2,1)S(1)} %bitcast.13, bf16[4,256,256]{2,1,0:T(8,128)(2,1)S(1)} %get-tuple-element.33.wo_ref), custom_call_target="tpu_custom_call" | custom-call | tf_op jit(solution)/shard_map/user_attention/pallas_call | solution.py:191
  110.8 1.9 %collective-permute-start = (bf16[4,512,256]{2,1,0:T(8,128)(2,1)S(1)}, bf16[4,512,256]{2,1,0:T(8,128)(2,1)S(1)}, u32[]{:S(2)}, u32[]{:S(2)}) collective-permute-start(bf16[4,512,256]{2,1,0:T(8,128)(2,1)S(1)} %get-tuple-element.37), channel_id=1, source_target_pairs={{0,1},{1,0},{2,3},{3,2},{4,5},{5,4},{6,7},{7,6},{8,9},{9,8},{10,11... | collective-permute-start | bytes 3145736 | tf_op jit(solution)/shard_map/ppermute | solution.py:37
  112.7 2.6 %collective-permute-done.theirs_ref = bf16[4,512,256]{2,1,0:T(8,128)(2,1)S(1)} collective-permute-done((bf16[4,512,256]{2,1,0:T(8,128)(2,1)S(1)}, bf16[4,512,256]{2,1,0:T(8,128)(2,1)S(1)}, u32[]{:S(2)}, u32[]{:S(2)}) %collective-permute-start) | collective-permute-done | bytes 1048608 | tf_op jit(solution)/shard_map/ppermute | solution.py:37
  115.3 0.5 pair_sum.1
  115.8 3.4 %collective-permute-start.2 = (bf16[512,256]{1,0:T(8,128)(2,1)S(1)}, bf16[512,256]{1,0:T(8,128)(2,1)S(1)}, u32[]{:S(2)}, u32[]{:S(2)}) collective-permute-start(bf16[512,256]{1,0:T(8,128)(2,1)S(1)} %get-tuple-element.40), channel_id=1, source_target_pairs={{0,2},{1,7},{2,4},{3,1},{4,6},{5,3},{6,0},{7,5},{8,10},{9,15},{10,... | collective-permute-start | bytes 786440 | tf_op jit(solution)/shard_map/ppermute | solution.py:47
  119.2 3.7 %collective-permute-start.1 = (bf16[512,256]{1,0:T(8,128)(2,1)S(1)}, bf16[512,256]{1,0:T(8,128)(2,1)S(1)}, u32[]{:S(2)}, u32[]{:S(2)}) collective-permute-start(bf16[512,256]{1,0:T(8,128)(2,1)S(1)} %get-tuple-element.39), channel_id=1, source_target_pairs={{0,6},{1,3},{2,0},{3,5},{4,2},{5,7},{6,4},{7,1},{8,14},{9,11},{10,... | collective-permute-start | bytes 786440 | tf_op jit(solution)/shard_map/ppermute | solution.py:47
  122.9 2.4 %collective-permute-done.2 = bf16[512,256]{1,0:T(8,128)(2,1)S(1)} collective-permute-done((bf16[512,256]{1,0:T(8,128)(2,1)S(1)}, bf16[512,256]{1,0:T(8,128)(2,1)S(1)}, u32[]{:S(2)}, u32[]{:S(2)}) %collective-permute-start.2) | collective-permute-done | bytes 262176 | tf_op jit(solution)/shard_map/ppermute | solution.py:47
  125.3 0.1 add_convert_fusion
  125.4 2.6 %collective-permute-start.3 = (bf16[512,256]{1,0:T(8,128)(2,1)S(1)}, bf16[512,256]{1,0:T(8,128)(2,1)S(1)}, u32[]{:S(2)}, u32[]{:S(2)}) collective-permute-start(bf16[512,256]{1,0:T(8,128)(2,1)S(1)} %add_convert_fusion), channel_id=1, source_target_pairs={{0,2},{1,7},{2,4},{3,1},{4,6},{5,3},{6,0},{7,5},{8,10},{9,15},{10,... | collective-permute-start | bytes 786440 | tf_op jit(solution)/shard_map/ppermute | solution.py:47
  128.0 0.6 constant_dynamic-slice_fusion
  128.6 0.0 collective-permute-done.1
  128.6 6.3 %collective-permute-done.3 = bf16[512,256]{1,0:T(8,128)(2,1)S(1)} collective-permute-done((bf16[512,256]{1,0:T(8,128)(2,1)S(1)}, bf16[512,256]{1,0:T(8,128)(2,1)S(1)}, u32[]{:S(2)}, u32[]{:S(2)}) %collective-permute-start.3) | collective-permute-done | bytes 262176 | tf_op jit(solution)/shard_map/ppermute | solution.py:47
  134.8 0.9 select_convert_fusion
  (10 shorter events, 0.1 us)
Async XLA Ops:
  7.2 54.6 %copy-start = (bf16[256,2048]{1,0:T(8,128)(2,1)S(1)}, bf16[256,2048]{1,0:T(8,128)(2,1)}, u32[]{:S(2)}) copy-start(bf16[256,2048]{1,0:T(8,128)(2,1)} %param.15) | copy-start | bytes 3145732
  7.2 35.1 %copy-start.3 = (bf16[2048,1,128]{2,0,1:T(8,128)(2,1)S(1)}, bf16[2048,1,128]{2,0,1:T(8,128)(2,1)}, u32[]{:S(2)}) copy-start(bf16[2048,1,128]{2,0,1:T(8,128)(2,1)} %param.14) | copy-start | bytes 1572868
  8.8 23.7 %all-to-all-start = ((bf16[8,32,640]{2,1,0:T(8,128)(2,1)}), bf16[8,32,640]{2,1,0:T(8,128)(2,1)}, u32[]{:S(2)}, u32[]{:S(2)}) async-start(bf16[8,32,640]{2,1,0:T(8,128)(2,1)} %user_weights.1), calls=%async_computation | async-start | bytes 655360 | tf_op jit(solution)/shard_map/all_to_all | solution.py:237
  19.2 53.5 %all-gather.2.cloned.1.call-start = ((), (), s32[]{:S(2)}) async-start(), calls=%async_computation.6 | async-start | bytes 2949120 | tf_op jit(solution)/shard_map/all_gather | solution.py:261
  20.5 1.0 copy-start.2
  21.5 20.8 %copy-start.4 = (bf16[2048,256]{1,0:T(8,128)(2,1)S(1)}, bf16[2048,256]{1,0:T(8,128)(2,1)}, u32[]{:S(2)}) copy-start(bf16[2048,256]{1,0:T(8,128)(2,1)} %wq_ref.3) | copy-start | bytes 3145732
  62.8 11.5 %all-to-all-start.4 = ((bf16[8,8,2048]{2,1,0:T(8,128)(2,1)}), bf16[8,8,2048]{2,1,0:T(8,128)(2,1)S(1)}, u32[]{:S(2)}, u32[]{:S(2)}) async-start(bf16[8,8,2048]{2,1,0:T(8,128)(2,1)} %broadcast_in_dim.29), calls=%async_computation.4 | async-start | bytes 524288 | tf_op jit(solution)/shard_map/all_to_all | solution.py:33
  66.2 21.7 %copy-start.5 = (s32[1,512]{1,0:T(1,128)S(1)}, s32[1,512]{1,0:T(1,128)}, u32[]{:S(2)}) copy-start(s32[1,512]{1,0:T(1,128)} %param.20) | copy-start | bytes 6148
  76.1 31.0 %all-to-all-start.5 = ((bf16[64,8,640]{2,1,0:T(8,128)(2,1)}), bf16[64,8,640]{2,1,0:T(8,128)(2,1)S(1)}, u32[]{:S(2)}, u32[]{:S(2)}) async-start(bf16[64,8,640]{2,1,0:T(8,128)(2,1)} %get-tuple-element.32), calls=%async_computation.5 | async-start | bytes 1310720 | tf_op jit(solution)/shard_map/all_to_all | solution.py:305
  88.1 1.7 %copy-start.1 = (bf16[2048,640]{1,0:T(8,128)(2,1)S(1)}, bf16[2048,640]{1,0:T(8,128)(2,1)}, u32[]{:S(2)}) copy-start(bf16[2048,640]{1,0:T(8,128)(2,1)} %all-gather.2.cloned.1.call-done.weights_ref) | copy-start | bytes 7864324
  110.8 4.6 %collective-permute-start = (bf16[4,512,256]{2,1,0:T(8,128)(2,1)S(1)}, bf16[4,512,256]{2,1,0:T(8,128)(2,1)S(1)}, u32[]{:S(2)}, u32[]{:S(2)}) collective-permute-start(bf16[4,512,256]{2,1,0:T(8,128)(2,1)S(1)} %get-tuple-element.37), channel_id=1, source_target_pairs={{0,1},{1,0},{2,3},{3,2},{4,5},{5,4},{6,7},{7,6},{8,9},{9,8},{10,11... | collective-permute-start | bytes 3145736 | tf_op jit(solution)/shard_map/ppermute | solution.py:37
  115.8 9.5 %collective-permute-start.2 = (bf16[512,256]{1,0:T(8,128)(2,1)S(1)}, bf16[512,256]{1,0:T(8,128)(2,1)S(1)}, u32[]{:S(2)}, u32[]{:S(2)}) collective-permute-start(bf16[512,256]{1,0:T(8,128)(2,1)S(1)} %get-tuple-element.40), channel_id=1, source_target_pairs={{0,2},{1,7},{2,4},{3,1},{4,6},{5,3},{6,0},{7,5},{8,10},{9,15},{10,... | collective-permute-start | bytes 786440 | tf_op jit(solution)/shard_map/ppermute | solution.py:47
  119.2 9.4 %collective-permute-start.1 = (bf16[512,256]{1,0:T(8,128)(2,1)S(1)}, bf16[512,256]{1,0:T(8,128)(2,1)S(1)}, u32[]{:S(2)}, u32[]{:S(2)}) collective-permute-start(bf16[512,256]{1,0:T(8,128)(2,1)S(1)} %get-tuple-element.39), channel_id=1, source_target_pairs={{0,6},{1,3},{2,0},{3,5},{4,2},{5,7},{6,4},{7,1},{8,14},{9,11},{10,... | collective-permute-start | bytes 786440 | tf_op jit(solution)/shard_map/ppermute | solution.py:47
  125.4 9.5 %collective-permute-start.3 = (bf16[512,256]{1,0:T(8,128)(2,1)S(1)}, bf16[512,256]{1,0:T(8,128)(2,1)S(1)}, u32[]{:S(2)}, u32[]{:S(2)}) collective-permute-start(bf16[512,256]{1,0:T(8,128)(2,1)S(1)} %add_convert_fusion), channel_id=1, source_target_pairs={{0,2},{1,7},{2,4},{3,1},{4,6},{5,3},{6,0},{7,5},{8,10},{9,15},{10,... | collective-permute-start | bytes 786440 | tf_op jit(solution)/shard_map/ppermute | solution.py:47
Sparse Core Ops, SparseCore 0:
  32.7 39.9 all-gather.1

commit v6 on v5

--- a/solution.py
+++ b/solution.py
@@ -99,15 +99,7 @@
         pooled_ref[k] = pooled[k * per : (k + 1) * per].astype(jnp.bfloat16)
 
 
-def project_kernel(
-    scalar_ref,
-    gain_ref,
-    terms_ref,
-    last_ref,
-    weights_ref,
-    copies_ref,
-    embedded_ref,
-):
+def embed_kernel(gain_ref, terms_ref, last_ref, embedded_ref, normed_ref):
     total = last_ref[...]
     for k in range(terms_ref.shape[0]):
         total = total + terms_ref[k].astype(jnp.float32)
@@ -116,18 +108,7 @@
     wide = embedded.astype(jnp.float32)
     power = jnp.mean(wide * wide, axis=-1, keepdims=True)
     normed = wide * lax.rsqrt(power + epsilon) * gain_ref[...].astype(jnp.float32)
-    projected = jnp.dot(
-        normed.astype(jnp.bfloat16),
-        weights_ref[...],
-        preferred_element_type=jnp.float32,
-    ).astype(jnp.bfloat16)
-    kv_at = projected.shape[1]
-    share = copies_ref.shape[2] - kv_at
-    columns = pl.ds(pl.multiple_of((2 * scalar_ref[2] + scalar_ref[1]) * share, share), share)
-    features = embedded_ref[:, columns]
-    for k in range(copies_ref.shape[0]):
-        copies_ref[k, :, :kv_at] = projected
-        copies_ref[k, :, kv_at:] = features
+    normed_ref[...] = normed.astype(jnp.bfloat16)
 
 
 def layout_kernel(scalar_ref, weights_ref, theirs_ref, mine_ref):
@@ -144,7 +125,7 @@
 
 
 def user_kernel(
-    scalar_ref, places_ref, catalog_ref, wo_ref, mixed_ref, terms_ref, residual_ref, picked_ref
+    scalar_ref, places_ref, catalog_ref, mixed_ref, residual_ref, picked_ref
 ):
     length = scalar_ref[0]
     slots, q_width = mixed_ref.shape
@@ -172,14 +153,12 @@
             total = jnp.sum(parts, axis=1, keepdims=True)
             mixed = jnp.dot(parts.astype(jnp.bfloat16), values, preferred_element_type=jnp.float32)
             mixed_ref[start:upto, lanes] = (mixed / total).astype(jnp.bfloat16)
-    for k in range(terms_ref.shape[0]):
-        terms_ref[k] = dot_t(mixed_ref[...], wo_ref[k]).astype(jnp.bfloat16)
-
-
-def pair_kernel(mixed_ref, wo_ref, theirs_ref, *pair_refs):
-    for x, ref in enumerate(pair_refs):
-        terms = dot_t(mixed_ref[...], wo_ref[x])
-        ref[...] = (terms + theirs_ref[x].astype(jnp.float32)).astype(jnp.bfloat16)
+
+
+def output_kernel(mine_ref, others_ref, wo_mine_ref, wo_others_ref, *block_refs):
+    for k, ref in enumerate(block_refs):
+        terms = dot_t(mine_ref[...], wo_mine_ref[k]) + dot_t(others_ref[...], wo_others_ref[k])
+        ref[...] = terms.astype(jnp.bfloat16)
 
 
 SMEM = pl.BlockSpec(memory_space=pltpu.SMEM)
@@ -289,20 +268,21 @@
     partial_sum = jnp.dot(mixed, wo_item, preferred_element_type=jnp.float32)
     terms = spread(partial_sum.astype(jnp.bfloat16), NARROW)
     group = terms.shape[1]
-    copies, embedded = call(
-        project_kernel,
-        "project_items",
-        20,
-        (
-            jax.ShapeDtypeStruct((lax.axis_size(WIDE), group, kv_at + share), jnp.bfloat16),
-            jax.ShapeDtypeStruct((group, width), jnp.bfloat16),
-        ),
-        [SMEM] + [VMEM] * 4,
-        (scalars, gain_row, terms, last_raw, weights_all[:, :kv_at]),
+    embedded, items_normed = call(
+        embed_kernel,
+        "item_embeddings",
+        20,
+        [jax.ShapeDtypeStruct((group, width), jnp.bfloat16)] * 2,
+        [VMEM] * 3,
+        (gain_row, terms, last_raw),
     )
     item_part = lax.dynamic_slice_in_dim(embedded, me * share, share, 1)
-
-    catalog = lax.all_to_all(copies, WIDE, 0, 0).reshape(-1, kv_at + share)
+    projected = jnp.dot(
+        items_normed, weights_all[:, :kv_at], preferred_element_type=jnp.float32
+    ).astype(jnp.bfloat16)
+    projected = jnp.concatenate([projected, item_part], axis=1)
+
+    catalog = spread(projected, WIDE).reshape(-1, kv_at + share)
 
     wo_theirs, wo_mine = call(
         layout_kernel,
@@ -312,29 +292,28 @@
         [SMEM, VMEM],
         (scalars, weights_all),
     )
+    wo_others = swap_cores(wo_theirs)
     slots = history_items.shape[1]
-    user_mixed, theirs, residual = call(
+    user_mixed, residual = call(
         user_kernel,
         "user_attention",
         20,
         (
             jax.ShapeDtypeStruct((slots, heads_width), jnp.bfloat16),
-            jax.ShapeDtypeStruct((n_x, slots, share), jnp.bfloat16),
             jax.ShapeDtypeStruct((slots, share), jnp.bfloat16),
         ),
-        [SMEM] + [VMEM] * 3,
-        (scalars, places, catalog, wo_theirs),
+        [SMEM] + [VMEM] * 2,
+        (scalars, places, catalog),
         [pltpu.VMEM((slots, kv_at), jnp.bfloat16)],
     )
 
-    theirs = swap_cores(theirs)
     first, direct, second, own = call(
-        pair_kernel,
-        "pair_sum",
+        output_kernel,
+        "output_blocks",
         20,
         [jax.ShapeDtypeStruct((slots, share), jnp.bfloat16)] * n_x,
-        [VMEM] * 3,
-        (user_mixed, wo_mine, theirs),
+        [VMEM] * 4,
+        (user_mixed, swap_cores(user_mixed), wo_mine, wo_others),
     )
     relay = along_x(first, 1)
     direct = along_x(direct, -1)

time: 143 us -> 142 us (level)
  waiting for transfers between devices: 41.3 us -> 39.1 us
  matrix products: 0.58 us -> 2.3 us
    all_to_all x1 -> x2, waiting for transfers between devices: 0.01 us -> 21.4 us  [spread(): return lax.all_to_all(copies, axis, 0, 0)]
    all_to_all x1 -> x0, waiting for transfers between devices: 16.6 us -> none  [local(): catalog = lax.all_to_all(copies, WIDE, 0, 0).reshape(-1, kv_at + share)]
    all_to_all x1 -> x0, starting transfers between devices: 11.8 us -> none  [local(): catalog = lax.all_to_all(copies, WIDE, 0, 0).reshape(-1, kv_at + share)]
    all_to_all x1 -> x2, starting transfers between devices: 3.41 us -> 14.1 us  [spread(): return lax.all_to_all(copies, axis, 0, 0)]
    all_gather x1, waiting for transfers between devices: 6.49 us -> 0.02 us  [local(): weights_all = lax.all_gather(weights_z, 'y', axis=0, tiled=True)]
    ppermute x1 -> x2, starting transfers between devices: 1.92 us -> 3.83 us  [swap_cores(): return lax.ppermute(values, 'core', [(0, 1), (1, 0)])]
    dot_general x0 -> x1, matrix products: none -> 1.72 us  [local(): jnp.dot(items_normed, weights_all[:, :kv_at], preferred_element_type=jnp....]
    slice x1 -> x0, local copies, waits for them, and re-layouts: 1.57 us -> none  [local(): weights_all[:, :kv_at]]
  transfers between devices with their start and end apart: 8 -> 9, of which waited for: 6 -> 6; matrix products, arithmetic and copies ran while one was open for 6% -> 4% of each run, Pallas kernels for 2% -> 5%
where the time goes in v6:
time: 142 us; the launch traced here: 141 us
  waiting for transfers between devices  39.1 us (28%)
  starting transfers between devices  37.9 us (27%)
  blocking collectives  26.8 us (19%)
  between operations  14.9 us (10%)
  Pallas kernels  9.35 us (7%)
  local copies, waits for them, and re-layouts  6.09 us (4%)
  other arithmetic  4.18 us (3%)
  matrix products  2.3 us (2%)
    all_to_all x2, waiting for transfers between devices, spread(): return lax.all_to_all(copies, axis, 0, 0)  21.4 us
    all_to_all x2, starting transfers between devices, spread(): return lax.all_to_all(copies, axis, 0, 0)  14.1 us
    all_to_all x1, starting transfers between devices, local(): weights_z = lax.all_to_all(copies, 'z', 0, 0).reshape(n_z * depth, columns)  10.3 us
    all_to_all x1, blocking collectives, local(): last_raw = lax.all_to_all(messages, NARROW, 0, 0)  9.72 us
    ppermute x3, starting transfers between devices, along_x(): return lax.ppermute(values, NARROW, pairs)  9.64 us
    pallas_call x8, Pallas kernels, call(): pl.pallas_call(kernel, name=name, out_shape=outs, in_specs=in_specs, out_...  9.35 us
    ppermute x3, waiting for transfers between devices, along_x(): return lax.ppermute(values, NARROW, pairs)  9.27 us
    all_to_all x1, blocking collectives, local(): probes = lax.all_to_all(probes, NARROW, 0, 0)  8.52 us
  transfers between devices with their start and end apart: 9, of which 6 were waited for; matrix products, arithmetic and copies ran while one was open for 4% of the time, Pallas kernels for 5%

profile of v6, /device:TPU:16, one launch (start us, length us, event | category | flops | bytes accessed | tf_op | source)
XLA Modules:
  0.0 140.6 jit_solution(5410786112395419801)
XLA Ops:
  7.2 0.0 copy-start
  7.2 1.7 %user_weights.1 = bf16[8,32,640]{2,1,0:T(8,128)(2,1)} custom-call(bf16[32,256]{1,0:T(8,128)(2,1)} %wq_ref.2, bf16[32,128]{1,0:T(8,128)(2,1)} %bitcast.18, bf16[32,256]{1,0:T(8,128)(2,1)} %bitcast.17), custom_call_target="tpu_custom_call" | custom-call | tf_op jit(solution)/shard_map/user_weights/pallas_call | solution.py:170
  8.9 10.3 %all-to-all-start = ((bf16[8,32,640]{2,1,0:T(8,128)(2,1)}), bf16[8,32,640]{2,1,0:T(8,128)(2,1)}, u32[]{:S(2)}, u32[]{:S(2)}) async-start(bf16[8,32,640]{2,1,0:T(8,128)(2,1)} %user_weights.1), calls=%async_computation | async-start | bytes 655360 | tf_op jit(solution)/shard_map/all_to_all | solution.py:216
  19.2 0.0 all-gather.2.cloned.1.call-start
  19.2 0.7 broadcast_in_dim.34.gain_ref
  19.9 0.7 convert_element_type.43
  20.6 1.2 fusion.5
  21.9 1.0 copy-done.2
  22.9 0.1 last_rows.1
  23.6 0.7 broadcast_in_dim.16.gain_ref
  24.3 0.1 pad_add_fusion.scalar_ref
  24.4 1.2 fusion.7.normed_ref
  25.7 6.9 %all-to-all-done = bf16[8,32,640]{2,1,0:T(8,128)(2,1)} async-done(((bf16[8,32,640]{2,1,0:T(8,128)(2,1)}), bf16[8,32,640]{2,1,0:T(8,128)(2,1)}, u32[]{:S(2)}, u32[]{:S(2)}) %all-to-all-start) | async-done | bytes 327712 | tf_op jit(solution)/shard_map/all_to_all | solution.py:216
  32.6 0.0 all-gather.2.cloned.1.call-update
  32.6 9.7 %all_to_all.30.last_ref = f32[8,8,256]{2,1,0:T(8,128)S(1)} all-to-all(f32[8,8,256]{2,1,0:T(8,128)S(1)} %last_rows.1), channel_id=1, replica_groups=mesh['y'=8,'z'=8,'x'=4,'core'=2] {'x','core'}, dimensions={0} | all-to-all | bytes 131072 | tf_op jit(solution)/shard_map/all_to_all | solution.py:241
  42.3 1.3 item_probes.1
  43.6 8.5 %all_to_all.31.probes_ref = bf16[8,4,2048]{2,1,0:T(4,128)(2,1)S(1)} all-to-all(bf16[8,4,2048]{2,1,0:T(4,128)(2,1)S(1)} %get-tuple-element.24), channel_id=1, replica_groups=mesh['y'=8,'z'=8,'x'=4,'core'=2] {'x','core'}, dimensions={0} | all-to-all | bytes 262144 | tf_op jit(solution)/shard_map/all_to_all | solution.py:256
  52.1 0.7 item_attention.1
  52.9 8.5 %all_to_all.32 = bf16[8,4,2048]{2,1,0:T(4,128)(2,1)S(1)} all-to-all(bf16[8,4,2048]{2,1,0:T(4,128)(2,1)S(1)} %item_attention.1), channel_id=1, replica_groups=mesh['y'=8,'z'=8,'x'=4,'core'=2] {'x','core'}, dimensions={0} | all-to-all | bytes 262144 | tf_op jit(solution)/shard_map/all_to_all | solution.py:265
  61.4 0.3 convolution_convert_fusion.1
  61.8 0.1 reshape.41
  61.9 0.2 convolution_convert_fusion
  62.1 0.7 broadcast_in_dim.35
  62.8 3.4 %all-to-all-start.4 = ((bf16[8,8,2048]{2,1,0:T(8,128)(2,1)}), bf16[8,8,2048]{2,1,0:T(8,128)(2,1)S(1)}, u32[]{:S(2)}, u32[]{:S(2)}) async-start(bf16[8,8,2048]{2,1,0:T(8,128)(2,1)} %broadcast_in_dim.35), calls=%async_computation.4 | async-start | bytes 524288 | tf_op jit(solution)/shard_map/all_to_all | solution.py:33
  66.3 7.4 %all-to-all-done.4.terms_ref = bf16[8,8,2048]{2,1,0:T(8,128)(2,1)S(1)} async-done(((bf16[8,8,2048]{2,1,0:T(8,128)(2,1)}), bf16[8,8,2048]{2,1,0:T(8,128)(2,1)S(1)}, u32[]{:S(2)}, u32[]{:S(2)}) %all-to-all-start.4) | async-done | bytes 262176 | tf_op jit(solution)/shard_map/all_to_all | solution.py:33
  73.7 0.1 item_embeddings.1
  73.9 0.0 copy-start.5
  73.9 0.0 all-gather.2.cloned.1.call-done.weights_ref
  73.9 1.7 %fusion.2 = bf16[8,384]{1,0:T(8,128)(2,1)S(1)} fusion(bf16[8,2048]{1,0:T(8,128)(2,1)S(1)} %get-tuple-element.30, bf16[2048,640]{1,0:T(8,128)(2,1)} %all-gather.2.cloned.1.call-done.weights_ref), kind=kOutput, calls=%fused_computation.6 | convolution fusion | flops 12585984 | bytes 1611776 | tf_op jit(solution)/shard_map/dot_general | solution.py:280
  75.6 0.9 broadcast_in_dim.37
  76.5 10.6 %all-to-all-start.5 = ((bf16[64,8,640]{2,1,0:T(8,128)(2,1)}), bf16[64,8,640]{2,1,0:T(8,128)(2,1)S(1)}, u32[]{:S(2)}, u32[]{:S(2)}) async-start(bf16[64,8,640]{2,1,0:T(8,128)(2,1)} %broadcast_in_dim.37), calls=%async_computation.5 | async-start | bytes 1310720 | tf_op jit(solution)/shard_map/all_to_all | solution.py:33
  87.2 1.7 %copy-done.1 = bf16[2048,640]{1,0:T(8,128)(2,1)S(1)} copy-done((bf16[2048,640]{1,0:T(8,128)(2,1)S(1)}, bf16[2048,640]{1,0:T(8,128)(2,1)}, u32[]{:S(2)}) %copy-start.1) | copy-done | bytes 2621464
  88.9 1.4 %output_weights.1 = (bf16[4,256,256]{2,1,0:T(8,128)(2,1)}, bf16[4,256,256]{2,1,0:T(8,128)(2,1)S(1)}) custom-call(s32[3]{0:T(128)S(1)} %pad_add_fusion.scalar_ref, bf16[2048,640]{1,0:T(8,128)(2,1)S(1)} %copy-done.1), custom_call_target="tpu_custom_call" | custom-call | tf_op jit(solution)/shard_map/output_weights/pallas_call | solution.py:170
  90.4 1.9 %collective-permute-start.1 = (bf16[4,256,256]{2,1,0:T(8,128)(2,1)}, bf16[4,256,256]{2,1,0:T(8,128)(2,1)S(1)}, u32[]{:S(2)}, u32[]{:S(2)}) collective-permute-start(bf16[4,256,256]{2,1,0:T(8,128)(2,1)} %get-tuple-element.35), channel_id=1, source_target_pairs={{0,1},{1,0},{2,3},{3,2},{4,5},{5,4},{6,7},{7,6},{8,9},{9,8},{10,11... | collective-permute-start | bytes 1572872 | tf_op jit(solution)/shard_map/ppermute | solution.py:37
  92.3 0.1 copy.13.places_ref
  92.4 13.9 %all-to-all-done.5 = bf16[64,8,640]{2,1,0:T(8,128)(2,1)S(1)} async-done(((bf16[64,8,640]{2,1,0:T(8,128)(2,1)}), bf16[64,8,640]{2,1,0:T(8,128)(2,1)S(1)}, u32[]{:S(2)}, u32[]{:S(2)}) %all-to-all-start.5) | async-done | bytes 655392 | tf_op jit(solution)/shard_map/all_to_all | solution.py:33
  106.4 3.3 %user_attention.1 = (bf16[512,256]{1,0:T(8,128)(2,1)S(1)}, bf16[512,256]{1,0:T(8,128)(2,1)S(1)}) custom-call(s32[3]{0:T(128)S(1)} %pad_add_fusion.scalar_ref, s32[512,1]{1,0:T(8,128)S(1)} %copy.13.places_ref, bf16[512,640]{1,0:T(8,128)(2,1)S(1)} %bitcast.14), custom_call_target="tpu_custom_call" | custom-call | tf_op jit(solution)/shard_map/user_attention/pallas_call | solution.py:170
  109.7 1.9 %collective-permute-start = (bf16[512,256]{1,0:T(8,128)(2,1)S(1)}, bf16[512,256]{1,0:T(8,128)(2,1)S(1)}, u32[]{:S(2)}, u32[]{:S(2)}) collective-permute-start(bf16[512,256]{1,0:T(8,128)(2,1)S(1)} %get-tuple-element.33.mine_ref), channel_id=1, source_target_pairs={{0,1},{1,0},{2,3},{3,2},{4,5},{5,4},{6,7},{7,6},{8,9},{9,8},{10,11... | collective-permute-start | bytes 786440 | tf_op jit(solution)/shard_map/ppermute | solution.py:37
  111.6 1.5 %collective-permute-done.others_ref = bf16[512,256]{1,0:T(8,128)(2,1)S(1)} collective-permute-done((bf16[512,256]{1,0:T(8,128)(2,1)S(1)}, bf16[512,256]{1,0:T(8,128)(2,1)S(1)}, u32[]{:S(2)}, u32[]{:S(2)}) %collective-permute-start) | collective-permute-done | bytes 262176 | tf_op jit(solution)/shard_map/ppermute | solution.py:37
  113.1 0.7 output_blocks.1
  113.9 3.4 %collective-permute-start.3 = (bf16[512,256]{1,0:T(8,128)(2,1)S(1)}, bf16[512,256]{1,0:T(8,128)(2,1)S(1)}, u32[]{:S(2)}, u32[]{:S(2)}) collective-permute-start(bf16[512,256]{1,0:T(8,128)(2,1)S(1)} %get-tuple-element.38), channel_id=1, source_target_pairs={{0,2},{1,7},{2,4},{3,1},{4,6},{5,3},{6,0},{7,5},{8,10},{9,15},{10,... | collective-permute-start | bytes 786440 | tf_op jit(solution)/shard_map/ppermute | solution.py:47
  117.3 3.7 %collective-permute-start.2 = (bf16[512,256]{1,0:T(8,128)(2,1)S(1)}, bf16[512,256]{1,0:T(8,128)(2,1)S(1)}, u32[]{:S(2)}, u32[]{:S(2)}) collective-permute-start(bf16[512,256]{1,0:T(8,128)(2,1)S(1)} %get-tuple-element.37), channel_id=1, source_target_pairs={{0,6},{1,3},{2,0},{3,5},{4,2},{5,7},{6,4},{7,1},{8,14},{9,11},{10,... | collective-permute-start | bytes 786440 | tf_op jit(solution)/shard_map/ppermute | solution.py:47
  121.0 2.4 %collective-permute-done.3 = bf16[512,256]{1,0:T(8,128)(2,1)S(1)} collective-permute-done((bf16[512,256]{1,0:T(8,128)(2,1)S(1)}, bf16[512,256]{1,0:T(8,128)(2,1)S(1)}, u32[]{:S(2)}, u32[]{:S(2)}) %collective-permute-start.3) | collective-permute-done | bytes 262176 | tf_op jit(solution)/shard_map/ppermute | solution.py:47
  123.4 0.1 add_convert_fusion
  123.4 2.6 %collective-permute-start.4 = (bf16[512,256]{1,0:T(8,128)(2,1)S(1)}, bf16[512,256]{1,0:T(8,128)(2,1)S(1)}, u32[]{:S(2)}, u32[]{:S(2)}) collective-permute-start(bf16[512,256]{1,0:T(8,128)(2,1)S(1)} %add_convert_fusion), channel_id=1, source_target_pairs={{0,2},{1,7},{2,4},{3,1},{4,6},{5,3},{6,0},{7,5},{8,10},{9,15},{10,... | collective-permute-start | bytes 786440 | tf_op jit(solution)/shard_map/ppermute | solution.py:47
  126.0 0.0 collective-permute-done.2
  126.1 6.9 %collective-permute-done.4 = bf16[512,256]{1,0:T(8,128)(2,1)S(1)} collective-permute-done((bf16[512,256]{1,0:T(8,128)(2,1)S(1)}, bf16[512,256]{1,0:T(8,128)(2,1)S(1)}, u32[]{:S(2)}, u32[]{:S(2)}) %collective-permute-start.4) | collective-permute-done | bytes 262176 | tf_op jit(solution)/shard_map/ppermute | solution.py:47
  132.9 0.9 select_convert_fusion
  (16 shorter events, 0.1 us)
Async XLA Ops:
  7.2 54.7 %copy-start = (bf16[256,2048]{1,0:T(8,128)(2,1)S(1)}, bf16[256,2048]{1,0:T(8,128)(2,1)}, u32[]{:S(2)}) copy-start(bf16[256,2048]{1,0:T(8,128)(2,1)} %param.15) | copy-start | bytes 3145732
  7.2 35.2 %copy-start.3 = (bf16[2048,1,128]{2,0,1:T(8,128)(2,1)S(1)}, bf16[2048,1,128]{2,0,1:T(8,128)(2,1)}, u32[]{:S(2)}) copy-start(bf16[2048,1,128]{2,0,1:T(8,128)(2,1)} %param.14) | copy-start | bytes 1572868
  7.2 35.1 %copy-start.4 = (bf16[2048,256]{1,0:T(8,128)(2,1)S(1)}, bf16[2048,256]{1,0:T(8,128)(2,1)}, u32[]{:S(2)}) copy-start(bf16[2048,256]{1,0:T(8,128)(2,1)} %wq_ref.3) | copy-start | bytes 3145732
  8.9 23.7 %all-to-all-start = ((bf16[8,32,640]{2,1,0:T(8,128)(2,1)}), bf16[8,32,640]{2,1,0:T(8,128)(2,1)}, u32[]{:S(2)}, u32[]{:S(2)}) async-start(bf16[8,32,640]{2,1,0:T(8,128)(2,1)} %user_weights.1), calls=%async_computation | async-start | bytes 655360 | tf_op jit(solution)/shard_map/all_to_all | solution.py:216
  19.2 54.7 %all-gather.2.cloned.1.call-start = ((), (), s32[]{:S(2)}) async-start(), calls=%async_computation.6 | async-start | bytes 2949120 | tf_op jit(solution)/shard_map/all_gather | solution.py:240
  21.9 1.0 copy-start.2
  62.8 10.9 %all-to-all-start.4 = ((bf16[8,8,2048]{2,1,0:T(8,128)(2,1)}), bf16[8,8,2048]{2,1,0:T(8,128)(2,1)S(1)}, u32[]{:S(2)}, u32[]{:S(2)}) async-start(bf16[8,8,2048]{2,1,0:T(8,128)(2,1)} %broadcast_in_dim.35), calls=%async_computation.4 | async-start | bytes 524288 | tf_op jit(solution)/shard_map/all_to_all | solution.py:33
  73.9 16.5 %copy-start.5 = (bf16[8,256]{1,0:T(8,128)(2,1)}, bf16[8,256]{1,0:T(8,128)(2,1)S(1)}, u32[]{:S(2)}) copy-start(bf16[8,256]{1,0:T(8,128)(2,1)S(1)} %constant_dynamic-slice_fusion) | copy-start | bytes 12292
  75.6 16.6 %copy-start.6 = (s32[1,512]{1,0:T(1,128)S(1)}, s32[1,512]{1,0:T(1,128)}, u32[]{:S(2)}) copy-start(s32[1,512]{1,0:T(1,128)} %param.20) | copy-start | bytes 6148
  76.5 29.8 %all-to-all-start.5 = ((bf16[64,8,640]{2,1,0:T(8,128)(2,1)}), bf16[64,8,640]{2,1,0:T(8,128)(2,1)S(1)}, u32[]{:S(2)}, u32[]{:S(2)}) async-start(bf16[64,8,640]{2,1,0:T(8,128)(2,1)} %broadcast_in_dim.37), calls=%async_computation.5 | async-start | bytes 1310720 | tf_op jit(solution)/shard_map/all_to_all | solution.py:33
  87.2 1.7 %copy-start.1 = (bf16[2048,640]{1,0:T(8,128)(2,1)S(1)}, bf16[2048,640]{1,0:T(8,128)(2,1)}, u32[]{:S(2)}) copy-start(bf16[2048,640]{1,0:T(8,128)(2,1)} %all-gather.2.cloned.1.call-done.weights_ref) | copy-start | bytes 7864324
  90.4 21.3 %collective-permute-start.1 = (bf16[4,256,256]{2,1,0:T(8,128)(2,1)}, bf16[4,256,256]{2,1,0:T(8,128)(2,1)S(1)}, u32[]{:S(2)}, u32[]{:S(2)}) collective-permute-start(bf16[4,256,256]{2,1,0:T(8,128)(2,1)} %get-tuple-element.35), channel_id=1, source_target_pairs={{0,1},{1,0},{2,3},{3,2},{4,5},{5,4},{6,7},{7,6},{8,9},{9,8},{10,11... | collective-permute-start | bytes 1572872 | tf_op jit(solution)/shard_map/ppermute | solution.py:37
  109.7 3.4 %collective-permute-start = (bf16[512,256]{1,0:T(8,128)(2,1)S(1)}, bf16[512,256]{1,0:T(8,128)(2,1)S(1)}, u32[]{:S(2)}, u32[]{:S(2)}) collective-permute-start(bf16[512,256]{1,0:T(8,128)(2,1)S(1)} %get-tuple-element.33.mine_ref), channel_id=1, source_target_pairs={{0,1},{1,0},{2,3},{3,2},{4,5},{5,4},{6,7},{7,6},{8,9},{9,8},{10,11... | collective-permute-start | bytes 786440 | tf_op jit(solution)/shard_map/ppermute | solution.py:37
  113.9 9.5 %collective-permute-start.3 = (bf16[512,256]{1,0:T(8,128)(2,1)S(1)}, bf16[512,256]{1,0:T(8,128)(2,1)S(1)}, u32[]{:S(2)}, u32[]{:S(2)}) collective-permute-start(bf16[512,256]{1,0:T(8,128)(2,1)S(1)} %get-tuple-element.38), channel_id=1, source_target_pairs={{0,2},{1,7},{2,4},{3,1},{4,6},{5,3},{6,0},{7,5},{8,10},{9,15},{10,... | collective-permute-start | bytes 786440 | tf_op jit(solution)/shard_map/ppermute | solution.py:47
  117.3 8.8 %collective-permute-start.2 = (bf16[512,256]{1,0:T(8,128)(2,1)S(1)}, bf16[512,256]{1,0:T(8,128)(2,1)S(1)}, u32[]{:S(2)}, u32[]{:S(2)}) collective-permute-start(bf16[512,256]{1,0:T(8,128)(2,1)S(1)} %get-tuple-element.37), channel_id=1, source_target_pairs={{0,6},{1,3},{2,0},{3,5},{4,2},{5,7},{6,4},{7,1},{8,14},{9,11},{10,... | collective-permute-start | bytes 786440 | tf_op jit(solution)/shard_map/ppermute | solution.py:47
  123.4 9.5 %collective-permute-start.4 = (bf16[512,256]{1,0:T(8,128)(2,1)S(1)}, bf16[512,256]{1,0:T(8,128)(2,1)S(1)}, u32[]{:S(2)}, u32[]{:S(2)}) collective-permute-start(bf16[512,256]{1,0:T(8,128)(2,1)S(1)} %add_convert_fusion), channel_id=1, source_target_pairs={{0,2},{1,7},{2,4},{3,1},{4,6},{5,3},{6,0},{7,5},{8,10},{9,15},{10,... | collective-permute-start | bytes 786440 | tf_op jit(solution)/shard_map/ppermute | solution.py:47
Sparse Core Ops, SparseCore 0:
  32.7 40.2 all-gather.1

commit v7 on v6

--- a/solution.py
+++ b/solution.py
@@ -125,7 +125,7 @@
 
 
 def user_kernel(
-    scalar_ref, places_ref, catalog_ref, mixed_ref, residual_ref, picked_ref
+    scalar_ref, places_ref, catalog_ref, mixed_ref, residual_ref, query_ref, key_ref, value_ref
 ):
     length = scalar_ref[0]
     slots, q_width = mixed_ref.shape
@@ -133,32 +133,41 @@
     every = lax.broadcasted_iota(jnp.int32, (slots, catalog), 1)
     picks = jnp.where(places_ref[...] == every, 1.0, 0.0).astype(jnp.bfloat16)
     picked = jnp.dot(picks, catalog_ref[...], preferred_element_type=jnp.float32)
-    picked_ref[...] = picked[:, :kv_at].astype(jnp.bfloat16)
+    scale = 1.0 / math.sqrt(HEAD_DIM)
+    query_ref[...] = (picked[:, :q_width] * scale).astype(jnp.bfloat16)
+    key_ref[...] = picked[:, q_width : q_width + HEAD_DIM].astype(jnp.bfloat16)
+    values = picked[:, q_width + HEAD_DIM : kv_at]
+    value_ref[...] = jnp.concatenate([values, jnp.ones_like(values)], axis=1).astype(jnp.bfloat16)
     residual_ref[...] = picked[:, kv_at:].astype(jnp.bfloat16)
-    scale = 1.0 / math.sqrt(HEAD_DIM)
     chunk = min(slots, 256)
     for start in range(0, slots, chunk):
         upto = start + chunk
-        keys = picked_ref[:upto, q_width : q_width + HEAD_DIM]
-        values = picked_ref[:upto, q_width + HEAD_DIM : kv_at]
         row = start + lax.broadcasted_iota(jnp.int32, (chunk, upto), 0)
         column = lax.broadcasted_iota(jnp.int32, (chunk, upto), 1)
         allowed = (column <= row) & (column < length)
         for head in range(q_width // HEAD_DIM):
             lanes = slice(head * HEAD_DIM, (head + 1) * HEAD_DIM)
-            scores = dot_t(picked_ref[start:upto, lanes], keys) * scale
+            scores = dot_t(query_ref[start:upto, lanes], key_ref[:upto, :])
             scores = jnp.where(allowed, scores, -1e30)
-            top = jnp.max(scores, axis=1, keepdims=True)
-            parts = jnp.exp(scores - top)
-            total = jnp.sum(parts, axis=1, keepdims=True)
-            mixed = jnp.dot(parts.astype(jnp.bfloat16), values, preferred_element_type=jnp.float32)
-            mixed_ref[start:upto, lanes] = (mixed / total).astype(jnp.bfloat16)
+            parts = jnp.exp(scores - jnp.max(scores, axis=1, keepdims=True))
+            mixed = jnp.dot(
+                parts.astype(jnp.bfloat16), value_ref[:upto, :], preferred_element_type=jnp.float32
+            )
+            mixed = mixed[:, :HEAD_DIM] / mixed[:, HEAD_DIM:]
+            mixed_ref[start:upto, lanes] = mixed.astype(jnp.bfloat16)
 
 
 def output_kernel(mine_ref, others_ref, wo_mine_ref, wo_others_ref, *block_refs):
+    skip = wo_mine_ref.shape[0] - len(block_refs)
     for k, ref in enumerate(block_refs):
-        terms = dot_t(mine_ref[...], wo_mine_ref[k]) + dot_t(others_ref[...], wo_others_ref[k])
+        terms = dot_t(mine_ref[...], wo_mine_ref[skip + k])
+        terms += dot_t(others_ref[...], wo_others_ref[skip + k])
         ref[...] = terms.astype(jnp.bfloat16)
+
+
+def first_output_kernel(mine_ref, others_ref, wo_mine_ref, wo_others_ref, block_ref):
+    terms = dot_t(mine_ref[...], wo_mine_ref[0]) + dot_t(others_ref[...], wo_others_ref[0])
+    block_ref[...] = terms.astype(jnp.bfloat16)
 
 
 SMEM = pl.BlockSpec(memory_space=pltpu.SMEM)
@@ -304,24 +313,27 @@
         ),
         [SMEM] + [VMEM] * 2,
         (scalars, places, catalog),
-        [pltpu.VMEM((slots, kv_at), jnp.bfloat16)],
-    )
-
-    first, direct, second, own = call(
-        output_kernel,
-        "output_blocks",
-        20,
-        [jax.ShapeDtypeStruct((slots, share), jnp.bfloat16)] * n_x,
-        [VMEM] * 4,
-        (user_mixed, swap_cores(user_mixed), wo_mine, wo_others),
+        [
+            pltpu.VMEM((slots, heads_width), jnp.bfloat16),
+            pltpu.VMEM((slots, HEAD_DIM), jnp.bfloat16),
+            pltpu.VMEM((slots, 2 * HEAD_DIM), jnp.bfloat16),
+        ],
+    )
+
+    block = jax.ShapeDtypeStruct((slots, share), jnp.bfloat16)
+    operands = (user_mixed, swap_cores(user_mixed), wo_mine, wo_others)
+    first = call(first_output_kernel, "output_first", 20, block, [VMEM] * 4, operands)
+    direct, second, own = call(
+        output_kernel, "output_blocks", 20, [block] * (n_x - 1), [VMEM] * 4, operands
     )
     relay = along_x(first, 1)
     direct = along_x(direct, -1)
     relay = (relay.astype(jnp.float32) + second.astype(jnp.float32)).astype(jnp.bfloat16)
     relay = along_x(relay, 1)
-    summed = own.astype(jnp.float32) + direct.astype(jnp.float32) + relay.astype(jnp.float32)
     live = (jnp.arange(slots, dtype=jnp.int32) < length)[:, None]
-    user_states = jnp.where(live, residual.astype(jnp.float32) + summed, 0.0).astype(jnp.bfloat16)
+    summed = residual.astype(jnp.float32) + own.astype(jnp.float32) + direct.astype(jnp.float32)
+    summed = lax.optimization_barrier(summed) + relay.astype(jnp.float32)
+    user_states = jnp.where(live, summed, 0.0).astype(jnp.bfloat16)
     return (item_part, user_states)
 
 

time: 142 us -> 141 us (level)
    pallas_call x8 -> x9, Pallas kernels: 9.35 us -> 9.51 us  [call(): pl.pallas_call(kernel, name=name, out_shape=outs, in_specs=in_specs, out_...]
  transfers between devices with their start and end apart: 9 -> 9, of which waited for: 6 -> 7; matrix products, arithmetic and copies ran while one was open for 4% -> 5% of each run, Pallas kernels for 5% -> 5%
where the time goes in v7:
time: 141 us; the launch traced here: 140 us
  waiting for transfers between devices  38.8 us (28%)
  starting transfers between devices  37.5 us (27%)
  blocking collectives  26.8 us (19%)
  between operations  14.9 us (11%)
  Pallas kernels  9.51 us (7%)
  local copies, waits for them, and re-layouts  6.09 us (4%)
  other arithmetic  4.24 us (3%)
  matrix products  2.3 us (2%)
    all_to_all x2, waiting for transfers between devices, spread(): return lax.all_to_all(copies, axis, 0, 0)  21.4 us
    all_to_all x2, starting transfers between devices, spread(): return lax.all_to_all(copies, axis, 0, 0)  14.1 us
    all_to_all x1, starting transfers between devices, local(): weights_z = lax.all_to_all(copies, 'z', 0, 0).reshape(n_z * depth, columns)  10.3 us
    all_to_all x1, blocking collectives, local(): last_raw = lax.all_to_all(messages, NARROW, 0, 0)  9.72 us
    pallas_call x9, Pallas kernels, call(): pl.pallas_call(kernel, name=name, out_shape=outs, in_specs=in_specs, out_...  9.51 us
    ppermute x3, starting transfers between devices, along_x(): return lax.ppermute(values, NARROW, pairs)  9.23 us
    ppermute x3, waiting for transfers between devices, along_x(): return lax.ppermute(values, NARROW, pairs)  8.98 us
    all_to_all x1, blocking collectives, local(): probes = lax.all_to_all(probes, NARROW, 0, 0)  8.52 us
  transfers between devices with their start and end apart: 9, of which 7 were waited for; matrix products, arithmetic and copies ran while one was open for 5% of the time, Pallas kernels for 5%

profile of v7, /device:TPU:16, one launch (start us, length us, event | category | flops | bytes accessed | tf_op | source)
XLA Modules:
  0.0 140.1 jit_solution(18383269295167150218)
XLA Ops:
  7.2 1.7 %user_weights.1 = bf16[8,32,640]{2,1,0:T(8,128)(2,1)} custom-call(bf16[32,256]{1,0:T(8,128)(2,1)} %wq_ref.2, bf16[32,128]{1,0:T(8,128)(2,1)} %bitcast.18, bf16[32,256]{1,0:T(8,128)(2,1)} %bitcast.17), custom_call_target="tpu_custom_call" | custom-call | tf_op jit(solution)/shard_map/user_weights/pallas_call | solution.py:179
  8.9 10.3 %all-to-all-start = ((bf16[8,32,640]{2,1,0:T(8,128)(2,1)}), bf16[8,32,640]{2,1,0:T(8,128)(2,1)}, u32[]{:S(2)}, u32[]{:S(2)}) async-start(bf16[8,32,640]{2,1,0:T(8,128)(2,1)} %user_weights.1), calls=%async_computation | async-start | bytes 655360 | tf_op jit(solution)/shard_map/all_to_all | solution.py:225
  19.2 0.0 all-gather.2.cloned.1.call-start
  19.2 0.7 broadcast_in_dim.34.gain_ref
  19.9 0.7 convert_element_type.43
  20.6 1.2 fusion.5
  21.9 1.0 copy-done.2
  22.9 0.1 last_rows.1
  23.6 0.7 broadcast_in_dim.16.gain_ref
  24.3 0.1 pad_add_fusion.scalar_ref
  24.4 1.2 fusion.7.normed_ref
  25.7 6.9 %all-to-all-done = bf16[8,32,640]{2,1,0:T(8,128)(2,1)} async-done(((bf16[8,32,640]{2,1,0:T(8,128)(2,1)}), bf16[8,32,640]{2,1,0:T(8,128)(2,1)}, u32[]{:S(2)}, u32[]{:S(2)}) %all-to-all-start) | async-done | bytes 327712 | tf_op jit(solution)/shard_map/all_to_all | solution.py:225
  32.6 0.0 all-gather.2.cloned.1.call-update
  32.6 9.7 %all_to_all.30.last_ref = f32[8,8,256]{2,1,0:T(8,128)S(1)} all-to-all(f32[8,8,256]{2,1,0:T(8,128)S(1)} %last_rows.1), channel_id=1, replica_groups=mesh['y'=8,'z'=8,'x'=4,'core'=2] {'x','core'}, dimensions={0} | all-to-all | bytes 131072 | tf_op jit(solution)/shard_map/all_to_all | solution.py:250
  42.3 1.3 item_probes.1
  43.6 8.5 %all_to_all.31.probes_ref = bf16[8,4,2048]{2,1,0:T(4,128)(2,1)S(1)} all-to-all(bf16[8,4,2048]{2,1,0:T(4,128)(2,1)S(1)} %get-tuple-element.23), channel_id=1, replica_groups=mesh['y'=8,'z'=8,'x'=4,'core'=2] {'x','core'}, dimensions={0} | all-to-all | bytes 262144 | tf_op jit(solution)/shard_map/all_to_all | solution.py:265
  52.1 0.7 item_attention.1
  52.9 8.5 %all_to_all.32 = bf16[8,4,2048]{2,1,0:T(4,128)(2,1)S(1)} all-to-all(bf16[8,4,2048]{2,1,0:T(4,128)(2,1)S(1)} %item_attention.1), channel_id=1, replica_groups=mesh['y'=8,'z'=8,'x'=4,'core'=2] {'x','core'}, dimensions={0} | all-to-all | bytes 262144 | tf_op jit(solution)/shard_map/all_to_all | solution.py:274
  61.4 0.3 convolution_convert_fusion.1
  61.8 0.1 reshape.41
  61.9 0.2 convolution_convert_fusion
  62.1 0.7 broadcast_in_dim.35
  62.8 3.4 %all-to-all-start.4 = ((bf16[8,8,2048]{2,1,0:T(8,128)(2,1)}), bf16[8,8,2048]{2,1,0:T(8,128)(2,1)S(1)}, u32[]{:S(2)}, u32[]{:S(2)}) async-start(bf16[8,8,2048]{2,1,0:T(8,128)(2,1)} %broadcast_in_dim.35), calls=%async_computation.4 | async-start | bytes 524288 | tf_op jit(solution)/shard_map/all_to_all | solution.py:33
  66.3 7.4 %all-to-all-done.4.terms_ref = bf16[8,8,2048]{2,1,0:T(8,128)(2,1)S(1)} async-done(((bf16[8,8,2048]{2,1,0:T(8,128)(2,1)}), bf16[8,8,2048]{2,1,0:T(8,128)(2,1)S(1)}, u32[]{:S(2)}, u32[]{:S(2)}) %all-to-all-start.4) | async-done | bytes 262176 | tf_op jit(solution)/shard_map/all_to_all | solution.py:33
  73.7 0.1 item_embeddings.1
  73.9 0.0 all-gather.2.cloned.1.call-done.weights_ref
  73.9 1.7 %fusion.2 = bf16[8,384]{1,0:T(8,128)(2,1)S(1)} fusion(bf16[8,2048]{1,0:T(8,128)(2,1)S(1)} %get-tuple-element.29, bf16[2048,640]{1,0:T(8,128)(2,1)} %all-gather.2.cloned.1.call-done.weights_ref), kind=kOutput, calls=%fused_computation.6 | convolution fusion | flops 12585984 | bytes 1611776 | tf_op jit(solution)/shard_map/dot_general | solution.py:289
  75.6 0.9 broadcast_in_dim.37
  76.5 10.6 %all-to-all-start.5 = ((bf16[64,8,640]{2,1,0:T(8,128)(2,1)}), bf16[64,8,640]{2,1,0:T(8,128)(2,1)S(1)}, u32[]{:S(2)}, u32[]{:S(2)}) async-start(bf16[64,8,640]{2,1,0:T(8,128)(2,1)} %broadcast_in_dim.37), calls=%async_computation.5 | async-start | bytes 1310720 | tf_op jit(solution)/shard_map/all_to_all | solution.py:33
  87.2 1.7 %copy-done.1 = bf16[2048,640]{1,0:T(8,128)(2,1)S(1)} copy-done((bf16[2048,640]{1,0:T(8,128)(2,1)S(1)}, bf16[2048,640]{1,0:T(8,128)(2,1)}, u32[]{:S(2)}) %copy-start.1) | copy-done | bytes 2621464
  88.9 1.4 %output_weights.1 = (bf16[4,256,256]{2,1,0:T(8,128)(2,1)}, bf16[4,256,256]{2,1,0:T(8,128)(2,1)S(1)}) custom-call(s32[3]{0:T(128)S(1)} %pad_add_fusion.scalar_ref, bf16[2048,640]{1,0:T(8,128)(2,1)S(1)} %copy-done.1), custom_call_target="tpu_custom_call" | custom-call | tf_op jit(solution)/shard_map/output_weights/pallas_call | solution.py:179
  90.4 1.9 %collective-permute-start.1 = (bf16[4,256,256]{2,1,0:T(8,128)(2,1)}, bf16[4,256,256]{2,1,0:T(8,128)(2,1)S(1)}, u32[]{:S(2)}, u32[]{:S(2)}) collective-permute-start(bf16[4,256,256]{2,1,0:T(8,128)(2,1)} %get-tuple-element.34), channel_id=1, source_target_pairs={{0,1},{1,0},{2,3},{3,2},{4,5},{5,4},{6,7},{7,6},{8,9},{9,8},{10,11... | collective-permute-start | bytes 1572872 | tf_op jit(solution)/shard_map/ppermute | solution.py:37
  92.3 0.1 copy.13.places_ref
  92.4 13.9 %all-to-all-done.5 = bf16[64,8,640]{2,1,0:T(8,128)(2,1)S(1)} async-done(((bf16[64,8,640]{2,1,0:T(8,128)(2,1)}), bf16[64,8,640]{2,1,0:T(8,128)(2,1)S(1)}, u32[]{:S(2)}, u32[]{:S(2)}) %all-to-all-start.5) | async-done | bytes 655392 | tf_op jit(solution)/shard_map/all_to_all | solution.py:33
  106.4 3.3 %user_attention.1 = (bf16[512,256]{1,0:T(8,128)(2,1)S(1)}, bf16[512,256]{1,0:T(8,128)(2,1)S(1)}) custom-call(s32[3]{0:T(128)S(1)} %pad_add_fusion.scalar_ref, s32[512,1]{1,0:T(8,128)S(1)} %copy.13.places_ref, bf16[512,640]{1,0:T(8,128)(2,1)S(1)} %bitcast.14), custom_call_target="tpu_custom_call" | custom-call | tf_op jit(solution)/shard_map/user_attention/pallas_call | solution.py:179
  109.7 1.9 %collective-permute-start = (bf16[512,256]{1,0:T(8,128)(2,1)S(1)}, bf16[512,256]{1,0:T(8,128)(2,1)S(1)}, u32[]{:S(2)}, u32[]{:S(2)}) collective-permute-start(bf16[512,256]{1,0:T(8,128)(2,1)S(1)} %get-tuple-element.32.mine_ref), channel_id=1, source_target_pairs={{0,1},{1,0},{2,3},{3,2},{4,5},{5,4},{6,7},{7,6},{8,9},{9,8},{10,11... | collective-permute-start | bytes 786440 | tf_op jit(solution)/shard_map/ppermute | solution.py:37
  111.6 1.5 %collective-permute-done.others_ref = bf16[512,256]{1,0:T(8,128)(2,1)S(1)} collective-permute-done((bf16[512,256]{1,0:T(8,128)(2,1)S(1)}, bf16[512,256]{1,0:T(8,128)(2,1)S(1)}, u32[]{:S(2)}, u32[]{:S(2)}) %collective-permute-start) | collective-permute-done | bytes 262176 | tf_op jit(solution)/shard_map/ppermute | solution.py:37
  113.1 0.3 output_first.1
  113.4 3.4 %collective-permute-start.3 = (bf16[512,256]{1,0:T(8,128)(2,1)S(1)}, bf16[512,256]{1,0:T(8,128)(2,1)S(1)}, u32[]{:S(2)}, u32[]{:S(2)}) collective-permute-start(bf16[512,256]{1,0:T(8,128)(2,1)S(1)} %output_first.1), channel_id=1, source_target_pairs={{0,2},{1,7},{2,4},{3,1},{4,6},{5,3},{6,0},{7,5},{8,10},{9,15},{10,... | collective-permute-start | bytes 786440 | tf_op jit(solution)/shard_map/ppermute | solution.py:47
  116.8 0.6 output_blocks.1
  117.4 3.7 %collective-permute-start.2 = (bf16[512,256]{1,0:T(8,128)(2,1)S(1)}, bf16[512,256]{1,0:T(8,128)(2,1)S(1)}, u32[]{:S(2)}, u32[]{:S(2)}) collective-permute-start(bf16[512,256]{1,0:T(8,128)(2,1)S(1)} %get-tuple-element.36), channel_id=1, source_target_pairs={{0,6},{1,3},{2,0},{3,5},{4,2},{5,7},{6,4},{7,1},{8,14},{9,11},{10,... | collective-permute-start | bytes 786440 | tf_op jit(solution)/shard_map/ppermute | solution.py:47
  121.1 1.8 %collective-permute-done.3 = bf16[512,256]{1,0:T(8,128)(2,1)S(1)} collective-permute-done((bf16[512,256]{1,0:T(8,128)(2,1)S(1)}, bf16[512,256]{1,0:T(8,128)(2,1)S(1)}, u32[]{:S(2)}, u32[]{:S(2)}) %collective-permute-start.3) | collective-permute-done | bytes 262176 | tf_op jit(solution)/shard_map/ppermute | solution.py:47
  122.9 0.1 add_convert_fusion
  123.0 2.2 %collective-permute-start.4 = (bf16[512,256]{1,0:T(8,128)(2,1)S(1)}, bf16[512,256]{1,0:T(8,128)(2,1)S(1)}, u32[]{:S(2)}, u32[]{:S(2)}) collective-permute-start(bf16[512,256]{1,0:T(8,128)(2,1)S(1)} %add_convert_fusion), channel_id=1, source_target_pairs={{0,2},{1,7},{2,4},{3,1},{4,6},{5,3},{6,0},{7,5},{8,10},{9,15},{10,... | collective-permute-start | bytes 786440 | tf_op jit(solution)/shard_map/ppermute | solution.py:47
  125.2 0.5 collective-permute-done.2
  125.7 0.1 convert_add_fusion
  125.8 6.7 %collective-permute-done.4 = bf16[512,256]{1,0:T(8,128)(2,1)S(1)} collective-permute-done((bf16[512,256]{1,0:T(8,128)(2,1)S(1)}, bf16[512,256]{1,0:T(8,128)(2,1)S(1)}, u32[]{:S(2)}, u32[]{:S(2)}) %collective-permute-start.4) | collective-permute-done | bytes 262176 | tf_op jit(solution)/shard_map/ppermute | solution.py:47
  132.4 0.8 select_convert_fusion
  (18 shorter events, 0.1 us)
Async XLA Ops:
  7.2 54.7 %copy-start = (bf16[256,2048]{1,0:T(8,128)(2,1)S(1)}, bf16[256,2048]{1,0:T(8,128)(2,1)}, u32[]{:S(2)}) copy-start(bf16[256,2048]{1,0:T(8,128)(2,1)} %param.15) | copy-start | bytes 3145732
  7.2 35.2 %copy-start.3 = (bf16[2048,1,128]{2,0,1:T(8,128)(2,1)S(1)}, bf16[2048,1,128]{2,0,1:T(8,128)(2,1)}, u32[]{:S(2)}) copy-start(bf16[2048,1,128]{2,0,1:T(8,128)(2,1)} %param.14) | copy-start | bytes 1572868
  7.2 35.1 %copy-start.4 = (bf16[2048,256]{1,0:T(8,128)(2,1)S(1)}, bf16[2048,256]{1,0:T(8,128)(2,1)}, u32[]{:S(2)}) copy-start(bf16[2048,256]{1,0:T(8,128)(2,1)} %wq_ref.3) | copy-start | bytes 3145732
  8.9 23.7 %all-to-all-start = ((bf16[8,32,640]{2,1,0:T(8,128)(2,1)}), bf16[8,32,640]{2,1,0:T(8,128)(2,1)}, u32[]{:S(2)}, u32[]{:S(2)}) async-start(bf16[8,32,640]{2,1,0:T(8,128)(2,1)} %user_weights.1), calls=%async_computation | async-start | bytes 655360 | tf_op jit(solution)/shard_map/all_to_all | solution.py:225
  19.2 54.7 %all-gather.2.cloned.1.call-start = ((), (), s32[]{:S(2)}) async-start(), calls=%async_computation.6 | async-start | bytes 2949120 | tf_op jit(solution)/shard_map/all_gather | solution.py:249
  21.9 1.0 copy-start.2
  62.8 10.9 %all-to-all-start.4 = ((bf16[8,8,2048]{2,1,0:T(8,128)(2,1)}), bf16[8,8,2048]{2,1,0:T(8,128)(2,1)S(1)}, u32[]{:S(2)}, u32[]{:S(2)}) async-start(bf16[8,8,2048]{2,1,0:T(8,128)(2,1)} %broadcast_in_dim.35), calls=%async_computation.4 | async-start | bytes 524288 | tf_op jit(solution)/shard_map/all_to_all | solution.py:33
  73.9 16.5 %copy-start.5 = (bf16[8,256]{1,0:T(8,128)(2,1)}, bf16[8,256]{1,0:T(8,128)(2,1)S(1)}, u32[]{:S(2)}) copy-start(bf16[8,256]{1,0:T(8,128)(2,1)S(1)} %constant_dynamic-slice_fusion) | copy-start | bytes 12292
  75.6 16.6 %copy-start.6 = (s32[1,512]{1,0:T(1,128)S(1)}, s32[1,512]{1,0:T(1,128)}, u32[]{:S(2)}) copy-start(s32[1,512]{1,0:T(1,128)} %param.20) | copy-start | bytes 6148
  76.5 29.8 %all-to-all-start.5 = ((bf16[64,8,640]{2,1,0:T(8,128)(2,1)}), bf16[64,8,640]{2,1,0:T(8,128)(2,1)S(1)}, u32[]{:S(2)}, u32[]{:S(2)}) async-start(bf16[64,8,640]{2,1,0:T(8,128)(2,1)} %broadcast_in_dim.37), calls=%async_computation.5 | async-start | bytes 1310720 | tf_op jit(solution)/shard_map/all_to_all | solution.py:33
  87.2 1.7 %copy-start.1 = (bf16[2048,640]{1,0:T(8,128)(2,1)S(1)}, bf16[2048,640]{1,0:T(8,128)(2,1)}, u32[]{:S(2)}) copy-start(bf16[2048,640]{1,0:T(8,128)(2,1)} %all-gather.2.cloned.1.call-done.weights_ref) | copy-start | bytes 7864324
  90.4 21.2 %collective-permute-start.1 = (bf16[4,256,256]{2,1,0:T(8,128)(2,1)}, bf16[4,256,256]{2,1,0:T(8,128)(2,1)S(1)}, u32[]{:S(2)}, u32[]{:S(2)}) collective-permute-start(bf16[4,256,256]{2,1,0:T(8,128)(2,1)} %get-tuple-element.34), channel_id=1, source_target_pairs={{0,1},{1,0},{2,3},{3,2},{4,5},{5,4},{6,7},{7,6},{8,9},{9,8},{10,11... | collective-permute-start | bytes 1572872 | tf_op jit(solution)/shard_map/ppermute | solution.py:37
  109.7 3.4 %collective-permute-start = (bf16[512,256]{1,0:T(8,128)(2,1)S(1)}, bf16[512,256]{1,0:T(8,128)(2,1)S(1)}, u32[]{:S(2)}, u32[]{:S(2)}) collective-permute-start(bf16[512,256]{1,0:T(8,128)(2,1)S(1)} %get-tuple-element.32.mine_ref), channel_id=1, source_target_pairs={{0,1},{1,0},{2,3},{3,2},{4,5},{5,4},{6,7},{7,6},{8,9},{9,8},{10,11... | collective-permute-start | bytes 786440 | tf_op jit(solution)/shard_map/ppermute | solution.py:37
  113.4 9.5 %collective-permute-start.3 = (bf16[512,256]{1,0:T(8,128)(2,1)S(1)}, bf16[512,256]{1,0:T(8,128)(2,1)S(1)}, u32[]{:S(2)}, u32[]{:S(2)}) collective-permute-start(bf16[512,256]{1,0:T(8,128)(2,1)S(1)} %output_first.1), channel_id=1, source_target_pairs={{0,2},{1,7},{2,4},{3,1},{4,6},{5,3},{6,0},{7,5},{8,10},{9,15},{10,... | collective-permute-start | bytes 786440 | tf_op jit(solution)/shard_map/ppermute | solution.py:47
  117.4 8.3 %collective-permute-start.2 = (bf16[512,256]{1,0:T(8,128)(2,1)S(1)}, bf16[512,256]{1,0:T(8,128)(2,1)S(1)}, u32[]{:S(2)}, u32[]{:S(2)}) collective-permute-start(bf16[512,256]{1,0:T(8,128)(2,1)S(1)} %get-tuple-element.36), channel_id=1, source_target_pairs={{0,6},{1,3},{2,0},{3,5},{4,2},{5,7},{6,4},{7,1},{8,14},{9,11},{10,... | collective-permute-start | bytes 786440 | tf_op jit(solution)/shard_map/ppermute | solution.py:47
  123.0 9.5 %collective-permute-start.4 = (bf16[512,256]{1,0:T(8,128)(2,1)S(1)}, bf16[512,256]{1,0:T(8,128)(2,1)S(1)}, u32[]{:S(2)}, u32[]{:S(2)}) collective-permute-start(bf16[512,256]{1,0:T(8,128)(2,1)S(1)} %add_convert_fusion), channel_id=1, source_target_pairs={{0,2},{1,7},{2,4},{3,1},{4,6},{5,3},{6,0},{7,5},{8,10},{9,15},{10,... | collective-permute-start | bytes 786440 | tf_op jit(solution)/shard_map/ppermute | solution.py:47
Sparse Core Ops, SparseCore 0:
  32.7 40.2 all-gather.1

commit v8 on v7

--- a/solution.py
+++ b/solution.py
@@ -134,7 +134,10 @@
     picks = jnp.where(places_ref[...] == every, 1.0, 0.0).astype(jnp.bfloat16)
     picked = jnp.dot(picks, catalog_ref[...], preferred_element_type=jnp.float32)
     scale = 1.0 / math.sqrt(HEAD_DIM)
-    query_ref[...] = (picked[:, :q_width] * scale).astype(jnp.bfloat16)
+    heads = q_width // HEAD_DIM
+    for head in range(heads):
+        lanes = slice(head * HEAD_DIM, (head + 1) * HEAD_DIM)
+        query_ref[head] = (picked[:, lanes] * scale).astype(jnp.bfloat16)
     key_ref[...] = picked[:, q_width : q_width + HEAD_DIM].astype(jnp.bfloat16)
     values = picked[:, q_width + HEAD_DIM : kv_at]
     value_ref[...] = jnp.concatenate([values, jnp.ones_like(values)], axis=1).astype(jnp.bfloat16)
@@ -145,16 +148,19 @@
         row = start + lax.broadcasted_iota(jnp.int32, (chunk, upto), 0)
         column = lax.broadcasted_iota(jnp.int32, (chunk, upto), 1)
         allowed = (column <= row) & (column < length)
-        for head in range(q_width // HEAD_DIM):
+        queries = query_ref[:, start:upto, :].reshape(heads * chunk, HEAD_DIM)
+        scores = dot_t(queries, key_ref[:upto, :]).reshape(heads, chunk, upto)
+        scores = jnp.where(allowed[None], scores, -1e30)
+        parts = jnp.exp(scores - jnp.max(scores, axis=2, keepdims=True)).astype(jnp.bfloat16)
+        mixed = jnp.dot(
+            parts.reshape(heads * chunk, upto),
+            value_ref[:upto, :],
+            preferred_element_type=jnp.float32,
+        )
+        mixed = (mixed[:, :HEAD_DIM] / mixed[:, HEAD_DIM:]).astype(jnp.bfloat16)
+        for head in range(heads):
             lanes = slice(head * HEAD_DIM, (head + 1) * HEAD_DIM)
-            scores = dot_t(query_ref[start:upto, lanes], key_ref[:upto, :])
-            scores = jnp.where(allowed, scores, -1e30)
-            parts = jnp.exp(scores - jnp.max(scores, axis=1, keepdims=True))
-            mixed = jnp.dot(
-                parts.astype(jnp.bfloat16), value_ref[:upto, :], preferred_element_type=jnp.float32
-            )
-            mixed = mixed[:, :HEAD_DIM] / mixed[:, HEAD_DIM:]
-            mixed_ref[start:upto, lanes] = mixed.astype(jnp.bfloat16)
+            mixed_ref[start:upto, lanes] = mixed[head * chunk : (head + 1) * chunk]
 
 
 def output_kernel(mine_ref, others_ref, wo_mine_ref, wo_others_ref, *block_refs):
@@ -314,7 +320,7 @@
         [SMEM] + [VMEM] * 2,
         (scalars, places, catalog),
         [
-            pltpu.VMEM((slots, heads_width), jnp.bfloat16),
+            pltpu.VMEM((per, slots, HEAD_DIM), jnp.bfloat16),
             pltpu.VMEM((slots, HEAD_DIM), jnp.bfloat16),
             pltpu.VMEM((slots, 2 * HEAD_DIM), jnp.bfloat16),
         ],

time: 141 us -> 141 us (level)
  no operation moved by 1% of the time
where the time goes in v8:
time: 141 us; the launch traced here: 140 us
  waiting for transfers between devices  38.9 us (28%)
  starting transfers between devices  37.5 us (27%)
  blocking collectives  26.8 us (19%)
  between operations  14.9 us (11%)
  Pallas kernels  8.97 us (6%)
  local copies, waits for them, and re-layouts  6.09 us (4%)
  other arithmetic  4.24 us (3%)
  matrix products  2.3 us (2%)
    all_to_all x2, waiting for transfers between devices, spread(): return lax.all_to_all(copies, axis, 0, 0)  21.4 us
    all_to_all x2, starting transfers between devices, spread(): return lax.all_to_all(copies, axis, 0, 0)  14.1 us
    all_to_all x1, starting transfers between devices, local(): weights_z = lax.all_to_all(copies, 'z', 0, 0).reshape(n_z * depth, columns)  10.3 us
    all_to_all x1, blocking collectives, local(): last_raw = lax.all_to_all(messages, NARROW, 0, 0)  9.72 us
    ppermute x3, starting transfers between devices, along_x(): return lax.ppermute(values, NARROW, pairs)  9.21 us
    ppermute x3, waiting for transfers between devices, along_x(): return lax.ppermute(values, NARROW, pairs)  9 us
    pallas_call x9, Pallas kernels, call(): pl.pallas_call(kernel, name=name, out_shape=outs, in_specs=in_specs, out_...  8.97 us
    all_to_all x1, blocking collectives, local(): probes = lax.all_to_all(probes, NARROW, 0, 0)  8.52 us
  transfers between devices with their start and end apart: 9, of which 7 were waited for; matrix products, arithmetic and copies ran while one was open for 5% of the time, Pallas kernels for 5%

profile of v8, /device:TPU:16, one launch (start us, length us, event | category | flops | bytes accessed | tf_op | source)
XLA Modules:
  0.0 139.6 jit_solution(17753989455179575851)
XLA Ops:
  7.2 1.7 %user_weights.1 = bf16[8,32,640]{2,1,0:T(8,128)(2,1)} custom-call(bf16[32,256]{1,0:T(8,128)(2,1)} %wq_ref.2, bf16[32,128]{1,0:T(8,128)(2,1)} %bitcast.18, bf16[32,256]{1,0:T(8,128)(2,1)} %bitcast.17), custom_call_target="tpu_custom_call" | custom-call | tf_op jit(solution)/shard_map/user_weights/pallas_call | solution.py:185
  8.9 10.3 %all-to-all-start = ((bf16[8,32,640]{2,1,0:T(8,128)(2,1)}), bf16[8,32,640]{2,1,0:T(8,128)(2,1)}, u32[]{:S(2)}, u32[]{:S(2)}) async-start(bf16[8,32,640]{2,1,0:T(8,128)(2,1)} %user_weights.1), calls=%async_computation | async-start | bytes 655360 | tf_op jit(solution)/shard_map/all_to_all | solution.py:231
  19.2 0.0 all-gather.2.cloned.1.call-start
  19.2 0.7 broadcast_in_dim.34.gain_ref
  19.9 0.7 convert_element_type.43
  20.6 1.2 fusion.5
  21.9 1.0 copy-done.2
  22.9 0.1 last_rows.1
  23.6 0.7 broadcast_in_dim.16.gain_ref
  24.3 0.1 pad_add_fusion.scalar_ref
  24.4 1.2 fusion.7.normed_ref
  25.7 6.9 %all-to-all-done = bf16[8,32,640]{2,1,0:T(8,128)(2,1)} async-done(((bf16[8,32,640]{2,1,0:T(8,128)(2,1)}), bf16[8,32,640]{2,1,0:T(8,128)(2,1)}, u32[]{:S(2)}, u32[]{:S(2)}) %all-to-all-start) | async-done | bytes 327712 | tf_op jit(solution)/shard_map/all_to_all | solution.py:231
  32.6 0.0 all-gather.2.cloned.1.call-update
  32.6 9.7 %all_to_all.30.last_ref = f32[8,8,256]{2,1,0:T(8,128)S(1)} all-to-all(f32[8,8,256]{2,1,0:T(8,128)S(1)} %last_rows.1), channel_id=1, replica_groups=mesh['y'=8,'z'=8,'x'=4,'core'=2] {'x','core'}, dimensions={0} | all-to-all | bytes 131072 | tf_op jit(solution)/shard_map/all_to_all | solution.py:256
  42.3 1.3 item_probes.1
  43.6 8.5 %all_to_all.31.probes_ref = bf16[8,4,2048]{2,1,0:T(4,128)(2,1)S(1)} all-to-all(bf16[8,4,2048]{2,1,0:T(4,128)(2,1)S(1)} %get-tuple-element.23), channel_id=1, replica_groups=mesh['y'=8,'z'=8,'x'=4,'core'=2] {'x','core'}, dimensions={0} | all-to-all | bytes 262144 | tf_op jit(solution)/shard_map/all_to_all | solution.py:271
  52.1 0.7 item_attention.1
  52.9 8.5 %all_to_all.32 = bf16[8,4,2048]{2,1,0:T(4,128)(2,1)S(1)} all-to-all(bf16[8,4,2048]{2,1,0:T(4,128)(2,1)S(1)} %item_attention.1), channel_id=1, replica_groups=mesh['y'=8,'z'=8,'x'=4,'core'=2] {'x','core'}, dimensions={0} | all-to-all | bytes 262144 | tf_op jit(solution)/shard_map/all_to_all | solution.py:280
  61.4 0.3 convolution_convert_fusion.1
  61.8 0.1 reshape.41
  61.9 0.2 convolution_convert_fusion
  62.1 0.7 broadcast_in_dim.35
  62.8 3.4 %all-to-all-start.4 = ((bf16[8,8,2048]{2,1,0:T(8,128)(2,1)}), bf16[8,8,2048]{2,1,0:T(8,128)(2,1)S(1)}, u32[]{:S(2)}, u32[]{:S(2)}) async-start(bf16[8,8,2048]{2,1,0:T(8,128)(2,1)} %broadcast_in_dim.35), calls=%async_computation.4 | async-start | bytes 524288 | tf_op jit(solution)/shard_map/all_to_all | solution.py:33
  66.3 7.4 %all-to-all-done.4.terms_ref = bf16[8,8,2048]{2,1,0:T(8,128)(2,1)S(1)} async-done(((bf16[8,8,2048]{2,1,0:T(8,128)(2,1)}), bf16[8,8,2048]{2,1,0:T(8,128)(2,1)S(1)}, u32[]{:S(2)}, u32[]{:S(2)}) %all-to-all-start.4) | async-done | bytes 262176 | tf_op jit(solution)/shard_map/all_to_all | solution.py:33
  73.7 0.1 item_embeddings.1
  73.9 0.0 all-gather.2.cloned.1.call-done.weights_ref
  73.9 1.7 %fusion.2 = bf16[8,384]{1,0:T(8,128)(2,1)S(1)} fusion(bf16[8,2048]{1,0:T(8,128)(2,1)S(1)} %get-tuple-element.29, bf16[2048,640]{1,0:T(8,128)(2,1)} %all-gather.2.cloned.1.call-done.weights_ref), kind=kOutput, calls=%fused_computation.6 | convolution fusion | flops 12585984 | bytes 1611776 | tf_op jit(solution)/shard_map/dot_general | solution.py:295
  75.6 0.9 broadcast_in_dim.37
  76.5 10.6 %all-to-all-start.5 = ((bf16[64,8,640]{2,1,0:T(8,128)(2,1)}), bf16[64,8,640]{2,1,0:T(8,128)(2,1)S(1)}, u32[]{:S(2)}, u32[]{:S(2)}) async-start(bf16[64,8,640]{2,1,0:T(8,128)(2,1)} %broadcast_in_dim.37), calls=%async_computation.5 | async-start | bytes 1310720 | tf_op jit(solution)/shard_map/all_to_all | solution.py:33
  87.2 1.7 %copy-done.1 = bf16[2048,640]{1,0:T(8,128)(2,1)S(1)} copy-done((bf16[2048,640]{1,0:T(8,128)(2,1)S(1)}, bf16[2048,640]{1,0:T(8,128)(2,1)}, u32[]{:S(2)}) %copy-start.1) | copy-done | bytes 2621464
  88.9 1.4 %output_weights.1 = (bf16[4,256,256]{2,1,0:T(8,128)(2,1)}, bf16[4,256,256]{2,1,0:T(8,128)(2,1)S(1)}) custom-call(s32[3]{0:T(128)S(1)} %pad_add_fusion.scalar_ref, bf16[2048,640]{1,0:T(8,128)(2,1)S(1)} %copy-done.1), custom_call_target="tpu_custom_call" | custom-call | tf_op jit(solution)/shard_map/output_weights/pallas_call | solution.py:185
  90.4 1.9 %collective-permute-start.1 = (bf16[4,256,256]{2,1,0:T(8,128)(2,1)}, bf16[4,256,256]{2,1,0:T(8,128)(2,1)S(1)}, u32[]{:S(2)}, u32[]{:S(2)}) collective-permute-start(bf16[4,256,256]{2,1,0:T(8,128)(2,1)} %get-tuple-element.34), channel_id=1, source_target_pairs={{0,1},{1,0},{2,3},{3,2},{4,5},{5,4},{6,7},{7,6},{8,9},{9,8},{10,11... | collective-permute-start | bytes 1572872 | tf_op jit(solution)/shard_map/ppermute | solution.py:37
  92.3 0.1 copy.13.places_ref
  92.4 13.9 %all-to-all-done.5 = bf16[64,8,640]{2,1,0:T(8,128)(2,1)S(1)} async-done(((bf16[64,8,640]{2,1,0:T(8,128)(2,1)}), bf16[64,8,640]{2,1,0:T(8,128)(2,1)S(1)}, u32[]{:S(2)}, u32[]{:S(2)}) %all-to-all-start.5) | async-done | bytes 655392 | tf_op jit(solution)/shard_map/all_to_all | solution.py:33
  106.4 2.8 %user_attention.1 = (bf16[512,256]{1,0:T(8,128)(2,1)S(1)}, bf16[512,256]{1,0:T(8,128)(2,1)S(1)}) custom-call(s32[3]{0:T(128)S(1)} %pad_add_fusion.scalar_ref, s32[512,1]{1,0:T(8,128)S(1)} %copy.13.places_ref, bf16[512,640]{1,0:T(8,128)(2,1)S(1)} %bitcast.14), custom_call_target="tpu_custom_call" | custom-call | tf_op jit(solution)/shard_map/user_attention/pallas_call | solution.py:185
  109.1 1.9 %collective-permute-start = (bf16[512,256]{1,0:T(8,128)(2,1)S(1)}, bf16[512,256]{1,0:T(8,128)(2,1)S(1)}, u32[]{:S(2)}, u32[]{:S(2)}) collective-permute-start(bf16[512,256]{1,0:T(8,128)(2,1)S(1)} %get-tuple-element.32.mine_ref), channel_id=1, source_target_pairs={{0,1},{1,0},{2,3},{3,2},{4,5},{5,4},{6,7},{7,6},{8,9},{9,8},{10,11... | collective-permute-start | bytes 786440 | tf_op jit(solution)/shard_map/ppermute | solution.py:37
  111.1 1.5 %collective-permute-done.others_ref = bf16[512,256]{1,0:T(8,128)(2,1)S(1)} collective-permute-done((bf16[512,256]{1,0:T(8,128)(2,1)S(1)}, bf16[512,256]{1,0:T(8,128)(2,1)S(1)}, u32[]{:S(2)}, u32[]{:S(2)}) %collective-permute-start) | collective-permute-done | bytes 262176 | tf_op jit(solution)/shard_map/ppermute | solution.py:37
  112.6 0.3 output_first.1
  112.9 3.4 %collective-permute-start.3 = (bf16[512,256]{1,0:T(8,128)(2,1)S(1)}, bf16[512,256]{1,0:T(8,128)(2,1)S(1)}, u32[]{:S(2)}, u32[]{:S(2)}) collective-permute-start(bf16[512,256]{1,0:T(8,128)(2,1)S(1)} %output_first.1), channel_id=1, source_target_pairs={{0,2},{1,7},{2,4},{3,1},{4,6},{5,3},{6,0},{7,5},{8,10},{9,15},{10,... | collective-permute-start | bytes 786440 | tf_op jit(solution)/shard_map/ppermute | solution.py:47
  116.3 0.6 output_blocks.1
  116.9 3.7 %collective-permute-start.2 = (bf16[512,256]{1,0:T(8,128)(2,1)S(1)}, bf16[512,256]{1,0:T(8,128)(2,1)S(1)}, u32[]{:S(2)}, u32[]{:S(2)}) collective-permute-start(bf16[512,256]{1,0:T(8,128)(2,1)S(1)} %get-tuple-element.36), channel_id=1, source_target_pairs={{0,6},{1,3},{2,0},{3,5},{4,2},{5,7},{6,4},{7,1},{8,14},{9,11},{10,... | collective-permute-start | bytes 786440 | tf_op jit(solution)/shard_map/ppermute | solution.py:47
  120.6 1.8 %collective-permute-done.3 = bf16[512,256]{1,0:T(8,128)(2,1)S(1)} collective-permute-done((bf16[512,256]{1,0:T(8,128)(2,1)S(1)}, bf16[512,256]{1,0:T(8,128)(2,1)S(1)}, u32[]{:S(2)}, u32[]{:S(2)}) %collective-permute-start.3) | collective-permute-done | bytes 262176 | tf_op jit(solution)/shard_map/ppermute | solution.py:47
  122.4 0.1 add_convert_fusion
  122.4 2.2 %collective-permute-start.4 = (bf16[512,256]{1,0:T(8,128)(2,1)S(1)}, bf16[512,256]{1,0:T(8,128)(2,1)S(1)}, u32[]{:S(2)}, u32[]{:S(2)}) collective-permute-start(bf16[512,256]{1,0:T(8,128)(2,1)S(1)} %add_convert_fusion), channel_id=1, source_target_pairs={{0,2},{1,7},{2,4},{3,1},{4,6},{5,3},{6,0},{7,5},{8,10},{9,15},{10,... | collective-permute-start | bytes 786440 | tf_op jit(solution)/shard_map/ppermute | solution.py:47
  124.6 0.5 collective-permute-done.2
  125.2 0.1 convert_add_fusion
  125.3 6.7 %collective-permute-done.4 = bf16[512,256]{1,0:T(8,128)(2,1)S(1)} collective-permute-done((bf16[512,256]{1,0:T(8,128)(2,1)S(1)}, bf16[512,256]{1,0:T(8,128)(2,1)S(1)}, u32[]{:S(2)}, u32[]{:S(2)}) %collective-permute-start.4) | collective-permute-done | bytes 262176 | tf_op jit(solution)/shard_map/ppermute | solution.py:47
  131.9 0.8 select_convert_fusion
  (18 shorter events, 0.1 us)
Async XLA Ops:
  7.2 54.7 %copy-start = (bf16[256,2048]{1,0:T(8,128)(2,1)S(1)}, bf16[256,2048]{1,0:T(8,128)(2,1)}, u32[]{:S(2)}) copy-start(bf16[256,2048]{1,0:T(8,128)(2,1)} %param.15) | copy-start | bytes 3145732
  7.2 35.2 %copy-start.3 = (bf16[2048,1,128]{2,0,1:T(8,128)(2,1)S(1)}, bf16[2048,1,128]{2,0,1:T(8,128)(2,1)}, u32[]{:S(2)}) copy-start(bf16[2048,1,128]{2,0,1:T(8,128)(2,1)} %param.14) | copy-start | bytes 1572868
  7.2 35.1 %copy-start.4 = (bf16[2048,256]{1,0:T(8,128)(2,1)S(1)}, bf16[2048,256]{1,0:T(8,128)(2,1)}, u32[]{:S(2)}) copy-start(bf16[2048,256]{1,0:T(8,128)(2,1)} %wq_ref.3) | copy-start | bytes 3145732
  8.9 23.7 %all-to-all-start = ((bf16[8,32,640]{2,1,0:T(8,128)(2,1)}), bf16[8,32,640]{2,1,0:T(8,128)(2,1)}, u32[]{:S(2)}, u32[]{:S(2)}) async-start(bf16[8,32,640]{2,1,0:T(8,128)(2,1)} %user_weights.1), calls=%async_computation | async-start | bytes 655360 | tf_op jit(solution)/shard_map/all_to_all | solution.py:231
  19.2 54.7 %all-gather.2.cloned.1.call-start = ((), (), s32[]{:S(2)}) async-start(), calls=%async_computation.6 | async-start | bytes 2949120 | tf_op jit(solution)/shard_map/all_gather | solution.py:255
  21.9 1.0 copy-start.2
  62.8 10.9 %all-to-all-start.4 = ((bf16[8,8,2048]{2,1,0:T(8,128)(2,1)}), bf16[8,8,2048]{2,1,0:T(8,128)(2,1)S(1)}, u32[]{:S(2)}, u32[]{:S(2)}) async-start(bf16[8,8,2048]{2,1,0:T(8,128)(2,1)} %broadcast_in_dim.35), calls=%async_computation.4 | async-start | bytes 524288 | tf_op jit(solution)/shard_map/all_to_all | solution.py:33
  73.9 16.5 %copy-start.5 = (bf16[8,256]{1,0:T(8,128)(2,1)}, bf16[8,256]{1,0:T(8,128)(2,1)S(1)}, u32[]{:S(2)}) copy-start(bf16[8,256]{1,0:T(8,128)(2,1)S(1)} %constant_dynamic-slice_fusion) | copy-start | bytes 12292
  75.6 16.6 %copy-start.6 = (s32[1,512]{1,0:T(1,128)S(1)}, s32[1,512]{1,0:T(1,128)}, u32[]{:S(2)}) copy-start(s32[1,512]{1,0:T(1,128)} %param.20) | copy-start | bytes 6148
  76.5 29.8 %all-to-all-start.5 = ((bf16[64,8,640]{2,1,0:T(8,128)(2,1)}), bf16[64,8,640]{2,1,0:T(8,128)(2,1)S(1)}, u32[]{:S(2)}, u32[]{:S(2)}) async-start(bf16[64,8,640]{2,1,0:T(8,128)(2,1)} %broadcast_in_dim.37), calls=%async_computation.5 | async-start | bytes 1310720 | tf_op jit(solution)/shard_map/all_to_all | solution.py:33
  87.2 1.7 %copy-start.1 = (bf16[2048,640]{1,0:T(8,128)(2,1)S(1)}, bf16[2048,640]{1,0:T(8,128)(2,1)}, u32[]{:S(2)}) copy-start(bf16[2048,640]{1,0:T(8,128)(2,1)} %all-gather.2.cloned.1.call-done.weights_ref) | copy-start | bytes 7864324
  90.4 20.7 %collective-permute-start.1 = (bf16[4,256,256]{2,1,0:T(8,128)(2,1)}, bf16[4,256,256]{2,1,0:T(8,128)(2,1)S(1)}, u32[]{:S(2)}, u32[]{:S(2)}) collective-permute-start(bf16[4,256,256]{2,1,0:T(8,128)(2,1)} %get-tuple-element.34), channel_id=1, source_target_pairs={{0,1},{1,0},{2,3},{3,2},{4,5},{5,4},{6,7},{7,6},{8,9},{9,8},{10,11... | collective-permute-start | bytes 1572872 | tf_op jit(solution)/shard_map/ppermute | solution.py:37
  109.1 3.4 %collective-permute-start = (bf16[512,256]{1,0:T(8,128)(2,1)S(1)}, bf16[512,256]{1,0:T(8,128)(2,1)S(1)}, u32[]{:S(2)}, u32[]{:S(2)}) collective-permute-start(bf16[512,256]{1,0:T(8,128)(2,1)S(1)} %get-tuple-element.32.mine_ref), channel_id=1, source_target_pairs={{0,1},{1,0},{2,3},{3,2},{4,5},{5,4},{6,7},{7,6},{8,9},{9,8},{10,11... | collective-permute-start | bytes 786440 | tf_op jit(solution)/shard_map/ppermute | solution.py:37
  112.9 9.5 %collective-permute-start.3 = (bf16[512,256]{1,0:T(8,128)(2,1)S(1)}, bf16[512,256]{1,0:T(8,128)(2,1)S(1)}, u32[]{:S(2)}, u32[]{:S(2)}) collective-permute-start(bf16[512,256]{1,0:T(8,128)(2,1)S(1)} %output_first.1), channel_id=1, source_target_pairs={{0,2},{1,7},{2,4},{3,1},{4,6},{5,3},{6,0},{7,5},{8,10},{9,15},{10,... | collective-permute-start | bytes 786440 | tf_op jit(solution)/shard_map/ppermute | solution.py:47
  116.9 8.3 %collective-permute-start.2 = (bf16[512,256]{1,0:T(8,128)(2,1)S(1)}, bf16[512,256]{1,0:T(8,128)(2,1)S(1)}, u32[]{:S(2)}, u32[]{:S(2)}) collective-permute-start(bf16[512,256]{1,0:T(8,128)(2,1)S(1)} %get-tuple-element.36), channel_id=1, source_target_pairs={{0,6},{1,3},{2,0},{3,5},{4,2},{5,7},{6,4},{7,1},{8,14},{9,11},{10,... | collective-permute-start | bytes 786440 | tf_op jit(solution)/shard_map/ppermute | solution.py:47
  122.4 9.5 %collective-permute-start.4 = (bf16[512,256]{1,0:T(8,128)(2,1)S(1)}, bf16[512,256]{1,0:T(8,128)(2,1)S(1)}, u32[]{:S(2)}, u32[]{:S(2)}) collective-permute-start(bf16[512,256]{1,0:T(8,128)(2,1)S(1)} %add_convert_fusion), channel_id=1, source_target_pairs={{0,2},{1,7},{2,4},{3,1},{4,6},{5,3},{6,0},{7,5},{8,10},{9,15},{10,... | collective-permute-start | bytes 786440 | tf_op jit(solution)/shard_map/ppermute | solution.py:47
Sparse Core Ops, SparseCore 0:
  32.7 40.2 all-gather.1

commit v9 on v8

--- a/solution.py
+++ b/solution.py
@@ -124,15 +124,28 @@
         mine_ref[k] = weights_ref[rows, -out_width:]
 
 
+def one_hot(places_ref, slots, catalog):
+    every = lax.broadcasted_iota(jnp.int32, (slots, catalog), 1)
+    return jnp.where(places_ref[...] == every, 1.0, 0.0).astype(jnp.bfloat16)
+
+
+def residual_kernel(places_ref, catalog_ref, mixed_ref, residual_ref):
+    del mixed_ref
+    slots, share = residual_ref.shape
+    picks = one_hot(places_ref, slots, catalog_ref.shape[0])
+    residual_ref[...] = jnp.dot(
+        picks, catalog_ref[:, -share:], preferred_element_type=jnp.float32
+    ).astype(jnp.bfloat16)
+
+
 def user_kernel(
-    scalar_ref, places_ref, catalog_ref, mixed_ref, residual_ref, query_ref, key_ref, value_ref
+    scalar_ref, places_ref, catalog_ref, mixed_ref, query_ref, key_ref, value_ref
 ):
     length = scalar_ref[0]
     slots, q_width = mixed_ref.shape
     catalog, kv_at = catalog_ref.shape[0], q_width + 2 * HEAD_DIM
-    every = lax.broadcasted_iota(jnp.int32, (slots, catalog), 1)
-    picks = jnp.where(places_ref[...] == every, 1.0, 0.0).astype(jnp.bfloat16)
-    picked = jnp.dot(picks, catalog_ref[...], preferred_element_type=jnp.float32)
+    picks = one_hot(places_ref, slots, catalog)
+    picked = jnp.dot(picks, catalog_ref[:, :kv_at], preferred_element_type=jnp.float32)
     scale = 1.0 / math.sqrt(HEAD_DIM)
     heads = q_width // HEAD_DIM
     for head in range(heads):
@@ -141,7 +154,6 @@
     key_ref[...] = picked[:, q_width : q_width + HEAD_DIM].astype(jnp.bfloat16)
     values = picked[:, q_width + HEAD_DIM : kv_at]
     value_ref[...] = jnp.concatenate([values, jnp.ones_like(values)], axis=1).astype(jnp.bfloat16)
-    residual_ref[...] = picked[:, kv_at:].astype(jnp.bfloat16)
     chunk = min(slots, 256)
     for start in range(0, slots, chunk):
         upto = start + chunk
@@ -309,14 +321,11 @@
     )
     wo_others = swap_cores(wo_theirs)
     slots = history_items.shape[1]
-    user_mixed, residual = call(
+    user_mixed = call(
         user_kernel,
         "user_attention",
         20,
-        (
-            jax.ShapeDtypeStruct((slots, heads_width), jnp.bfloat16),
-            jax.ShapeDtypeStruct((slots, share), jnp.bfloat16),
-        ),
+        jax.ShapeDtypeStruct((slots, heads_width), jnp.bfloat16),
         [SMEM] + [VMEM] * 2,
         (scalars, places, catalog),
         [
@@ -324,6 +333,15 @@
             pltpu.VMEM((slots, HEAD_DIM), jnp.bfloat16),
             pltpu.VMEM((slots, 2 * HEAD_DIM), jnp.bfloat16),
         ],
+    )
+
+    residual = call(
+        residual_kernel,
+        "residual_rows",
+        20,
+        jax.ShapeDtypeStruct((slots, share), jnp.bfloat16),
+        [VMEM] * 3,
+        (places, catalog, user_mixed),
     )
 
     block = jax.ShapeDtypeStruct((slots, share), jnp.bfloat16)

time: 141 us -> 141 us (level)
    pallas_call x9 -> x10, Pallas kernels: 8.97 us -> 9.25 us  [call(): pl.pallas_call(kernel, name=name, out_shape=outs, in_specs=in_specs, out_...]
where the time goes in v9:
time: 141 us; the launch traced here: 140 us
  waiting for transfers between devices  38.5 us (27%)
  starting transfers between devices  37.5 us (27%)
  blocking collectives  26.8 us (19%)
  between operations  14.9 us (11%)
  Pallas kernels  9.25 us (7%)
  local copies, waits for them, and re-layouts  6.09 us (4%)
  other arithmetic  4.24 us (3%)
  matrix products  2.3 us (2%)
    all_to_all x2, waiting for transfers between devices, spread(): return lax.all_to_all(copies, axis, 0, 0)  21.4 us
    all_to_all x2, starting transfers between devices, spread(): return lax.all_to_all(copies, axis, 0, 0)  14.1 us
    all_to_all x1, starting transfers between devices, local(): weights_z = lax.all_to_all(copies, 'z', 0, 0).reshape(n_z * depth, columns)  10.3 us
    all_to_all x1, blocking collectives, local(): last_raw = lax.all_to_all(messages, NARROW, 0, 0)  9.72 us
    pallas_call x10, Pallas kernels, call(): pl.pallas_call(kernel, name=name, out_shape=outs, in_specs=in_specs, out_...  9.25 us
    ppermute x3, starting transfers between devices, along_x(): return lax.ppermute(values, NARROW, pairs)  9.2 us
    ppermute x3, waiting for transfers between devices, along_x(): return lax.ppermute(values, NARROW, pairs)  8.66 us
    all_to_all x1, blocking collectives, local(): probes = lax.all_to_all(probes, NARROW, 0, 0)  8.52 us
  transfers between devices with their start and end apart: 9, of which 7 were waited for; matrix products, arithmetic and copies ran while one was open for 5% of the time, Pallas kernels for 5%

profile of v9, /device:TPU:16, one launch (start us, length us, event | category | flops | bytes accessed | tf_op | source)
XLA Modules:
  0.0 139.5 jit_solution(17065257289478723780)
XLA Ops:
  7.2 1.7 %user_weights.1 = bf16[8,32,640]{2,1,0:T(8,128)(2,1)} custom-call(bf16[32,256]{1,0:T(8,128)(2,1)} %wq_ref.2, bf16[32,128]{1,0:T(8,128)(2,1)} %bitcast.19, bf16[32,256]{1,0:T(8,128)(2,1)} %bitcast.18), custom_call_target="tpu_custom_call" | custom-call | tf_op jit(solution)/shard_map/user_weights/pallas_call | solution.py:197
  8.9 10.3 %all-to-all-start = ((bf16[8,32,640]{2,1,0:T(8,128)(2,1)}), bf16[8,32,640]{2,1,0:T(8,128)(2,1)}, u32[]{:S(2)}, u32[]{:S(2)}) async-start(bf16[8,32,640]{2,1,0:T(8,128)(2,1)} %user_weights.1), calls=%async_computation | async-start | bytes 655360 | tf_op jit(solution)/shard_map/all_to_all | solution.py:243
  19.2 0.0 all-gather.2.cloned.1.call-start
  19.3 0.7 broadcast_in_dim.34.gain_ref
  20.0 0.7 convert_element_type.43
  20.6 1.2 fusion.5
  21.9 1.0 copy-done.2
  22.9 0.1 last_rows.1
  23.7 0.7 broadcast_in_dim.16.gain_ref
  24.3 0.1 pad_add_fusion.scalar_ref
  24.4 1.2 fusion.7.normed_ref
  25.7 6.9 %all-to-all-done = bf16[8,32,640]{2,1,0:T(8,128)(2,1)} async-done(((bf16[8,32,640]{2,1,0:T(8,128)(2,1)}), bf16[8,32,640]{2,1,0:T(8,128)(2,1)}, u32[]{:S(2)}, u32[]{:S(2)}) %all-to-all-start) | async-done | bytes 327712 | tf_op jit(solution)/shard_map/all_to_all | solution.py:243
  32.6 9.7 %all_to_all.30.last_ref = f32[8,8,256]{2,1,0:T(8,128)S(1)} all-to-all(f32[8,8,256]{2,1,0:T(8,128)S(1)} %last_rows.1), channel_id=1, replica_groups=mesh['y'=8,'z'=8,'x'=4,'core'=2] {'x','core'}, dimensions={0} | all-to-all | bytes 131072 | tf_op jit(solution)/shard_map/all_to_all | solution.py:268
  42.3 1.3 item_probes.1
  43.6 8.5 %all_to_all.31.probes_ref = bf16[8,4,2048]{2,1,0:T(4,128)(2,1)S(1)} all-to-all(bf16[8,4,2048]{2,1,0:T(4,128)(2,1)S(1)} %get-tuple-element.21), channel_id=1, replica_groups=mesh['y'=8,'z'=8,'x'=4,'core'=2] {'x','core'}, dimensions={0} | all-to-all | bytes 262144 | tf_op jit(solution)/shard_map/all_to_all | solution.py:283
  52.1 0.7 item_attention.1
  52.9 8.5 %all_to_all.32 = bf16[8,4,2048]{2,1,0:T(4,128)(2,1)S(1)} all-to-all(bf16[8,4,2048]{2,1,0:T(4,128)(2,1)S(1)} %item_attention.1), channel_id=1, replica_groups=mesh['y'=8,'z'=8,'x'=4,'core'=2] {'x','core'}, dimensions={0} | all-to-all | bytes 262144 | tf_op jit(solution)/shard_map/all_to_all | solution.py:292
  61.4 0.3 convolution_convert_fusion.1
  61.8 0.1 reshape.41
  61.9 0.2 convolution_convert_fusion
  62.1 0.7 broadcast_in_dim.35
  62.8 3.4 %all-to-all-start.4 = ((bf16[8,8,2048]{2,1,0:T(8,128)(2,1)}), bf16[8,8,2048]{2,1,0:T(8,128)(2,1)S(1)}, u32[]{:S(2)}, u32[]{:S(2)}) async-start(bf16[8,8,2048]{2,1,0:T(8,128)(2,1)} %broadcast_in_dim.35), calls=%async_computation.4 | async-start | bytes 524288 | tf_op jit(solution)/shard_map/all_to_all | solution.py:33
  66.3 7.4 %all-to-all-done.4.terms_ref = bf16[8,8,2048]{2,1,0:T(8,128)(2,1)S(1)} async-done(((bf16[8,8,2048]{2,1,0:T(8,128)(2,1)}), bf16[8,8,2048]{2,1,0:T(8,128)(2,1)S(1)}, u32[]{:S(2)}, u32[]{:S(2)}) %all-to-all-start.4) | async-done | bytes 262176 | tf_op jit(solution)/shard_map/all_to_all | solution.py:33
  73.7 0.1 item_embeddings.1
  73.9 0.0 all-gather.2.cloned.1.call-done.weights_ref
  73.9 1.7 %fusion.2 = bf16[8,384]{1,0:T(8,128)(2,1)S(1)} fusion(bf16[8,2048]{1,0:T(8,128)(2,1)S(1)} %get-tuple-element.26, bf16[2048,640]{1,0:T(8,128)(2,1)} %all-gather.2.cloned.1.call-done.weights_ref), kind=kOutput, calls=%fused_computation.6 | convolution fusion | flops 12585984 | bytes 1611776 | tf_op jit(solution)/shard_map/dot_general | solution.py:307
  75.7 0.9 broadcast_in_dim.37
  76.5 10.6 %all-to-all-start.5 = ((bf16[64,8,640]{2,1,0:T(8,128)(2,1)}), bf16[64,8,640]{2,1,0:T(8,128)(2,1)S(1)}, u32[]{:S(2)}, u32[]{:S(2)}) async-start(bf16[64,8,640]{2,1,0:T(8,128)(2,1)} %broadcast_in_dim.37), calls=%async_computation.5 | async-start | bytes 1310720 | tf_op jit(solution)/shard_map/all_to_all | solution.py:33
  87.2 1.7 %copy-done.1 = bf16[2048,640]{1,0:T(8,128)(2,1)S(1)} copy-done((bf16[2048,640]{1,0:T(8,128)(2,1)S(1)}, bf16[2048,640]{1,0:T(8,128)(2,1)}, u32[]{:S(2)}) %copy-start.1) | copy-done | bytes 2621464
  88.9 1.4 %output_weights.1 = (bf16[4,256,256]{2,1,0:T(8,128)(2,1)}, bf16[4,256,256]{2,1,0:T(8,128)(2,1)S(1)}) custom-call(s32[3]{0:T(128)S(1)} %pad_add_fusion.scalar_ref, bf16[2048,640]{1,0:T(8,128)(2,1)S(1)} %copy-done.1), custom_call_target="tpu_custom_call" | custom-call | tf_op jit(solution)/shard_map/output_weights/pallas_call | solution.py:197
  90.4 1.9 %collective-permute-start.1 = (bf16[4,256,256]{2,1,0:T(8,128)(2,1)}, bf16[4,256,256]{2,1,0:T(8,128)(2,1)S(1)}, u32[]{:S(2)}, u32[]{:S(2)}) collective-permute-start(bf16[4,256,256]{2,1,0:T(8,128)(2,1)} %get-tuple-element.30), channel_id=1, source_target_pairs={{0,1},{1,0},{2,3},{3,2},{4,5},{5,4},{6,7},{7,6},{8,9},{9,8},{10,11... | collective-permute-start | bytes 1572872 | tf_op jit(solution)/shard_map/ppermute | solution.py:37
  92.3 0.1 copy.14.places_ref
  92.4 13.9 %all-to-all-done.5 = bf16[64,8,640]{2,1,0:T(8,128)(2,1)S(1)} async-done(((bf16[64,8,640]{2,1,0:T(8,128)(2,1)}), bf16[64,8,640]{2,1,0:T(8,128)(2,1)S(1)}, u32[]{:S(2)}, u32[]{:S(2)}) %all-to-all-start.5) | async-done | bytes 655392 | tf_op jit(solution)/shard_map/all_to_all | solution.py:33
  106.4 2.7 %user_attention.1.mixed_ref.mine_ref = bf16[512,256]{1,0:T(8,128)(2,1)S(1)} custom-call(s32[3]{0:T(128)S(1)} %pad_add_fusion.scalar_ref, s32[512,1]{1,0:T(8,128)S(1)} %copy.14.places_ref, bf16[512,640]{1,0:T(8,128)(2,1)S(1)} %bitcast.14), custom_call_target="tpu_custom_call" | custom-call | tf_op jit(solution)/shard_map/user_attention/pallas_call | solution.py:197
  109.1 1.9 %collective-permute-start = (bf16[512,256]{1,0:T(8,128)(2,1)S(1)}, bf16[512,256]{1,0:T(8,128)(2,1)S(1)}, u32[]{:S(2)}, u32[]{:S(2)}) collective-permute-start(bf16[512,256]{1,0:T(8,128)(2,1)S(1)} %user_attention.1.mixed_ref.mine_ref), channel_id=1, source_target_pairs={{0,1},{1,0},{2,3},{3,2},{4,5},{5,4},{6,7},{7,6},{8,9},{9,8},{10,11... | collective-permute-start | bytes 786440 | tf_op jit(solution)/shard_map/ppermute | solution.py:37
  111.0 1.5 %collective-permute-done.others_ref = bf16[512,256]{1,0:T(8,128)(2,1)S(1)} collective-permute-done((bf16[512,256]{1,0:T(8,128)(2,1)S(1)}, bf16[512,256]{1,0:T(8,128)(2,1)S(1)}, u32[]{:S(2)}, u32[]{:S(2)}) %collective-permute-start) | collective-permute-done | bytes 262176 | tf_op jit(solution)/shard_map/ppermute | solution.py:37
  112.5 0.3 output_first.1
  112.8 3.4 %collective-permute-start.3 = (bf16[512,256]{1,0:T(8,128)(2,1)S(1)}, bf16[512,256]{1,0:T(8,128)(2,1)S(1)}, u32[]{:S(2)}, u32[]{:S(2)}) collective-permute-start(bf16[512,256]{1,0:T(8,128)(2,1)S(1)} %output_first.1), channel_id=1, source_target_pairs={{0,2},{1,7},{2,4},{3,1},{4,6},{5,3},{6,0},{7,5},{8,10},{9,15},{10,... | collective-permute-start | bytes 786440 | tf_op jit(solution)/shard_map/ppermute | solution.py:47
  116.2 0.6 output_blocks.1
  116.8 3.7 %collective-permute-start.2 = (bf16[512,256]{1,0:T(8,128)(2,1)S(1)}, bf16[512,256]{1,0:T(8,128)(2,1)S(1)}, u32[]{:S(2)}, u32[]{:S(2)}) collective-permute-start(bf16[512,256]{1,0:T(8,128)(2,1)S(1)} %get-tuple-element.32), channel_id=1, source_target_pairs={{0,6},{1,3},{2,0},{3,5},{4,2},{5,7},{6,4},{7,1},{8,14},{9,11},{10,... | collective-permute-start | bytes 786440 | tf_op jit(solution)/shard_map/ppermute | solution.py:47
  120.5 1.8 %collective-permute-done.3 = bf16[512,256]{1,0:T(8,128)(2,1)S(1)} collective-permute-done((bf16[512,256]{1,0:T(8,128)(2,1)S(1)}, bf16[512,256]{1,0:T(8,128)(2,1)S(1)}, u32[]{:S(2)}, u32[]{:S(2)}) %collective-permute-start.3) | collective-permute-done | bytes 262176 | tf_op jit(solution)/shard_map/ppermute | solution.py:47
  122.3 0.1 add_convert_fusion
  122.4 2.2 %collective-permute-start.4 = (bf16[512,256]{1,0:T(8,128)(2,1)S(1)}, bf16[512,256]{1,0:T(8,128)(2,1)S(1)}, u32[]{:S(2)}, u32[]{:S(2)}) collective-permute-start(bf16[512,256]{1,0:T(8,128)(2,1)S(1)} %add_convert_fusion), channel_id=1, source_target_pairs={{0,2},{1,7},{2,4},{3,1},{4,6},{5,3},{6,0},{7,5},{8,10},{9,15},{10,... | collective-permute-start | bytes 786440 | tf_op jit(solution)/shard_map/ppermute | solution.py:47
  124.5 0.3 residual_rows.1
  124.9 0.2 collective-permute-done.2
  125.1 0.1 convert_add_fusion
  125.2 6.7 %collective-permute-done.4 = bf16[512,256]{1,0:T(8,128)(2,1)S(1)} collective-permute-done((bf16[512,256]{1,0:T(8,128)(2,1)S(1)}, bf16[512,256]{1,0:T(8,128)(2,1)S(1)}, u32[]{:S(2)}, u32[]{:S(2)}) %collective-permute-start.4) | collective-permute-done | bytes 262176 | tf_op jit(solution)/shard_map/ppermute | solution.py:47
  131.9 0.8 select_convert_fusion
  (19 shorter events, 0.1 us)
Async XLA Ops:
  7.2 54.7 %copy-start = (bf16[256,2048]{1,0:T(8,128)(2,1)S(1)}, bf16[256,2048]{1,0:T(8,128)(2,1)}, u32[]{:S(2)}) copy-start(bf16[256,2048]{1,0:T(8,128)(2,1)} %param.15) | copy-start | bytes 3145732
  7.2 35.2 %copy-start.3 = (bf16[2048,1,128]{2,0,1:T(8,128)(2,1)S(1)}, bf16[2048,1,128]{2,0,1:T(8,128)(2,1)}, u32[]{:S(2)}) copy-start(bf16[2048,1,128]{2,0,1:T(8,128)(2,1)} %param.14) | copy-start | bytes 1572868
  7.2 35.2 %copy-start.4 = (bf16[2048,256]{1,0:T(8,128)(2,1)S(1)}, bf16[2048,256]{1,0:T(8,128)(2,1)}, u32[]{:S(2)}) copy-start(bf16[2048,256]{1,0:T(8,128)(2,1)} %wq_ref.3) | copy-start | bytes 3145732
  8.9 23.7 %all-to-all-start = ((bf16[8,32,640]{2,1,0:T(8,128)(2,1)}), bf16[8,32,640]{2,1,0:T(8,128)(2,1)}, u32[]{:S(2)}, u32[]{:S(2)}) async-start(bf16[8,32,640]{2,1,0:T(8,128)(2,1)} %user_weights.1), calls=%async_computation | async-start | bytes 655360 | tf_op jit(solution)/shard_map/all_to_all | solution.py:243
  19.2 54.7 %all-gather.2.cloned.1.call-start = ((), (), s32[]{:S(2)}) async-start(), calls=%async_computation.6 | async-start | bytes 2949120 | tf_op jit(solution)/shard_map/all_gather | solution.py:267
  21.9 1.0 copy-start.2
  62.8 10.9 %all-to-all-start.4 = ((bf16[8,8,2048]{2,1,0:T(8,128)(2,1)}), bf16[8,8,2048]{2,1,0:T(8,128)(2,1)S(1)}, u32[]{:S(2)}, u32[]{:S(2)}) async-start(bf16[8,8,2048]{2,1,0:T(8,128)(2,1)} %broadcast_in_dim.35), calls=%async_computation.4 | async-start | bytes 524288 | tf_op jit(solution)/shard_map/all_to_all | solution.py:33
  73.9 16.5 %copy-start.5 = (bf16[8,256]{1,0:T(8,128)(2,1)}, bf16[8,256]{1,0:T(8,128)(2,1)S(1)}, u32[]{:S(2)}) copy-start(bf16[8,256]{1,0:T(8,128)(2,1)S(1)} %constant_dynamic-slice_fusion) | copy-start | bytes 12292
  75.6 16.6 %copy-start.6 = (s32[1,512]{1,0:T(1,128)S(1)}, s32[1,512]{1,0:T(1,128)}, u32[]{:S(2)}) copy-start(s32[1,512]{1,0:T(1,128)} %param.20) | copy-start | bytes 6148
  76.5 29.8 %all-to-all-start.5 = ((bf16[64,8,640]{2,1,0:T(8,128)(2,1)}), bf16[64,8,640]{2,1,0:T(8,128)(2,1)S(1)}, u32[]{:S(2)}, u32[]{:S(2)}) async-start(bf16[64,8,640]{2,1,0:T(8,128)(2,1)} %broadcast_in_dim.37), calls=%async_computation.5 | async-start | bytes 1310720 | tf_op jit(solution)/shard_map/all_to_all | solution.py:33
  87.2 1.7 %copy-start.1 = (bf16[2048,640]{1,0:T(8,128)(2,1)S(1)}, bf16[2048,640]{1,0:T(8,128)(2,1)}, u32[]{:S(2)}) copy-start(bf16[2048,640]{1,0:T(8,128)(2,1)} %all-gather.2.cloned.1.call-done.weights_ref) | copy-start | bytes 7864324
  90.4 20.6 %collective-permute-start.1 = (bf16[4,256,256]{2,1,0:T(8,128)(2,1)}, bf16[4,256,256]{2,1,0:T(8,128)(2,1)S(1)}, u32[]{:S(2)}, u32[]{:S(2)}) collective-permute-start(bf16[4,256,256]{2,1,0:T(8,128)(2,1)} %get-tuple-element.30), channel_id=1, source_target_pairs={{0,1},{1,0},{2,3},{3,2},{4,5},{5,4},{6,7},{7,6},{8,9},{9,8},{10,11... | collective-permute-start | bytes 1572872 | tf_op jit(solution)/shard_map/ppermute | solution.py:37
  109.1 3.4 %collective-permute-start = (bf16[512,256]{1,0:T(8,128)(2,1)S(1)}, bf16[512,256]{1,0:T(8,128)(2,1)S(1)}, u32[]{:S(2)}, u32[]{:S(2)}) collective-permute-start(bf16[512,256]{1,0:T(8,128)(2,1)S(1)} %user_attention.1.mixed_ref.mine_ref), channel_id=1, source_target_pairs={{0,1},{1,0},{2,3},{3,2},{4,5},{5,4},{6,7},{7,6},{8,9},{9,8},{10,11... | collective-permute-start | bytes 786440 | tf_op jit(solution)/shard_map/ppermute | solution.py:37
  112.8 9.5 %collective-permute-start.3 = (bf16[512,256]{1,0:T(8,128)(2,1)S(1)}, bf16[512,256]{1,0:T(8,128)(2,1)S(1)}, u32[]{:S(2)}, u32[]{:S(2)}) collective-permute-start(bf16[512,256]{1,0:T(8,128)(2,1)S(1)} %output_first.1), channel_id=1, source_target_pairs={{0,2},{1,7},{2,4},{3,1},{4,6},{5,3},{6,0},{7,5},{8,10},{9,15},{10,... | collective-permute-start | bytes 786440 | tf_op jit(solution)/shard_map/ppermute | solution.py:47
  116.8 8.3 %collective-permute-start.2 = (bf16[512,256]{1,0:T(8,128)(2,1)S(1)}, bf16[512,256]{1,0:T(8,128)(2,1)S(1)}, u32[]{:S(2)}, u32[]{:S(2)}) collective-permute-start(bf16[512,256]{1,0:T(8,128)(2,1)S(1)} %get-tuple-element.32), channel_id=1, source_target_pairs={{0,6},{1,3},{2,0},{3,5},{4,2},{5,7},{6,4},{7,1},{8,14},{9,11},{10,... | collective-permute-start | bytes 786440 | tf_op jit(solution)/shard_map/ppermute | solution.py:47
  122.4 9.5 %collective-permute-start.4 = (bf16[512,256]{1,0:T(8,128)(2,1)S(1)}, bf16[512,256]{1,0:T(8,128)(2,1)S(1)}, u32[]{:S(2)}, u32[]{:S(2)}) collective-permute-start(bf16[512,256]{1,0:T(8,128)(2,1)S(1)} %add_convert_fusion), channel_id=1, source_target_pairs={{0,2},{1,7},{2,4},{3,1},{4,6},{5,3},{6,0},{7,5},{8,10},{9,15},{10,... | collective-permute-start | bytes 786440 | tf_op jit(solution)/shard_map/ppermute | solution.py:47
Sparse Core Ops, SparseCore 0:
  32.7 40.2 all-gather.1

commit v10 on v9

--- a/solution.py
+++ b/solution.py
@@ -154,7 +154,7 @@
     key_ref[...] = picked[:, q_width : q_width + HEAD_DIM].astype(jnp.bfloat16)
     values = picked[:, q_width + HEAD_DIM : kv_at]
     value_ref[...] = jnp.concatenate([values, jnp.ones_like(values)], axis=1).astype(jnp.bfloat16)
-    chunk = min(slots, 256)
+    chunk = min(slots, 128)
     for start in range(0, slots, chunk):
         upto = start + chunk
         row = start + lax.broadcasted_iota(jnp.int32, (chunk, upto), 0)

time: 141 us -> 141 us (level)
  no operation moved by 1% of the time
where the time goes in v10:
time: 141 us; the launch traced here: 140 us
  waiting for transfers between devices  38.5 us (27%)
  starting transfers between devices  37.5 us (27%)
  blocking collectives  26.8 us (19%)
  between operations  14.9 us (11%)
  Pallas kernels  9.3 us (7%)
  local copies, waits for them, and re-layouts  6.09 us (4%)
  other arithmetic  4.24 us (3%)
  matrix products  2.3 us (2%)
    all_to_all x2, waiting for transfers between devices, spread(): return lax.all_to_all(copies, axis, 0, 0)  21.4 us
    all_to_all x2, starting transfers between devices, spread(): return lax.all_to_all(copies, axis, 0, 0)  14.1 us
    all_to_all x1, starting transfers between devices, local(): weights_z = lax.all_to_all(copies, 'z', 0, 0).reshape(n_z * depth, columns)  10.3 us
    all_to_all x1, blocking collectives, local(): last_raw = lax.all_to_all(messages, NARROW, 0, 0)  9.72 us
    pallas_call x10, Pallas kernels, call(): pl.pallas_call(kernel, name=name, out_shape=outs, in_specs=in_specs, out_...  9.3 us
    ppermute x3, starting transfers between devices, along_x(): return lax.ppermute(values, NARROW, pairs)  9.21 us
    ppermute x3, waiting for transfers between devices, along_x(): return lax.ppermute(values, NARROW, pairs)  8.65 us
    all_to_all x1, blocking collectives, local(): probes = lax.all_to_all(probes, NARROW, 0, 0)  8.52 us
  transfers between devices with their start and end apart: 9, of which 7 were waited for; matrix products, arithmetic and copies ran while one was open for 5% of the time, Pallas kernels for 5%

profile of v10, /device:TPU:16, one launch (start us, length us, event | category | flops | bytes accessed | tf_op | source)
XLA Modules:
  0.0 139.6 jit_solution(8102625213746779328)
XLA Ops:
  7.2 1.7 %user_weights.1 = bf16[8,32,640]{2,1,0:T(8,128)(2,1)} custom-call(bf16[32,256]{1,0:T(8,128)(2,1)} %wq_ref.2, bf16[32,128]{1,0:T(8,128)(2,1)} %bitcast.19, bf16[32,256]{1,0:T(8,128)(2,1)} %bitcast.18), custom_call_target="tpu_custom_call" | custom-call | tf_op jit(solution)/shard_map/user_weights/pallas_call | solution.py:197
  8.9 10.3 %all-to-all-start = ((bf16[8,32,640]{2,1,0:T(8,128)(2,1)}), bf16[8,32,640]{2,1,0:T(8,128)(2,1)}, u32[]{:S(2)}, u32[]{:S(2)}) async-start(bf16[8,32,640]{2,1,0:T(8,128)(2,1)} %user_weights.1), calls=%async_computation | async-start | bytes 655360 | tf_op jit(solution)/shard_map/all_to_all | solution.py:243
  19.2 0.0 all-gather.2.cloned.1.call-start
  19.3 0.7 broadcast_in_dim.34.gain_ref
  20.0 0.7 convert_element_type.43
  20.6 1.2 fusion.5
  21.9 1.0 copy-done.2
  22.9 0.1 last_rows.1
  23.7 0.7 broadcast_in_dim.16.gain_ref
  24.3 0.1 pad_add_fusion.scalar_ref
  24.4 1.2 fusion.7.normed_ref
  25.7 6.9 %all-to-all-done = bf16[8,32,640]{2,1,0:T(8,128)(2,1)} async-done(((bf16[8,32,640]{2,1,0:T(8,128)(2,1)}), bf16[8,32,640]{2,1,0:T(8,128)(2,1)}, u32[]{:S(2)}, u32[]{:S(2)}) %all-to-all-start) | async-done | bytes 327712 | tf_op jit(solution)/shard_map/all_to_all | solution.py:243
  32.6 9.7 %all_to_all.30.last_ref = f32[8,8,256]{2,1,0:T(8,128)S(1)} all-to-all(f32[8,8,256]{2,1,0:T(8,128)S(1)} %last_rows.1), channel_id=1, replica_groups=mesh['y'=8,'z'=8,'x'=4,'core'=2] {'x','core'}, dimensions={0} | all-to-all | bytes 131072 | tf_op jit(solution)/shard_map/all_to_all | solution.py:268
  42.3 1.3 item_probes.1
  43.6 8.5 %all_to_all.31.probes_ref = bf16[8,4,2048]{2,1,0:T(4,128)(2,1)S(1)} all-to-all(bf16[8,4,2048]{2,1,0:T(4,128)(2,1)S(1)} %get-tuple-element.21), channel_id=1, replica_groups=mesh['y'=8,'z'=8,'x'=4,'core'=2] {'x','core'}, dimensions={0} | all-to-all | bytes 262144 | tf_op jit(solution)/shard_map/all_to_all | solution.py:283
  52.1 0.7 item_attention.1
  52.9 8.5 %all_to_all.32 = bf16[8,4,2048]{2,1,0:T(4,128)(2,1)S(1)} all-to-all(bf16[8,4,2048]{2,1,0:T(4,128)(2,1)S(1)} %item_attention.1), channel_id=1, replica_groups=mesh['y'=8,'z'=8,'x'=4,'core'=2] {'x','core'}, dimensions={0} | all-to-all | bytes 262144 | tf_op jit(solution)/shard_map/all_to_all | solution.py:292
  61.4 0.3 convolution_convert_fusion.1
  61.8 0.1 reshape.41
  61.9 0.2 convolution_convert_fusion
  62.1 0.7 broadcast_in_dim.35
  62.8 3.4 %all-to-all-start.4 = ((bf16[8,8,2048]{2,1,0:T(8,128)(2,1)}), bf16[8,8,2048]{2,1,0:T(8,128)(2,1)S(1)}, u32[]{:S(2)}, u32[]{:S(2)}) async-start(bf16[8,8,2048]{2,1,0:T(8,128)(2,1)} %broadcast_in_dim.35), calls=%async_computation.4 | async-start | bytes 524288 | tf_op jit(solution)/shard_map/all_to_all | solution.py:33
  66.3 7.4 %all-to-all-done.4.terms_ref = bf16[8,8,2048]{2,1,0:T(8,128)(2,1)S(1)} async-done(((bf16[8,8,2048]{2,1,0:T(8,128)(2,1)}), bf16[8,8,2048]{2,1,0:T(8,128)(2,1)S(1)}, u32[]{:S(2)}, u32[]{:S(2)}) %all-to-all-start.4) | async-done | bytes 262176 | tf_op jit(solution)/shard_map/all_to_all | solution.py:33
  73.7 0.1 item_embeddings.1
  73.9 0.0 all-gather.2.cloned.1.call-done.weights_ref
  73.9 1.7 %fusion.2 = bf16[8,384]{1,0:T(8,128)(2,1)S(1)} fusion(bf16[8,2048]{1,0:T(8,128)(2,1)S(1)} %get-tuple-element.26, bf16[2048,640]{1,0:T(8,128)(2,1)} %all-gather.2.cloned.1.call-done.weights_ref), kind=kOutput, calls=%fused_computation.6 | convolution fusion | flops 12585984 | bytes 1611776 | tf_op jit(solution)/shard_map/dot_general | solution.py:307
  75.7 0.9 broadcast_in_dim.37
  76.5 10.6 %all-to-all-start.5 = ((bf16[64,8,640]{2,1,0:T(8,128)(2,1)}), bf16[64,8,640]{2,1,0:T(8,128)(2,1)S(1)}, u32[]{:S(2)}, u32[]{:S(2)}) async-start(bf16[64,8,640]{2,1,0:T(8,128)(2,1)} %broadcast_in_dim.37), calls=%async_computation.5 | async-start | bytes 1310720 | tf_op jit(solution)/shard_map/all_to_all | solution.py:33
  87.2 1.7 %copy-done.1 = bf16[2048,640]{1,0:T(8,128)(2,1)S(1)} copy-done((bf16[2048,640]{1,0:T(8,128)(2,1)S(1)}, bf16[2048,640]{1,0:T(8,128)(2,1)}, u32[]{:S(2)}) %copy-start.1) | copy-done | bytes 2621464
  88.9 1.4 %output_weights.1 = (bf16[4,256,256]{2,1,0:T(8,128)(2,1)}, bf16[4,256,256]{2,1,0:T(8,128)(2,1)S(1)}) custom-call(s32[3]{0:T(128)S(1)} %pad_add_fusion.scalar_ref, bf16[2048,640]{1,0:T(8,128)(2,1)S(1)} %copy-done.1), custom_call_target="tpu_custom_call" | custom-call | tf_op jit(solution)/shard_map/output_weights/pallas_call | solution.py:197
  90.4 1.9 %collective-permute-start.1 = (bf16[4,256,256]{2,1,0:T(8,128)(2,1)}, bf16[4,256,256]{2,1,0:T(8,128)(2,1)S(1)}, u32[]{:S(2)}, u32[]{:S(2)}) collective-permute-start(bf16[4,256,256]{2,1,0:T(8,128)(2,1)} %get-tuple-element.30), channel_id=1, source_target_pairs={{0,1},{1,0},{2,3},{3,2},{4,5},{5,4},{6,7},{7,6},{8,9},{9,8},{10,11... | collective-permute-start | bytes 1572872 | tf_op jit(solution)/shard_map/ppermute | solution.py:37
  92.3 0.1 copy.14.places_ref
  92.4 13.9 %all-to-all-done.5 = bf16[64,8,640]{2,1,0:T(8,128)(2,1)S(1)} async-done(((bf16[64,8,640]{2,1,0:T(8,128)(2,1)}), bf16[64,8,640]{2,1,0:T(8,128)(2,1)S(1)}, u32[]{:S(2)}, u32[]{:S(2)}) %all-to-all-start.5) | async-done | bytes 655392 | tf_op jit(solution)/shard_map/all_to_all | solution.py:33
  106.4 2.7 %user_attention.1.mixed_ref.mine_ref = bf16[512,256]{1,0:T(8,128)(2,1)S(1)} custom-call(s32[3]{0:T(128)S(1)} %pad_add_fusion.scalar_ref, s32[512,1]{1,0:T(8,128)S(1)} %copy.14.places_ref, bf16[512,640]{1,0:T(8,128)(2,1)S(1)} %bitcast.14), custom_call_target="tpu_custom_call" | custom-call | tf_op jit(solution)/shard_map/user_attention/pallas_call | solution.py:197
  109.1 1.9 %collective-permute-start = (bf16[512,256]{1,0:T(8,128)(2,1)S(1)}, bf16[512,256]{1,0:T(8,128)(2,1)S(1)}, u32[]{:S(2)}, u32[]{:S(2)}) collective-permute-start(bf16[512,256]{1,0:T(8,128)(2,1)S(1)} %user_attention.1.mixed_ref.mine_ref), channel_id=1, source_target_pairs={{0,1},{1,0},{2,3},{3,2},{4,5},{5,4},{6,7},{7,6},{8,9},{9,8},{10,11... | collective-permute-start | bytes 786440 | tf_op jit(solution)/shard_map/ppermute | solution.py:37
  111.0 1.5 %collective-permute-done.others_ref = bf16[512,256]{1,0:T(8,128)(2,1)S(1)} collective-permute-done((bf16[512,256]{1,0:T(8,128)(2,1)S(1)}, bf16[512,256]{1,0:T(8,128)(2,1)S(1)}, u32[]{:S(2)}, u32[]{:S(2)}) %collective-permute-start) | collective-permute-done | bytes 262176 | tf_op jit(solution)/shard_map/ppermute | solution.py:37
  112.5 0.3 output_first.1
  112.9 3.4 %collective-permute-start.3 = (bf16[512,256]{1,0:T(8,128)(2,1)S(1)}, bf16[512,256]{1,0:T(8,128)(2,1)S(1)}, u32[]{:S(2)}, u32[]{:S(2)}) collective-permute-start(bf16[512,256]{1,0:T(8,128)(2,1)S(1)} %output_first.1), channel_id=1, source_target_pairs={{0,2},{1,7},{2,4},{3,1},{4,6},{5,3},{6,0},{7,5},{8,10},{9,15},{10,... | collective-permute-start | bytes 786440 | tf_op jit(solution)/shard_map/ppermute | solution.py:47
  116.3 0.6 output_blocks.1
  116.9 3.7 %collective-permute-start.2 = (bf16[512,256]{1,0:T(8,128)(2,1)S(1)}, bf16[512,256]{1,0:T(8,128)(2,1)S(1)}, u32[]{:S(2)}, u32[]{:S(2)}) collective-permute-start(bf16[512,256]{1,0:T(8,128)(2,1)S(1)} %get-tuple-element.32), channel_id=1, source_target_pairs={{0,6},{1,3},{2,0},{3,5},{4,2},{5,7},{6,4},{7,1},{8,14},{9,11},{10,... | collective-permute-start | bytes 786440 | tf_op jit(solution)/shard_map/ppermute | solution.py:47
  120.6 1.8 %collective-permute-done.3 = bf16[512,256]{1,0:T(8,128)(2,1)S(1)} collective-permute-done((bf16[512,256]{1,0:T(8,128)(2,1)S(1)}, bf16[512,256]{1,0:T(8,128)(2,1)S(1)}, u32[]{:S(2)}, u32[]{:S(2)}) %collective-permute-start.3) | collective-permute-done | bytes 262176 | tf_op jit(solution)/shard_map/ppermute | solution.py:47
  122.4 0.1 add_convert_fusion
  122.4 2.2 %collective-permute-start.4 = (bf16[512,256]{1,0:T(8,128)(2,1)S(1)}, bf16[512,256]{1,0:T(8,128)(2,1)S(1)}, u32[]{:S(2)}, u32[]{:S(2)}) collective-permute-start(bf16[512,256]{1,0:T(8,128)(2,1)S(1)} %add_convert_fusion), channel_id=1, source_target_pairs={{0,2},{1,7},{2,4},{3,1},{4,6},{5,3},{6,0},{7,5},{8,10},{9,15},{10,... | collective-permute-start | bytes 786440 | tf_op jit(solution)/shard_map/ppermute | solution.py:47
  124.6 0.3 residual_rows.1
  124.9 0.2 collective-permute-done.2
  125.1 0.1 convert_add_fusion
  125.2 6.7 %collective-permute-done.4 = bf16[512,256]{1,0:T(8,128)(2,1)S(1)} collective-permute-done((bf16[512,256]{1,0:T(8,128)(2,1)S(1)}, bf16[512,256]{1,0:T(8,128)(2,1)S(1)}, u32[]{:S(2)}, u32[]{:S(2)}) %collective-permute-start.4) | collective-permute-done | bytes 262176 | tf_op jit(solution)/shard_map/ppermute | solution.py:47
  131.9 0.8 select_convert_fusion
  (19 shorter events, 0.1 us)
Async XLA Ops:
  7.2 54.7 %copy-start = (bf16[256,2048]{1,0:T(8,128)(2,1)S(1)}, bf16[256,2048]{1,0:T(8,128)(2,1)}, u32[]{:S(2)}) copy-start(bf16[256,2048]{1,0:T(8,128)(2,1)} %param.15) | copy-start | bytes 3145732
  7.2 35.2 %copy-start.3 = (bf16[2048,1,128]{2,0,1:T(8,128)(2,1)S(1)}, bf16[2048,1,128]{2,0,1:T(8,128)(2,1)}, u32[]{:S(2)}) copy-start(bf16[2048,1,128]{2,0,1:T(8,128)(2,1)} %param.14) | copy-start | bytes 1572868
  7.2 35.2 %copy-start.4 = (bf16[2048,256]{1,0:T(8,128)(2,1)S(1)}, bf16[2048,256]{1,0:T(8,128)(2,1)}, u32[]{:S(2)}) copy-start(bf16[2048,256]{1,0:T(8,128)(2,1)} %wq_ref.3) | copy-start | bytes 3145732
  8.9 23.7 %all-to-all-start = ((bf16[8,32,640]{2,1,0:T(8,128)(2,1)}), bf16[8,32,640]{2,1,0:T(8,128)(2,1)}, u32[]{:S(2)}, u32[]{:S(2)}) async-start(bf16[8,32,640]{2,1,0:T(8,128)(2,1)} %user_weights.1), calls=%async_computation | async-start | bytes 655360 | tf_op jit(solution)/shard_map/all_to_all | solution.py:243
  19.2 54.7 %all-gather.2.cloned.1.call-start = ((), (), s32[]{:S(2)}) async-start(), calls=%async_computation.6 | async-start | bytes 2949120 | tf_op jit(solution)/shard_map/all_gather | solution.py:267
  21.9 1.0 copy-start.2
  62.8 10.9 %all-to-all-start.4 = ((bf16[8,8,2048]{2,1,0:T(8,128)(2,1)}), bf16[8,8,2048]{2,1,0:T(8,128)(2,1)S(1)}, u32[]{:S(2)}, u32[]{:S(2)}) async-start(bf16[8,8,2048]{2,1,0:T(8,128)(2,1)} %broadcast_in_dim.35), calls=%async_computation.4 | async-start | bytes 524288 | tf_op jit(solution)/shard_map/all_to_all | solution.py:33
  73.9 16.5 %copy-start.5 = (bf16[8,256]{1,0:T(8,128)(2,1)}, bf16[8,256]{1,0:T(8,128)(2,1)S(1)}, u32[]{:S(2)}) copy-start(bf16[8,256]{1,0:T(8,128)(2,1)S(1)} %constant_dynamic-slice_fusion) | copy-start | bytes 12292
  75.6 16.6 %copy-start.6 = (s32[1,512]{1,0:T(1,128)S(1)}, s32[1,512]{1,0:T(1,128)}, u32[]{:S(2)}) copy-start(s32[1,512]{1,0:T(1,128)} %param.20) | copy-start | bytes 6148
  76.5 29.8 %all-to-all-start.5 = ((bf16[64,8,640]{2,1,0:T(8,128)(2,1)}), bf16[64,8,640]{2,1,0:T(8,128)(2,1)S(1)}, u32[]{:S(2)}, u32[]{:S(2)}) async-start(bf16[64,8,640]{2,1,0:T(8,128)(2,1)} %broadcast_in_dim.37), calls=%async_computation.5 | async-start | bytes 1310720 | tf_op jit(solution)/shard_map/all_to_all | solution.py:33
  87.2 1.7 %copy-start.1 = (bf16[2048,640]{1,0:T(8,128)(2,1)S(1)}, bf16[2048,640]{1,0:T(8,128)(2,1)}, u32[]{:S(2)}) copy-start(bf16[2048,640]{1,0:T(8,128)(2,1)} %all-gather.2.cloned.1.call-done.weights_ref) | copy-start | bytes 7864324
  90.4 20.7 %collective-permute-start.1 = (bf16[4,256,256]{2,1,0:T(8,128)(2,1)}, bf16[4,256,256]{2,1,0:T(8,128)(2,1)S(1)}, u32[]{:S(2)}, u32[]{:S(2)}) collective-permute-start(bf16[4,256,256]{2,1,0:T(8,128)(2,1)} %get-tuple-element.30), channel_id=1, source_target_pairs={{0,1},{1,0},{2,3},{3,2},{4,5},{5,4},{6,7},{7,6},{8,9},{9,8},{10,11... | collective-permute-start | bytes 1572872 | tf_op jit(solution)/shard_map/ppermute | solution.py:37
  109.1 3.4 %collective-permute-start = (bf16[512,256]{1,0:T(8,128)(2,1)S(1)}, bf16[512,256]{1,0:T(8,128)(2,1)S(1)}, u32[]{:S(2)}, u32[]{:S(2)}) collective-permute-start(bf16[512,256]{1,0:T(8,128)(2,1)S(1)} %user_attention.1.mixed_ref.mine_ref), channel_id=1, source_target_pairs={{0,1},{1,0},{2,3},{3,2},{4,5},{5,4},{6,7},{7,6},{8,9},{9,8},{10,11... | collective-permute-start | bytes 786440 | tf_op jit(solution)/shard_map/ppermute | solution.py:37
  112.9 9.5 %collective-permute-start.3 = (bf16[512,256]{1,0:T(8,128)(2,1)S(1)}, bf16[512,256]{1,0:T(8,128)(2,1)S(1)}, u32[]{:S(2)}, u32[]{:S(2)}) collective-permute-start(bf16[512,256]{1,0:T(8,128)(2,1)S(1)} %output_first.1), channel_id=1, source_target_pairs={{0,2},{1,7},{2,4},{3,1},{4,6},{5,3},{6,0},{7,5},{8,10},{9,15},{10,... | collective-permute-start | bytes 786440 | tf_op jit(solution)/shard_map/ppermute | solution.py:47
  116.9 8.3 %collective-permute-start.2 = (bf16[512,256]{1,0:T(8,128)(2,1)S(1)}, bf16[512,256]{1,0:T(8,128)(2,1)S(1)}, u32[]{:S(2)}, u32[]{:S(2)}) collective-permute-start(bf16[512,256]{1,0:T(8,128)(2,1)S(1)} %get-tuple-element.32), channel_id=1, source_target_pairs={{0,6},{1,3},{2,0},{3,5},{4,2},{5,7},{6,4},{7,1},{8,14},{9,11},{10,... | collective-permute-start | bytes 786440 | tf_op jit(solution)/shard_map/ppermute | solution.py:47
  122.4 9.5 %collective-permute-start.4 = (bf16[512,256]{1,0:T(8,128)(2,1)S(1)}, bf16[512,256]{1,0:T(8,128)(2,1)S(1)}, u32[]{:S(2)}, u32[]{:S(2)}) collective-permute-start(bf16[512,256]{1,0:T(8,128)(2,1)S(1)} %add_convert_fusion), channel_id=1, source_target_pairs={{0,2},{1,7},{2,4},{3,1},{4,6},{5,3},{6,0},{7,5},{8,10},{9,15},{10,... | collective-permute-start | bytes 786440 | tf_op jit(solution)/shard_map/ppermute | solution.py:47
Sparse Core Ops, SparseCore 0:
  32.7 40.2 all-gather.1
